TPU v7x, 512 devices: a whole 4x4x16 slice. The times are simulated.
512 devices in a mesh: patch: 64 (over y, z_hi, x), tensor: 8 (over z_lo, core).
Axes of the slice: x: 4, y: 4, z: 16 (z_hi: 4, z_lo: 4; z = z_hi * 4 + z_lo), core: 2. Of those that a mesh axis runs over, the one named last changes fastest.
Arguments:
- fresh_qkv: bfloat16 [3, 8192, 3072], P(None, 'patch', 'tensor'), may hold values from -14 to 14
- stale_kv: bfloat16 [2, 8192, 3072], P(None, 'patch', 'tensor'), may hold values from -6 to 6
- text_kv: bfloat16 [2, 512, 3072], P(None, None, 'tensor'), may hold values from -6 to 6
- positions: int32 [8192], P('patch'), may hold values from 0 to 8191, each once
- query_gain: float32 [128], replicated, may hold values from 1 to 4
- key_gain: float32 [128], replicated, may hold values from 1 to 4
- out_weight: bfloat16 [3072, 3072], P('tensor'), may hold values from -0.109375 to 0.109375
- gate_table: float32 [28, 3072], P(None, 'tensor'), may hold values from -4 to 4
- timestep: int32 [1], replicated, may hold values from 0 to 27
- hidden_in: bfloat16 [8192, 3072], P('patch', 'tensor'), may hold values from -2 to 2
- control: bfloat16 [8192, 3072], P('patch', 'tensor'), may hold values from -2 to 2
Outputs:
- hidden_out: bfloat16 [8192, 3072], P('patch', 'tensor')
Inputs may be any that keep to these rules, and one draw needn't show every extreme that they name: `positions`: every grid position 0 to 8191 once.
All inputs are finite; a program needn't handle non-finite values.
Results may differ from a plain program's by a relative error of at most 0.02.
Values may be sent and summed in bfloat16 or wider, within the bound.
No kernel may reach another device: no remote copies, remote signals or barrier semaphores. Data moves between devices by JAX's collectives and lax.ppermute only.
A program may use at most 64 MiB of HBM per device.

v0:
```python
import math

import jax
import jax.numpy as jnp
from jax import lax
from jax.sharding import PartitionSpec as P

HEAD_DIMENSION = 128


def pair_angles(positions, head_size):
    first = head_size // 8
    other = (head_size - first) // 2
    lead = first // 2
    mid = other // 2
    pair = jnp.arange(head_size // 2)
    expo = jnp.where(
        pair < lead,
        2.0 * pair / first,
        jnp.where(
            pair < lead + mid, 2.0 * (pair - lead) / other, 2.0 * (pair - lead - mid) / other
        ),
    ).astype(jnp.float32)
    omega = jnp.power(jnp.float32(10000.0), -expo)
    row_pos = (positions // 128).astype(jnp.float32)
    col_pos = (positions % 128).astype(jnp.float32)
    where_pos = jnp.where(
        pair[None, :] < lead,
        jnp.float32(0.0),
        jnp.where(pair[None, :] < lead + mid, row_pos[:, None], col_pos[:, None]),
    )
    angle = where_pos * omega[None, :]
    return (jnp.cos(angle), jnp.sin(angle))


def prepare(raw, gain, cosines, sines, head_size):
    count = raw.shape[0]
    values = raw.astype(jnp.float32).reshape(count, -1, head_size)
    values = values * lax.rsqrt(jnp.mean(values * values, axis=-1, keepdims=True) + 1e-06) * gain
    pairs = values.reshape(count, values.shape[1], head_size // 2, 2)
    first_part = pairs[..., 0]
    second_part = pairs[..., 1]
    cos_b = cosines[:, None, :]
    sin_b = sines[:, None, :]
    rotated = jnp.stack(
        [first_part * cos_b - second_part * sin_b, first_part * sin_b + second_part * cos_b],
        axis=-1,
    )
    return rotated.reshape(count, -1, head_size).astype(jnp.bfloat16)


def body(
    fresh_qkv,
    stale_kv,
    text_kv,
    positions,
    query_gain,
    key_gain,
    out_weight,
    gate_table,
    timestep,
    hidden_in,
    control,
):
    tok_rows = fresh_qkv.shape[1]
    heads_dev = fresh_qkv.shape[2] // HEAD_DIMENSION
    score_scale = 1.0 / math.sqrt(HEAD_DIMENSION)
    cosines, sines = pair_angles(positions, HEAD_DIMENSION)
    query = prepare(fresh_qkv[0], query_gain, cosines, sines, HEAD_DIMENSION)
    local_k = prepare(fresh_qkv[1], key_gain, cosines, sines, HEAD_DIMENSION)
    local_v = fresh_qkv[2].reshape(tok_rows, heads_dev, HEAD_DIMENSION)
    text_k = text_kv[0].reshape(-1, heads_dev, HEAD_DIMENSION)
    text_v = text_kv[1].reshape(-1, heads_dev, HEAD_DIMENSION)
    s_local = (
        jnp.einsum("qhd,khd->hqk", query, local_k, preferred_element_type=jnp.float32) * score_scale
    )
    s_text = (
        jnp.einsum("qhd,khd->hqk", query, text_k, preferred_element_type=jnp.float32) * score_scale
    )
    top = jnp.maximum(jnp.max(s_local, axis=2), jnp.max(s_text, axis=2))
    p_local = jnp.exp(s_local - top[:, :, None])
    p_text = jnp.exp(s_text - top[:, :, None])
    total = jnp.sum(p_local, axis=2) + jnp.sum(p_text, axis=2)
    running = jnp.einsum(
        "hqk,khd->hqd", p_local.astype(jnp.bfloat16), local_v, preferred_element_type=jnp.float32
    )
    running = running + jnp.einsum(
        "hqk,khd->hqd", p_text.astype(jnp.bfloat16), text_v, preferred_element_type=jnp.float32
    )
    own_start = lax.axis_index("patch") * tok_rows
    gathered = lax.all_gather(stale_kv, "patch", axis=1, tiled=True)
    count = gathered.shape[1]
    keys = gathered[0].reshape(count, heads_dev, HEAD_DIMENSION)
    values = gathered[1].reshape(count, heads_dev, HEAD_DIMENSION)
    scores = (
        jnp.einsum("qhd,khd->hqk", query, keys, preferred_element_type=jnp.float32) * score_scale
    )
    row_index = jnp.arange(count)
    own_rows = (row_index >= own_start) & (row_index < own_start + tok_rows)
    scores = jnp.where(own_rows[None, None, :], -jnp.inf, scores)
    new_top = jnp.maximum(top, jnp.max(scores, axis=2))
    factor = jnp.exp(top - new_top)
    probs = jnp.exp(scores - new_top[:, :, None])
    new_total = total * factor + jnp.sum(probs, axis=2)
    new_sum = running * factor[:, :, None] + jnp.einsum(
        "hqk,khd->hqd", probs.astype(jnp.bfloat16), values, preferred_element_type=jnp.float32
    )
    attended = (new_sum / new_total[:, :, None]).astype(jnp.bfloat16)
    attended = jnp.transpose(attended, (1, 0, 2)).reshape(tok_rows, heads_dev * HEAD_DIMENSION)
    projected = jnp.dot(attended, out_weight, preferred_element_type=jnp.float32)
    width_dev = hidden_in.shape[1]
    whole_sum = lax.psum(projected.astype(jnp.bfloat16), "tensor").astype(jnp.float32)
    summed = lax.dynamic_slice_in_dim(whole_sum, lax.axis_index("tensor") * width_dev, width_dev, 1)
    picker = (jnp.arange(gate_table.shape[0]) == timestep[0]).astype(jnp.float32)
    gate = jnp.dot(picker, gate_table, precision=lax.Precision.HIGHEST)
    mixed = hidden_in.astype(jnp.float32) + gate[None, :] * summed + control.astype(jnp.float32)
    return mixed.astype(jnp.bfloat16)


def solution(mesh):
    in_specs = (
        P(None, "patch", "tensor"),
        P(None, "patch", "tensor"),
        P(None, None, "tensor"),
        P("patch"),
        P(),
        P(),
        P("tensor", None),
        P(None, "tensor"),
        P(),
        P("patch", "tensor"),
        P("patch", "tensor"),
    )
    out_specs = P("patch", "tensor")
    return jax.shard_map(body, mesh=mesh, in_specs=in_specs, out_specs=out_specs, check_vma=False)
```

profile of v0, /device:TPU:1, one launch (start us, length us, event | category | flops | bytes accessed | tf_op | source)
XLA Modules:
  0.0 466.0 jit_solution(4261718116859585864)
XLA Ops:
  6.5 1.9 copy.28
  8.5 0.8 mul.210
  9.3 1.0 fusion.43
  10.5 0.8 mul.195
  11.5 1.2 fusion.42
  12.7 1.0 copy.40
  13.7 0.9 copy.27
  14.6 0.8 copy.25
  15.4 0.7 fusion.37
  16.6 0.5 subtract_convert_fusion
  17.6 0.3 fusion.45
  17.8 1.4 fusion.46
  19.2 336.1 %all-gather.2.cloned.1.call-done = bf16[2,8192,384]{1,2,0:T(8,128)(2,1)} async-done(((bf16[2,128,384]{1,2,0:T(8,128)(2,1)}), bf16[2,8192,384]{1,2,0:T(8,128)(2,1)}) %all-gather.2.cloned.1.call-update) | async-done | bytes 12582928 | tf_op jit(solution)/shard_map/all_gather | solution.py:91
  355.3 8.3 %fusion.41 = (bf16[1,8192,384]{1,2,0:T(8,128)(2,1)S(1)}, bf16[1,8192,384]{1,2,0:T(8,128)(2,1)}) fusion(bf16[2,8192,384]{1,2,0:T(8,128)(2,1)} %all-gather.2.cloned.1.call-done), kind=kLoop, calls=%fused_computation.74 | loop fusion | bytes 25165824 | tf_op jit(solution)/shard_map/slice | solution.py:93
  363.6 2.4 fusion.44
  366.0 2.0 fusion
  368.0 2.6 copy-done.1
  370.6 8.3 %fusion.9 = f32[128,3,128]{0,2,1:T(8,128)S(1)} fusion(bf16[8192,3,128]{0,2,1:T(8,128)(2,1)} %bitcast.55, f32[3,128,8192]{2,1,0:T(8,128)} %copy-done.1, f32[3,128]{1,0:T(4,128)S(1)} %get-tuple-element.7), kind=kOutput, calls=%fused_computation.14 | convolution fusion | flops 811597824 | bytes 19072512 | tf_op jit(solution)/shard_map/hqk,khd->hqd/dot_general | solution.py:105
  378.9 0.3 fusion.13
  379.2 0.4 fusion.15
  379.9 1.5 convolution_convert_fusion
  382.1 1.0 convolution_reduce_fusion
  383.1 74.5 %all-reduce.2.cloned.1.call-done = bf16[128,3072]{1,0:T(8,128)(2,1)} async-done(((bf16[128,3072]{1,0:T(8,128)(2,1)}), bf16[128,3072]{1,0:T(8,128)(2,1)}) %all-reduce.2.cloned.1.call-update) | async-done | bytes 786448 | tf_op jit(solution)/shard_map/psum | solution.py:112
  457.6 1.6 add_convert_fusion
  (34 shorter events, 1.6 us)
Async XLA Ops:
  6.5 373.4 %copy-start = (bf16[384,3072]{1,0:T(8,128)(2,1)S(1)}, bf16[384,3072]{1,0:T(8,128)(2,1)}, u32[]{:S(2)}) copy-start(bf16[384,3072]{1,0:T(8,128)(2,1)} %param.17) | copy-start | bytes 7077892
  6.5 348.8 %all-gather.2.cloned.1.call-start = ((), (), s32[]{:S(2)}) async-start(), calls=%async_computation | async-start | bytes 12779520 | tf_op jit(solution)/shard_map/all_gather | solution.py:91
  8.5 449.1 %all-reduce.2.cloned.1.call-start = ((), (), s32[]{:S(2)}) async-start(), calls=%async_computation.1 | async-start | bytes 1572864 | tf_op jit(solution)/shard_map/psum | solution.py:112
  366.0 4.6 copy-start.1
  370.6 8.6 %copy-start.2 = (bf16[1,512,384]{1,2,0:T(8,128)(2,1)S(1)}, bf16[1,512,384]{1,2,0:T(8,128)(2,1)}, u32[]{:S(2)}) copy-start(bf16[1,512,384]{1,2,0:T(8,128)(2,1)} %copy.27) | copy-start | bytes 1179652
  370.6 9.1 %copy-start.3 = (bf16[1,128,384]{1,2,0:T(8,128)(2,1)S(1)}, bf16[1,128,384]{1,2,0:T(8,128)(2,1)}, u32[]{:S(2)}) copy-start(bf16[1,128,384]{1,2,0:T(8,128)(2,1)} %copy.25) | copy-start | bytes 294916
  378.9 78.6 %copy-start.4 = (bf16[128,384]{1,0:T(8,128)(2,1)S(1)}, bf16[128,384]{1,0:T(8,128)(2,1)}, u32[]{:S(2)}) copy-start(bf16[128,384]{1,0:T(8,128)(2,1)} %param.21) | copy-start | bytes 294916
  378.9 78.6 %copy-start.5 = (bf16[128,384]{1,0:T(8,128)(2,1)S(1)}, bf16[128,384]{1,0:T(8,128)(2,1)}, u32[]{:S(2)}) copy-start(bf16[128,384]{1,0:T(8,128)(2,1)} %param.20) | copy-start | bytes 294916
Sparse Core Ops, SparseCore 0:
  11.3 343.9 all-gather.1
  381.6 75.9 all-reduce.1
where the time goes:
time: 468 us; the launch traced here: 466 us
  waiting for transfers between devices  411 us (88%)
  local copies, waits for them, and re-layouts  19.5 us (4%)
  matrix products  15.4 us (3%)
  between operations  14.3 us (3%)
  other arithmetic  6.14 us (1%)
    all_gather x1, waiting for transfers between devices, body(): gathered = lax.all_gather(stale_kv, 'patch', axis=1, tiled=True)  336 us
    psum x1, waiting for transfers between devices, body(): lax.psum(projected.astype(jnp.bfloat16), 'tensor').astype(jnp.float32)  74.5 us
  transfers between devices with their start and end apart: 2, of which 2 were waited for; matrix products, arithmetic and copies ran while one was open for 2% of the time, Pallas kernels for 0%

commit v1 on v0

v1 whole, which is shorter than its diff:
```python
import math

import jax
import jax.numpy as jnp
import numpy as np
from jax import lax
from jax.experimental import pallas as pl
from jax.experimental.pallas import tpu as pltpu
from jax.sharding import PartitionSpec as P

HD = 128
TOK = 128
HEADS_DEV = 3
WIDTH = HEADS_DEV * HD
TXT = 512
STAT = 16
SCALE2 = math.log2(math.e) / math.sqrt(HD)
AXES = ("patch", "tensor")
MIB = 1024 * 1024
F32 = jnp.float32
BF16 = jnp.bfloat16


def coords(flat):
    patch, tensor = divmod(flat, 8)
    return patch // 16, patch // 4 % 4, patch % 4, tensor // 2, tensor % 2


def flat_of(y, zh, x, zl, core):
    return (y * 16 + zh * 4 + x) * 8 + zl * 2 + core


def permute(value, where):
    pairs = [(i, flat_of(*where(*coords(i)))) for i in range(512)]
    return lax.ppermute(value, AXES, pairs)


def rings(axis_of_core):
    groups = {}
    for i in range(512):
        y, zh, x, zl, c = coords(i)
        rest = (y, zh, zl, c) if axis_of_core[c] == "x" else (x, zh, zl, c)
        groups.setdefault(rest, []).append(i)
    return list(groups.values())


QUERY_RINGS = rings("xy")
KEY_RINGS = rings("yx")
Z_RUNS = [[0, 2, 4, 6], [1, 3, 5, 7]]


def exchange(value, axes, groups):
    return lax.all_to_all(value, axes, 0, 0, axis_index_groups=groups, tiled=True)


def ring_places():
    patch = lax.axis_index("patch")
    x, y = patch % 4, patch // 16
    first = lax.axis_index("tensor") % 2 == 0
    return jnp.where(first, x, y), jnp.where(first, y, x)


def key_pair(value):
    return permute(value, lambda y, zh, x, zl, c: (y, zh ^ (1, 3)[c], x, zl, c))


def query_pair(value):
    return permute(value, lambda y, zh, x, zl, c: (y, zh ^ (3, 1)[c], x, zl, c))


def swap_core(value):
    return permute(value, lambda y, zh, x, zl, c: (y, zh, x, zl, 1 - c))


def frequencies():
    first = HD // 8
    other = (HD - first) // 2
    lead = first // 2
    mid = other // 2
    table = np.zeros((8, HD), np.float32)
    for lane in range(HD):
        pair = lane // 2
        if pair < lead:
            continue
        row = 0 if pair < lead + mid else 1
        k = pair - lead - row * mid
        table[row, lane] = np.power(np.float32(10000.0), -np.float32(2.0 * k / other))
        table[2, lane] = 0.0
    table[3] = np.where(np.arange(HD) % 2 == 0, -1.0, 1.0)
    return table


def prep_kernel(raw_hbm, pos_hbm, freq_hbm, qg_hbm, kg_hbm, q_out, k_out, raw, pos, freq, gains, sem):
    copies = [
        pltpu.make_async_copy(pos_hbm, pos, sem.at[0]),
        pltpu.make_async_copy(freq_hbm, freq, sem.at[1]),
        pltpu.make_async_copy(raw_hbm.at[pl.ds(0, 2)], raw, sem.at[2]),
        pltpu.make_async_copy(qg_hbm, gains.at[0], sem.at[3]),
        pltpu.make_async_copy(kg_hbm, gains.at[1], sem.at[4]),
    ]
    for c in copies:
        c.start()
    copies[0].wait()
    copies[1].wait()
    sub = lax.broadcasted_iota(jnp.int32, (TOK, HD), 0)
    lane = lax.broadcasted_iota(jnp.int32, (TOK, HD), 1)
    p_row = jnp.broadcast_to(pos[...], (TOK, HD))
    p_col = jnp.sum(
        jnp.where(sub == lane, p_row.astype(F32), 0.0), axis=1, keepdims=True
    ).astype(jnp.int32)
    rows = (p_col // 128).astype(F32)
    cols = (p_col % 128).astype(F32)
    angle = rows * freq[0:1, :] + cols * freq[1:2, :]
    cosv = jnp.cos(angle)
    sinv = jnp.sin(angle) * freq[3:4, :]
    even = lane % 2 == 0
    for c in copies[2:]:
        c.wait()
    for which, out in ((0, q_out), (1, k_out)):
        for h in range(HEADS_DEV):
            v = raw[which, :, h * HD : (h + 1) * HD].astype(F32)
            v = v * lax.rsqrt(jnp.mean(v * v, axis=-1, keepdims=True) + 1e-06) * gains[which]
            other = jnp.where(even, pltpu.roll(v, HD - 1, 1), pltpu.roll(v, 1, 1))
            out[:, h * HD : (h + 1) * HD] = (v * cosv + other * sinv).astype(BF16)


def prepare(fresh_qkv, positions, query_gain, key_gain):
    full = pl.BlockSpec(memory_space=pltpu.VMEM)
    return pl.pallas_call(
        prep_kernel,
        out_shape=(jax.ShapeDtypeStruct((TOK, WIDTH), BF16),) * 2,
        in_specs=[pl.BlockSpec(memory_space=pltpu.HBM)] * 5,
        out_specs=(full, full),
        scratch_shapes=[
            pltpu.VMEM((2, TOK, WIDTH), BF16),
            pltpu.VMEM((1, TOK), jnp.int32),
            pltpu.VMEM((8, HD), F32),
            pltpu.VMEM((2, 1, HD), F32),
            pltpu.SemaphoreType.DMA((5,)),
        ],
        compiler_params=pltpu.CompilerParams(vmem_limit_bytes=56 * MIB),
        name="prep",
    )(
        fresh_qkv,
        positions.reshape(1, TOK),
        jnp.asarray(frequencies()),
        query_gain.reshape(1, HD),
        key_gain.reshape(1, HD),
    )


def split3(v):
    hi = v.astype(BF16).astype(F32)
    rest = v - hi
    mid = rest.astype(BF16).astype(F32)
    return hi, mid, rest - mid


def attend(q, keys, values):
    s = [
        lax.dot_general(q, k, (((1,), (1,)), ((), ())), preferred_element_type=F32) for k in keys
    ]
    top = jnp.max(s[0], axis=1, keepdims=True)
    for t in s[1:]:
        top = jnp.maximum(top, jnp.max(t, axis=1, keepdims=True))
    top = top * SCALE2
    acc = None
    for t, v in zip(s, values):
        p = jnp.exp2(t * SCALE2 - top).astype(BF16)
        part = jnp.dot(p, v, preferred_element_type=F32)
        acc = part if acc is None else acc + part
    total = acc[:, HD:]
    return acc[:, :HD] / total, top + jnp.log2(total)


def attn_kernel(k_fresh, raw, text, stale, kv_own, kv_pair, q, out, kc, vc, kt, vt):
    q_at, k_at = ring_places()
    own_rows = pl.ds(pl.multiple_of(k_at * TOK, TOK), TOK)
    for h in range(HEADS_DEV):
        cut = slice(h * HD, (h + 1) * HD)
        for b in range(4):
            for at, kv in ((b, kv_own), (4 + b, kv_pair)):
                kc[h, at * TOK : (at + 1) * TOK, :] = kv[b, 0, :, cut]
                vc[h, at * TOK : (at + 1) * TOK, 0:HD] = kv[b, 1, :, cut]
        kc[h, own_rows, :] = k_fresh[:, cut]
        vc[h, own_rows, 0:HD] = raw[2, :, cut]
        vc[h, :, HD:] = jnp.ones((8 * TOK, HD), BF16)
        kt[h] = text[0, :, cut]
        vt[h, :, 0:HD] = text[1, :, cut]
        vt[h, :, HD:] = jnp.ones((TXT, HD), BF16)
    lane = lax.broadcasted_iota(jnp.int32, (TOK, HD), 1)

    def one(ring, half, own):
        stat = jnp.zeros((TOK, HD), F32)
        for h in range(HEADS_DEV):
            cut = slice(h * HD, (h + 1) * HD)
            keys, values = [kc[h]], [vc[h]]
            if own:
                keys.append(kt[h])
                values.append(vt[h])
            o, lse = attend(q[ring, half, :, cut], keys, values)
            out[ring, half * TOK : (half + 1) * TOK, cut] = o.astype(BF16)
            for part, v in enumerate(split3(lse)):
                stat = jnp.where(lane == 3 * h + part, v, stat)
        out[ring, 2 * TOK :, half * HD : (half + 1) * HD] = stat.T[:STAT].astype(BF16)

    out[:, 2 * TOK :, :] = jnp.zeros((4, STAT, WIDTH), BF16)
    one(q_at, 0, True)
    for h in range(HEADS_DEV):
        cut = slice(h * HD, (h + 1) * HD)
        kc[h, own_rows, :] = stale[0, :, cut]
        vc[h, own_rows, 0:HD] = stale[1, :, cut]
    one(q_at, 1, False)

    def step(d, carry):
        ring = (q_at + d) % 4
        one(ring, 0, False)
        one(ring, 1, False)
        return carry

    lax.fori_loop(1, 4, step, 0)


def attention(*args):
    full = pl.BlockSpec(memory_space=pltpu.VMEM)
    return pl.pallas_call(
        attn_kernel,
        out_shape=jax.ShapeDtypeStruct((4, 2 * TOK + STAT, WIDTH), BF16),
        in_specs=[full] * 7,
        out_specs=full,
        scratch_shapes=[
            pltpu.VMEM((HEADS_DEV, 8 * TOK, HD), BF16),
            pltpu.VMEM((HEADS_DEV, 8 * TOK, 2 * HD), BF16),
            pltpu.VMEM((HEADS_DEV, TXT, HD), BF16),
            pltpu.VMEM((HEADS_DEV, TXT, 2 * HD), BF16),
        ],
        compiler_params=pltpu.CompilerParams(vmem_limit_bytes=32 * MIB),
        name="attend",
    )(*args)


def merge(parts, stats):
    rows = []
    for st in stats:
        rows.append([st[3 * h : 3 * h + 1] + st[3 * h + 1 : 3 * h + 2] + st[3 * h + 2 : 3 * h + 3]
                     for h in range(HEADS_DEV)])
    sub = lax.broadcasted_iota(jnp.int32, (TOK, HD), 0)
    table = jnp.zeros((TOK, HD), F32)
    lses = []
    for h in range(HEADS_DEV):
        top = rows[0][h]
        for r in rows[1:]:
            top = jnp.maximum(top, r[h])
        weights = [jnp.exp2(r[h] - top) for r in rows]
        total = weights[0]
        for w in weights[1:]:
            total = total + w
        lses.append(top + jnp.log2(total))
        for i, w in enumerate(weights):
            table = jnp.where(sub == len(rows) * h + i, w / total, table)
    table = table.T
    outs = []
    for h in range(HEADS_DEV):
        acc = None
        for i, part in enumerate(parts):
            w = table[:, len(rows) * h + i : len(rows) * h + i + 1]
            term = part(h) * w
            acc = term if acc is None else acc + term
        outs.append(acc)
    return outs, lses


def merge_kernel(got, keep, send):
    refs = [got.at[i] for i in range(4)]
    sub = lax.broadcasted_iota(jnp.int32, (STAT, HD), 0)
    for half, out in ((0, keep), (1, send)):
        parts = [
            lambda h, r=r: r[half * TOK : (half + 1) * TOK, h * HD : (h + 1) * HD].astype(F32)
            for r in refs
        ]
        stats = [r[2 * TOK :, half * HD : (half + 1) * HD].astype(F32) for r in refs]
        outs, lses = merge(parts, stats)
        table = jnp.zeros((STAT, HD), F32)
        for h in range(HEADS_DEV):
            out[0:TOK, h * HD : (h + 1) * HD] = outs[h].astype(BF16)
            for part, v in enumerate(split3(lses[h])):
                table = jnp.where(sub == 3 * h + part, v, table)
        out[TOK:, :] = jnp.zeros((STAT, WIDTH), BF16)
        out[TOK:, 0:HD] = table.astype(BF16)


def merge_first(messages):
    full = pl.BlockSpec(memory_space=pltpu.VMEM)
    return pl.pallas_call(
        merge_kernel,
        out_shape=(jax.ShapeDtypeStruct((TOK + STAT, WIDTH), BF16),) * 2,
        in_specs=[full],
        out_specs=(full, full),
        compiler_params=pltpu.CompilerParams(vmem_limit_bytes=16 * MIB),
        name="merge",
    )(messages)


def project_kernel(mine, theirs, w, keep, give, att):
    refs = (mine, theirs)
    parts = [lambda h, r=r: r[0:TOK, h * HD : (h + 1) * HD].astype(F32) for r in refs]
    outs, _ = merge(parts, [r[TOK:, 0:HD].astype(F32) for r in refs])
    for h in range(HEADS_DEV):
        att[:, h * HD : (h + 1) * HD] = outs[h].astype(BF16)
    core = lax.axis_index("tensor") % 2
    for z in range(4):
        for out, c in ((give, 1 - core), (keep, core)):
            part = w[:, pl.ds(pl.multiple_of((2 * z + c) * WIDTH, HD), WIDTH)]
            out[z] = jnp.dot(att[...], part, preferred_element_type=F32).astype(out.dtype)


def project(mine, theirs, out_weight):
    full = pl.BlockSpec(memory_space=pltpu.VMEM)
    return pl.pallas_call(
        project_kernel,
        out_shape=(
            jax.ShapeDtypeStruct((4, TOK, WIDTH), F32),
            jax.ShapeDtypeStruct((4, TOK, WIDTH), BF16),
        ),
        in_specs=[full] * 3,
        out_specs=(full, full),
        scratch_shapes=[pltpu.VMEM((TOK, WIDTH), BF16)],
        compiler_params=pltpu.CompilerParams(vmem_limit_bytes=16 * MIB),
        name="project",
    )(mine, theirs, out_weight)


def pair_kernel(keep, got, out):
    out[...] = (keep[...] + got[...].astype(F32)).astype(BF16)


def pair_sum(keep, got):
    full = pl.BlockSpec(memory_space=pltpu.VMEM)
    return pl.pallas_call(
        pair_kernel,
        out_shape=jax.ShapeDtypeStruct((4, TOK, WIDTH), BF16),
        in_specs=[full] * 2,
        out_specs=full,
        compiler_params=pltpu.CompilerParams(vmem_limit_bytes=16 * MIB),
        name="pair_sum",
    )(keep, got)


def final_kernel(step, got, gate, hidden, control, out):
    total = got[0].astype(F32)
    for t in range(1, 4):
        total = total + got[t].astype(F32)
    row = gate[pl.ds(step[0], 1), :]
    out[...] = (hidden[...].astype(F32) + row * total + control[...].astype(F32)).astype(BF16)


def finish(timestep, got, gate_table, hidden_in, control):
    full = pl.BlockSpec(memory_space=pltpu.VMEM)
    return pl.pallas_call(
        final_kernel,
        out_shape=jax.ShapeDtypeStruct((TOK, WIDTH), BF16),
        in_specs=[pl.BlockSpec(memory_space=pltpu.SMEM)] + [full] * 4,
        out_specs=full,
        compiler_params=pltpu.CompilerParams(vmem_limit_bytes=16 * MIB),
        name="finish",
    )(timestep, got, gate_table, hidden_in, control)


def body(
    fresh_qkv,
    stale_kv,
    text_kv,
    positions,
    query_gain,
    key_gain,
    out_weight,
    gate_table,
    timestep,
    hidden_in,
    control,
):
    pair_kv = key_pair(stale_kv)
    q, k_fresh = prepare(fresh_qkv, positions, query_gain, key_gain)
    pair_q = query_pair(q)
    stale_kv, q = lax.optimization_barrier((stale_kv, q))
    kv_own = lax.all_gather(stale_kv, AXES, axis_index_groups=KEY_RINGS)
    pair_q, pair_kv, kv_own = lax.optimization_barrier((pair_q, pair_kv, kv_own))
    q_two = jnp.broadcast_to(jnp.stack([q, pair_q])[None], (4, 2, TOK, WIDTH))
    q_all = exchange(q_two, AXES, QUERY_RINGS)
    kv_pair = lax.all_gather(pair_kv, AXES, axis_index_groups=KEY_RINGS)
    partial = attention(k_fresh, fresh_qkv, text_kv, stale_kv, kv_own, kv_pair, q_all)
    keep, send = merge_first(exchange(partial, AXES, QUERY_RINGS))
    keep, give = project(keep, query_pair(send), out_weight)
    parts = exchange(pair_sum(keep, swap_core(give)), "tensor", Z_RUNS)
    return finish(timestep, parts, gate_table, hidden_in, control)


def solution(mesh):
    in_specs = (
        P(None, "patch", "tensor"),
        P(None, "patch", "tensor"),
        P(None, None, "tensor"),
        P("patch"),
        P(),
        P(),
        P("tensor", None),
        P(None, "tensor"),
        P(),
        P("patch", "tensor"),
        P("patch", "tensor"),
    )
    out_specs = P("patch", "tensor")
    return jax.shard_map(body, mesh=mesh, in_specs=in_specs, out_specs=out_specs, check_vma=False)
```

time: 468 us -> 113 us (0.24)
  waiting for transfers between devices: 411 us -> 21 us
  blocking collectives: 0 us -> 38.3 us
  starting transfers between devices: 0.04 us -> 37.5 us
  local copies, waits for them, and re-layouts: 19.5 us -> 2.12 us
  matrix products: 15.4 us -> 0 us
  between operations: 14.3 us -> 0.77 us
  Pallas kernels: 0 us -> 12.3 us
  other arithmetic: 6.14 us -> 0.92 us
    all_gather x1 -> x0, waiting for transfers between devices: 336 us -> none  [body(): gathered = lax.all_gather(stale_kv, 'patch', axis=1, tiled=True)]
    psum x1 -> x0, waiting for transfers between devices: 74.5 us -> none  [body(): lax.psum(projected.astype(jnp.bfloat16), 'tensor').astype(jnp.float32)]
    ppermute x0 -> x4, starting transfers between devices: none -> 27.4 us  [permute(): return lax.ppermute(value, AXES, pairs)]
    all_gather x0 -> x2, blocking collectives: none -> 26.3 us  [the longest x1 14.4 us: body(): kv_pair = lax.all_gather(pair_kv, AXES, axis_index_groups=KEY_RINGS)]
    dot_general x8 -> x0, matrix products: 15.4 us -> none  [the longest x1 8.31 us: body(): jnp.einsum('hqk,khd->hqd', probs.astype(jnp.bfloat16), values, preferred_...]
    pallas_call x0 -> x6, Pallas kernels: none -> 12.3 us  [the longest x1 6.67 us: attention(): pl.pallas_call(attn_kernel, out_shape=jax.ShapeDtypeStruct((4, 2 * TOK +...]
    slice x5 -> x0, local copies, waits for them, and re-layouts: 12.2 us -> none  [the longest x1 8.33 us: body(): keys = gathered[0].reshape(count, heads_dev, HEAD_DIMENSION)]
    all_to_all x0 -> x1, blocking collectives: none -> 12 us  [exchange(): lax.all_to_all(value, axes, 0, 0, axis_index_groups=groups, tiled=True)]
  transfers between devices with their start and end apart: 2 -> 6, of which waited for: 2 -> 3; matrix products, arithmetic and copies ran while one was open for 2% -> 0% of each run, Pallas kernels for 0% -> 0%
where the time goes in v1:
time: 113 us
  blocking collectives  38.3 us (34%)
  starting transfers between devices  37.5 us (33%)
  waiting for transfers between devices  21 us (19%)
  Pallas kernels  12.3 us (11%)
  local copies, waits for them, and re-layouts  2.12 us (2%)
    ppermute x4, starting transfers between devices, permute(): return lax.ppermute(value, AXES, pairs)  27.4 us
    all_gather x1, blocking collectives, body(): kv_pair = lax.all_gather(pair_kv, AXES, axis_index_groups=KEY_RINGS)  14.4 us
    all_to_all x1, blocking collectives, exchange(): lax.all_to_all(value, axes, 0, 0, axis_index_groups=groups, tiled=True)  12 us
    all_gather x1, blocking collectives, body(): kv_own = lax.all_gather(stale_kv, AXES, axis_index_groups=KEY_RINGS)  11.9 us
    all_to_all x2, waiting for transfers between devices, exchange(): lax.all_to_all(value, axes, 0, 0, axis_index_groups=groups, tiled=True)  10.6 us
    ppermute x4, waiting for transfers between devices, permute(): return lax.ppermute(value, AXES, pairs)  10.4 us
    all_to_all x2, starting transfers between devices, exchange(): lax.all_to_all(value, axes, 0, 0, axis_index_groups=groups, tiled=True)  10.1 us
    pallas_call x1, Pallas kernels, attention(): pl.pallas_call(attn_kernel, out_shape=jax.ShapeDtypeStruct((4, 2 * TOK +...  6.67 us
  transfers between devices with their start and end apart: 6, of which 3 were waited for; matrix products, arithmetic and copies ran while one was open for 0% of the time, Pallas kernels for 0%

profile of v1, /device:TPU:1, one launch (start us, length us, event | category | flops | bytes accessed | tf_op | source)
XLA Modules:
  0.0 112.9 jit_solution(15451528905662002098)
XLA Ops:
  0.0 2.5 %prep.1 = (bf16[128,384]{1,0:T(8,128)(2,1)}, bf16[128,384]{1,0:T(8,128)(2,1)}) custom-call(bf16[3,128,384]{2,1,0:T(8,128)(2,1)} %raw.1, s32[1,128]{1,0:T(1,128)} %bitcast.11, f32[8,128]{1,0:T(8,128)} %constant.2.clone.freq_hbm, f32[1,128]{1,0:T(1,128)} %bitcast.12, f32[1,128]{1,0:T(1,128)} %bitcast.13), custom_call_target="tpu_custom_call" | custom-call | tf_op jit(solution)/shard_map/prep/pallas_call | solution.py:129
  2.5 0.0 copy-start.1
  2.5 0.0 copy-start.2
  2.6 9.8 %collective-permute-start = (bf16[128,384]{1,0:T(8,128)(2,1)}, bf16[128,384]{1,0:T(8,128)(2,1)S(1)}, u32[]{:S(2)}, u32[]{:S(2)}) collective-permute-start(bf16[128,384]{1,0:T(8,128)(2,1)} %get-tuple-element.21), channel_id=1, source_target_pairs={{0,96},{1,33},{2,98},{3,35},{4,100},{5,37},{6,102},{7,39},{8,104},... | collective-permute-start | bytes 294920 | tf_op jit(solution)/shard_map/ppermute | solution.py:35
  12.4 8.8 %collective-permute-start.1 = (bf16[2,128,384]{2,1,0:T(8,128)(2,1)}, bf16[2,128,384]{2,1,0:T(8,128)(2,1)S(1)}, u32[]{:S(2)}, u32[]{:S(2)}) collective-permute-start(bf16[2,128,384]{2,1,0:T(8,128)(2,1)} %stale), channel_id=1, source_target_pairs={{0,32},{1,97},{2,34},{3,99},{4,36},{5,101},{6,38},{7,103},{8,40},{... | collective-permute-start | bytes 589832 | tf_op jit(solution)/shard_map/ppermute | solution.py:35
  21.2 11.9 %all-gather = bf16[8,128,384]{2,1,0:T(8,128)(2,1)S(1)} all-gather(bf16[2,128,384]{2,1,0:T(8,128)(2,1)} %stale), channel_id=2, replica_groups={{0,128,256,384},{1,9,17,25},{2,130,258,386},{3,11,19,27},{4,132,260,388..., dimensions={0}, use_global_device_ids=true | all-gather | bytes 983040 | tf_op jit(solution)/shard_map/all_gather | solution.py:386
  33.1 0.9 pad_maximum_fusion
  34.0 1.0 broadcast_in_dim.2
  34.9 3.9 %all-to-all-start = ((bf16[4,2,128,384]{3,2,1,0:T(8,128)(2,1)}), bf16[4,2,128,384]{3,2,1,0:T(8,128)(2,1)S(1)}, u32[]{:S(2)}, u32[]{:S(2)}) async-start(bf16[4,2,128,384]{3,2,1,0:T(8,128)(2,1)} %broadcast_in_dim.2), calls=%async_computation | async-start | bytes 1572864 | tf_op jit(solution)/shard_map/all_to_all | solution.py:53
  38.9 14.4 %all-gather.1 = bf16[8,128,384]{2,1,0:T(8,128)(2,1)S(1)} all-gather(bf16[2,128,384]{2,1,0:T(8,128)(2,1)S(1)} %collective-permute-done.1), channel_id=3, replica_groups={{0,128,256,384},{1,9,17,25},{2,130,258,386},{3,11,19,27},{4,132,260,388..., dimensions={0}, use_global_device_ids=true | all-gather | bytes 983040 | tf_op jit(solution)/shard_map/all_gather | solution.py:390
  53.3 0.0 copy-start.3
  53.3 1.1 copy-done.3
  54.4 6.7 %attend.1 = bf16[4,272,384]{2,1,0:T(8,128)(2,1)S(1)} custom-call(bf16[128,384]{1,0:T(8,128)(2,1)S(1)} %copy-done.6, bf16[3,128,384]{2,1,0:T(8,128)(2,1)S(1)} %copy-done.1, bf16[2,512,384]{2,1,0:T(8,128)(2,1)S(1)} %copy-done.3, bf16[2,128,384]{2,1,0:T(8,128)(2,1)S(1)} %copy-done.2, bf16[4,2,128,384]{3,2,1,0:T(8,128)(2,1)S(1)} %bitcast.7, ...), custom_call_target="tpu_custom_call" | custom-call | tf_op jit(solution)/shard_map/attend/pallas_call | solution.py:226
  61.1 12.0 %all_to_all.15.got = bf16[4,272,384]{2,1,0:T(8,128)(2,1)S(1)} all-to-all(bf16[4,272,384]{2,1,0:T(8,128)(2,1)S(1)} %attend.1), channel_id=1, replica_groups={{0,8,16,24},{1,129,257,385},{2,10,18,26},{3,131,259,387},{4,12,20,28},{..., dimensions={0} | all-to-all | bytes 1671168 | tf_op jit(solution)/shard_map/all_to_all | solution.py:53
  73.1 0.6 merge.1
  73.8 4.0 %collective-permute-start.2 = (bf16[144,384]{1,0:T(8,128)(2,1)S(1)}, bf16[144,384]{1,0:T(8,128)(2,1)S(1)}, u32[]{:S(2)}, u32[]{:S(2)}) collective-permute-start(bf16[144,384]{1,0:T(8,128)(2,1)S(1)} %get-tuple-element.24), channel_id=1, source_target_pairs={{0,96},{1,33},{2,98},{3,35},{4,100},{5,37},{6,102},{7,39},{8,104},... | collective-permute-start | bytes 331784 | tf_op jit(solution)/shard_map/ppermute | solution.py:35
  77.7 9.1 %collective-permute-done.2.theirs = bf16[144,384]{1,0:T(8,128)(2,1)S(1)} collective-permute-done((bf16[144,384]{1,0:T(8,128)(2,1)S(1)}, bf16[144,384]{1,0:T(8,128)(2,1)S(1)}, u32[]{:S(2)}, u32[]{:S(2)}) %collective-permute-start.2) | collective-permute-done | bytes 110624 | tf_op jit(solution)/shard_map/ppermute | solution.py:35
  86.8 1.0 project.1
  87.8 4.8 %collective-permute-start.3 = (bf16[4,128,384]{2,1,0:T(8,128)(2,1)S(1)}, bf16[4,128,384]{2,1,0:T(8,128)(2,1)S(1)}, u32[]{:S(2)}, u32[]{:S(2)}) collective-permute-start(bf16[4,128,384]{2,1,0:T(8,128)(2,1)S(1)} %get-tuple-element.26), channel_id=1, source_target_pairs={{0,1},{1,0},{2,3},{3,2},{4,5},{5,4},{6,7},{7,6},{8,9},{9,8},{10,11... | collective-permute-start | bytes 1179656 | tf_op jit(solution)/shard_map/ppermute | solution.py:35
  92.6 1.3 %collective-permute-done.3.got = bf16[4,128,384]{2,1,0:T(8,128)(2,1)S(1)} collective-permute-done((bf16[4,128,384]{2,1,0:T(8,128)(2,1)S(1)}, bf16[4,128,384]{2,1,0:T(8,128)(2,1)S(1)}, u32[]{:S(2)}, u32[]{:S(2)}) %collective-permute-start.3) | collective-permute-done | bytes 393248 | tf_op jit(solution)/shard_map/ppermute | solution.py:35
  94.0 0.8 pair_sum.1
  94.8 6.2 %all-to-all-start.2 = ((bf16[4,128,384]{2,1,0:T(8,128)(2,1)}), bf16[4,128,384]{2,1,0:T(8,128)(2,1)S(1)}, u32[]{:S(2)}, u32[]{:S(2)}) async-start(bf16[4,128,384]{2,1,0:T(8,128)(2,1)} %pair_sum.1), calls=%async_computation.2 | async-start | bytes 786432 | tf_op jit(solution)/shard_map/all_to_all | solution.py:53
  101.6 10.6 %all-to-all-done.2.got = bf16[4,128,384]{2,1,0:T(8,128)(2,1)S(1)} async-done(((bf16[4,128,384]{2,1,0:T(8,128)(2,1)}), bf16[4,128,384]{2,1,0:T(8,128)(2,1)S(1)}, u32[]{:S(2)}, u32[]{:S(2)}) %all-to-all-start.2) | async-done | bytes 393248 | tf_op jit(solution)/shard_map/all_to_all | solution.py:53
  112.2 0.7 finish.1
  (15 shorter events, 0.0 us)
Async XLA Ops:
  2.5 50.8 %copy-start.1 = (bf16[3,128,384]{2,1,0:T(8,128)(2,1)S(1)}, bf16[3,128,384]{2,1,0:T(8,128)(2,1)}, u32[]{:S(2)}) copy-start(bf16[3,128,384]{2,1,0:T(8,128)(2,1)} %raw.1) | copy-start | bytes 884740
  2.5 50.8 %copy-start.2 = (bf16[2,128,384]{2,1,0:T(8,128)(2,1)S(1)}, bf16[2,128,384]{2,1,0:T(8,128)(2,1)}, u32[]{:S(2)}) copy-start(bf16[2,128,384]{2,1,0:T(8,128)(2,1)} %stale) | copy-start | bytes 589828
  2.6 50.7 %copy-start.6 = (bf16[128,384]{1,0:T(8,128)(2,1)S(1)}, bf16[128,384]{1,0:T(8,128)(2,1)}, u32[]{:S(2)}) copy-start(bf16[128,384]{1,0:T(8,128)(2,1)} %get-tuple-element.16.k_fresh) | copy-start | bytes 294916
  2.6 30.5 %collective-permute-start = (bf16[128,384]{1,0:T(8,128)(2,1)}, bf16[128,384]{1,0:T(8,128)(2,1)S(1)}, u32[]{:S(2)}, u32[]{:S(2)}) collective-permute-start(bf16[128,384]{1,0:T(8,128)(2,1)} %get-tuple-element.21), channel_id=1, source_target_pairs={{0,96},{1,33},{2,98},{3,35},{4,100},{5,37},{6,102},{7,39},{8,104},... | collective-permute-start | bytes 294920 | tf_op jit(solution)/shard_map/ppermute | solution.py:35
  12.4 20.7 %collective-permute-start.1 = (bf16[2,128,384]{2,1,0:T(8,128)(2,1)}, bf16[2,128,384]{2,1,0:T(8,128)(2,1)S(1)}, u32[]{:S(2)}, u32[]{:S(2)}) collective-permute-start(bf16[2,128,384]{2,1,0:T(8,128)(2,1)} %stale), channel_id=1, source_target_pairs={{0,32},{1,97},{2,34},{3,99},{4,36},{5,101},{6,38},{7,103},{8,40},{... | collective-permute-start | bytes 589832 | tf_op jit(solution)/shard_map/ppermute | solution.py:35
  34.9 18.3 %all-to-all-start = ((bf16[4,2,128,384]{3,2,1,0:T(8,128)(2,1)}), bf16[4,2,128,384]{3,2,1,0:T(8,128)(2,1)S(1)}, u32[]{:S(2)}, u32[]{:S(2)}) async-start(bf16[4,2,128,384]{3,2,1,0:T(8,128)(2,1)} %broadcast_in_dim.2), calls=%async_computation | async-start | bytes 1572864 | tf_op jit(solution)/shard_map/all_to_all | solution.py:53
  53.3 1.1 %copy-start.3 = (bf16[2,512,384]{2,1,0:T(8,128)(2,1)S(1)}, bf16[2,512,384]{2,1,0:T(8,128)(2,1)}, u32[]{:S(2)}) copy-start(bf16[2,512,384]{2,1,0:T(8,128)(2,1)} %text.1) | copy-start | bytes 2359300
  61.1 25.7 %copy-start = (bf16[384,3072]{1,0:T(8,128)(2,1)S(1)}, bf16[384,3072]{1,0:T(8,128)(2,1)}, u32[]{:S(2)}) copy-start(bf16[384,3072]{1,0:T(8,128)(2,1)} %w.1) | copy-start | bytes 7077892
  73.8 13.1 %collective-permute-start.2 = (bf16[144,384]{1,0:T(8,128)(2,1)S(1)}, bf16[144,384]{1,0:T(8,128)(2,1)S(1)}, u32[]{:S(2)}, u32[]{:S(2)}) collective-permute-start(bf16[144,384]{1,0:T(8,128)(2,1)S(1)} %get-tuple-element.24), channel_id=1, source_target_pairs={{0,96},{1,33},{2,98},{3,35},{4,100},{5,37},{6,102},{7,39},{8,104},... | collective-permute-start | bytes 331784 | tf_op jit(solution)/shard_map/ppermute | solution.py:35
  86.8 25.4 %copy-start.4 = (bf16[128,384]{1,0:T(8,128)(2,1)S(1)}, bf16[128,384]{1,0:T(8,128)(2,1)}, u32[]{:S(2)}) copy-start(bf16[128,384]{1,0:T(8,128)(2,1)} %hidden.1) | copy-start | bytes 294916
  86.8 25.4 %copy-start.5 = (bf16[128,384]{1,0:T(8,128)(2,1)S(1)}, bf16[128,384]{1,0:T(8,128)(2,1)}, u32[]{:S(2)}) copy-start(bf16[128,384]{1,0:T(8,128)(2,1)} %control.1) | copy-start | bytes 294916
  86.8 25.4 %copy-start.7 = (f32[28,384]{1,0:T(8,128)S(1)}, f32[28,384]{1,0:T(8,128)}, u32[]{:S(2)}) copy-start(f32[28,384]{1,0:T(8,128)} %gate.1) | copy-start | bytes 129028
  87.8 6.2 %collective-permute-start.3 = (bf16[4,128,384]{2,1,0:T(8,128)(2,1)S(1)}, bf16[4,128,384]{2,1,0:T(8,128)(2,1)S(1)}, u32[]{:S(2)}, u32[]{:S(2)}) collective-permute-start(bf16[4,128,384]{2,1,0:T(8,128)(2,1)S(1)} %get-tuple-element.26), channel_id=1, source_target_pairs={{0,1},{1,0},{2,3},{3,2},{4,5},{5,4},{6,7},{7,6},{8,9},{9,8},{10,11... | collective-permute-start | bytes 1179656 | tf_op jit(solution)/shard_map/ppermute | solution.py:35
  94.8 17.4 %all-to-all-start.2 = ((bf16[4,128,384]{2,1,0:T(8,128)(2,1)}), bf16[4,128,384]{2,1,0:T(8,128)(2,1)S(1)}, u32[]{:S(2)}, u32[]{:S(2)}) async-start(bf16[4,128,384]{2,1,0:T(8,128)(2,1)} %pair_sum.1), calls=%async_computation.2 | async-start | bytes 786432 | tf_op jit(solution)/shard_map/all_to_all | solution.py:53

commit v2 on v1

--- a/solution.py
+++ b/solution.py
@@ -1,3 +1,4 @@
+import functools
 import math
 
 import jax
@@ -35,17 +36,18 @@
     return lax.ppermute(value, AXES, pairs)
 
 
-def rings(axis_of_core):
+def squares(flip):
     groups = {}
     for i in range(512):
         y, zh, x, zl, c = coords(i)
-        rest = (y, zh, zl, c) if axis_of_core[c] == "x" else (x, zh, zl, c)
-        groups.setdefault(rest, []).append(i)
+        f = flip[c]
+        groups.setdefault((min(x, x ^ f), min(y, y ^ f), zh, zl, c), []).append(i)
     return list(groups.values())
 
 
-QUERY_RINGS = rings("xy")
-KEY_RINGS = rings("yx")
+QUERY_FLIPS = (1, 3)
+QUERY_GROUPS = squares(QUERY_FLIPS)
+KEY_FLIPS = (3, 1)
 Z_RUNS = [[0, 2, 4, 6], [1, 3, 5, 7]]
 
 
@@ -53,11 +55,40 @@
     return lax.all_to_all(value, axes, 0, 0, axis_index_groups=groups, tiled=True)
 
 
-def ring_places():
+def query_place():
     patch = lax.axis_index("patch")
     x, y = patch % 4, patch // 16
     first = lax.axis_index("tensor") % 2 == 0
-    return jnp.where(first, x, y), jnp.where(first, y, x)
+    return jnp.where(first, y % 2 * 2 + x % 2, y // 2 * 2 + x // 2)
+
+
+def key_square(value):
+    def move(dx, dy):
+        return permute(
+            value,
+            lambda y, zh, x, zl, c: (y ^ dy * KEY_FLIPS[c], zh, x ^ dx * KEY_FLIPS[c], zl, c),
+        )
+
+    return [value, move(1, 0), move(0, 1), move(1, 1)]
+
+
+def spread_kernel(*refs):
+    out = refs[-1]
+    for i in range(4):
+        for j, ref in enumerate(refs[:-1]):
+            out[i, j] = ref[...]
+
+
+def spread(*values):
+    full = pl.BlockSpec(memory_space=pltpu.VMEM)
+    return pl.pallas_call(
+        spread_kernel,
+        out_shape=jax.ShapeDtypeStruct((4, len(values)) + values[0].shape, BF16),
+        in_specs=[full] * len(values),
+        out_specs=full,
+        compiler_params=pltpu.CompilerParams(vmem_limit_bytes=16 * MIB),
+        name="spread",
+    )(*values)
 
 
 def key_pair(value):
@@ -156,10 +187,11 @@
     return hi, mid, rest - mid
 
 
-def attend(q, keys, values):
-    s = [
-        lax.dot_general(q, k, (((1,), (1,)), ((), ())), preferred_element_type=F32) for k in keys
-    ]
+def scores(q, k):
+    return lax.dot_general(q, k, (((1,), (1,)), ((), ())), preferred_element_type=F32)
+
+
+def attend(s, values):
     top = jnp.max(s[0], axis=1, keepdims=True)
     for t in s[1:]:
         top = jnp.maximum(top, jnp.max(t, axis=1, keepdims=True))
@@ -167,76 +199,89 @@
     acc = None
     for t, v in zip(s, values):
         p = jnp.exp2(t * SCALE2 - top).astype(BF16)
+        v = jnp.concatenate([v, jnp.ones(v.shape, BF16)], axis=1)
         part = jnp.dot(p, v, preferred_element_type=F32)
         acc = part if acc is None else acc + part
     total = acc[:, HD:]
     return acc[:, :HD] / total, top + jnp.log2(total)
 
 
-def attn_kernel(k_fresh, raw, text, stale, kv_own, kv_pair, q, out, kc, vc, kt, vt):
-    q_at, k_at = ring_places()
-    own_rows = pl.ds(pl.multiple_of(k_at * TOK, TOK), TOK)
+def put(out, o, lse):
+    lane = lax.broadcasted_iota(jnp.int32, (TOK, HD), 1)
+    stat = jnp.zeros((TOK, HD), F32)
+    for h in range(HEADS_DEV):
+        out[0:TOK, h * HD : (h + 1) * HD] = o[h].astype(BF16)
+        for part, v in enumerate(split3(lse[h])):
+            stat = jnp.where(lane == 3 * h + part, v, stat)
+    out[TOK:, :] = jnp.zeros((STAT, WIDTH), BF16)
+    out[TOK:, 0:HD] = stat.T[:STAT].astype(BF16)
+
+
+def home_kernel(q, k_fresh, raw, text, out):
+    o, lse = [], []
     for h in range(HEADS_DEV):
         cut = slice(h * HD, (h + 1) * HD)
-        for b in range(4):
-            for at, kv in ((b, kv_own), (4 + b, kv_pair)):
-                kc[h, at * TOK : (at + 1) * TOK, :] = kv[b, 0, :, cut]
-                vc[h, at * TOK : (at + 1) * TOK, 0:HD] = kv[b, 1, :, cut]
-        kc[h, own_rows, :] = k_fresh[:, cut]
-        vc[h, own_rows, 0:HD] = raw[2, :, cut]
-        vc[h, :, HD:] = jnp.ones((8 * TOK, HD), BF16)
-        kt[h] = text[0, :, cut]
-        vt[h, :, 0:HD] = text[1, :, cut]
-        vt[h, :, HD:] = jnp.ones((TXT, HD), BF16)
-    lane = lax.broadcasted_iota(jnp.int32, (TOK, HD), 1)
-
-    def one(ring, half, own):
-        stat = jnp.zeros((TOK, HD), F32)
-        for h in range(HEADS_DEV):
-            cut = slice(h * HD, (h + 1) * HD)
-            keys, values = [kc[h]], [vc[h]]
-            if own:
-                keys.append(kt[h])
-                values.append(vt[h])
-            o, lse = attend(q[ring, half, :, cut], keys, values)
-            out[ring, half * TOK : (half + 1) * TOK, cut] = o.astype(BF16)
-            for part, v in enumerate(split3(lse)):
-                stat = jnp.where(lane == 3 * h + part, v, stat)
-        out[ring, 2 * TOK :, half * HD : (half + 1) * HD] = stat.T[:STAT].astype(BF16)
-
-    out[:, 2 * TOK :, :] = jnp.zeros((4, STAT, WIDTH), BF16)
-    one(q_at, 0, True)
+        keys = jnp.concatenate([k_fresh[:, cut], text[0, :, cut]], axis=0)
+        values = jnp.concatenate([raw[2, :, cut], text[1, :, cut]], axis=0)
+        a, b = attend([scores(q[:, cut], keys)], [values])
+        o.append(a)
+        lse.append(b)
+    put(out, o, lse)
+
+
+def attend_home(*args):
+    full = pl.BlockSpec(memory_space=pltpu.VMEM)
+    return pl.pallas_call(
+        home_kernel,
+        out_shape=jax.ShapeDtypeStruct((TOK + STAT, WIDTH), BF16),
+        in_specs=[full] * 4,
+        out_specs=full,
+        compiler_params=pltpu.CompilerParams(vmem_limit_bytes=16 * MIB),
+        cost_estimate=pl.CostEstimate(
+            flops=4 * TOK * 5 * TOK * WIDTH, bytes_accessed=MIB, transcendentals=2**18
+        ),
+        name="attend_home",
+    )(*args)
+
+
+def attn_kernel(half, *refs):
+    kv, q, out = refs[:8], refs[8], refs[9]
+    at = query_place()
+    o = [[None] * HEADS_DEV for _ in range(4)]
+    lse = [[None] * HEADS_DEV for _ in range(4)]
     for h in range(HEADS_DEV):
         cut = slice(h * HD, (h + 1) * HD)
-        kc[h, own_rows, :] = stale[0, :, cut]
-        vc[h, own_rows, 0:HD] = stale[1, :, cut]
-    one(q_at, 1, False)
-
-    def step(d, carry):
-        ring = (q_at + d) % 4
-        one(ring, 0, False)
-        one(ring, 1, False)
-        return carry
-
-    lax.fori_loop(1, 4, step, 0)
-
-
-def attention(*args):
-    full = pl.BlockSpec(memory_space=pltpu.VMEM)
-    return pl.pallas_call(
-        attn_kernel,
-        out_shape=jax.ShapeDtypeStruct((4, 2 * TOK + STAT, WIDTH), BF16),
-        in_specs=[full] * 7,
-        out_specs=full,
-        scratch_shapes=[
-            pltpu.VMEM((HEADS_DEV, 8 * TOK, HD), BF16),
-            pltpu.VMEM((HEADS_DEV, 8 * TOK, 2 * HD), BF16),
-            pltpu.VMEM((HEADS_DEV, TXT, HD), BF16),
-            pltpu.VMEM((HEADS_DEV, TXT, 2 * HD), BF16),
-        ],
+        keys = jnp.concatenate([r[0, :, cut] for r in kv], axis=0)
+        values = jnp.concatenate([r[1, :, cut] for r in kv], axis=0)
+        for pair in (0, 2):
+            rows = jnp.concatenate([q[at ^ pair, half, :, cut], q[at ^ (pair + 1), half, :, cut]], axis=0)
+            s = scores(rows, keys)
+            if half == 0 and pair == 0:
+                hidden = jnp.full((TOK, TOK), -jnp.inf, F32)
+                s = jnp.concatenate(
+                    [jnp.concatenate([hidden, s[:TOK, TOK:]], axis=1), s[TOK:]], axis=0
+                )
+            a, b = attend([s], [values])
+            for i in range(2):
+                o[pair + i][h] = a[i * TOK : (i + 1) * TOK]
+                lse[pair + i][h] = b[i * TOK : (i + 1) * TOK]
+    for d in range(4):
+        put(out.at[at ^ d], o[d], lse[d])
+
+
+def attention(half, kv, q):
+    full = pl.BlockSpec(memory_space=pltpu.VMEM)
+    return pl.pallas_call(
+        functools.partial(attn_kernel, half),
+        out_shape=jax.ShapeDtypeStruct((4, TOK + STAT, WIDTH), BF16),
+        in_specs=[full] * 9,
+        out_specs=full,
         compiler_params=pltpu.CompilerParams(vmem_limit_bytes=32 * MIB),
-        name="attend",
-    )(*args)
+        cost_estimate=pl.CostEstimate(
+            flops=4 * 4 * TOK * 8 * TOK * WIDTH, bytes_accessed=4 * MIB, transcendentals=2**21
+        ),
+        name="attend_own" if half == 0 else "attend_pair",
+    )(*kv, q)
 
 
 def merge(parts, stats):
@@ -270,51 +315,64 @@
     return outs, lses
 
 
-def merge_kernel(got, keep, send):
-    refs = [got.at[i] for i in range(4)]
+def partials(ref):
+    return (
+        [lambda h, i=i: ref[i, 0:TOK, h * HD : (h + 1) * HD].astype(F32) for i in range(4)],
+        [ref[i, TOK:, 0:HD].astype(F32) for i in range(4)],
+    )
+
+
+def merge_kernel(got, out):
+    outs, lses = merge(*partials(got))
     sub = lax.broadcasted_iota(jnp.int32, (STAT, HD), 0)
-    for half, out in ((0, keep), (1, send)):
-        parts = [
-            lambda h, r=r: r[half * TOK : (half + 1) * TOK, h * HD : (h + 1) * HD].astype(F32)
-            for r in refs
-        ]
-        stats = [r[2 * TOK :, half * HD : (half + 1) * HD].astype(F32) for r in refs]
-        outs, lses = merge(parts, stats)
-        table = jnp.zeros((STAT, HD), F32)
-        for h in range(HEADS_DEV):
-            out[0:TOK, h * HD : (h + 1) * HD] = outs[h].astype(BF16)
-            for part, v in enumerate(split3(lses[h])):
-                table = jnp.where(sub == 3 * h + part, v, table)
-        out[TOK:, :] = jnp.zeros((STAT, WIDTH), BF16)
-        out[TOK:, 0:HD] = table.astype(BF16)
+    table = jnp.zeros((STAT, HD), F32)
+    for h in range(HEADS_DEV):
+        out[0:TOK, h * HD : (h + 1) * HD] = outs[h].astype(BF16)
+        for part, v in enumerate(split3(lses[h])):
+            table = jnp.where(sub == 3 * h + part, v, table)
+    out[TOK:, :] = jnp.zeros((STAT, WIDTH), BF16)
+    out[TOK:, 0:HD] = table.astype(BF16)
 
 
 def merge_first(messages):
     full = pl.BlockSpec(memory_space=pltpu.VMEM)
     return pl.pallas_call(
         merge_kernel,
-        out_shape=(jax.ShapeDtypeStruct((TOK + STAT, WIDTH), BF16),) * 2,
+        out_shape=jax.ShapeDtypeStruct((TOK + STAT, WIDTH), BF16),
         in_specs=[full],
-        out_specs=(full, full),
+        out_specs=full,
         compiler_params=pltpu.CompilerParams(vmem_limit_bytes=16 * MIB),
         name="merge",
     )(messages)
 
 
-def project_kernel(mine, theirs, w, keep, give, att):
-    refs = (mine, theirs)
-    parts = [lambda h, r=r: r[0:TOK, h * HD : (h + 1) * HD].astype(F32) for r in refs]
-    outs, _ = merge(parts, [r[TOK:, 0:HD].astype(F32) for r in refs])
+def project_kernel(mine, theirs, home, w_hbm, keep, give, att, w, sem):
+    core = lax.axis_index("tensor") % 2
+    order = [(c, z) for c in range(2) for z in range(4)]
+
+    def columns(c, z):
+        return pl.ds(pl.multiple_of((2 * z + (core + 1 - c) % 2) * WIDTH, HD), WIDTH)
+
+    copies = [
+        pltpu.make_async_copy(w_hbm.at[:, columns(c, z)], w.at[c, z], sem.at[4 * c + z])
+        for c, z in order
+    ]
+    for c in copies:
+        c.start()
+    parts, stats = partials(mine)
+    for ref in (theirs, home):
+        parts.append(lambda h, ref=ref: ref[0:TOK, h * HD : (h + 1) * HD].astype(F32))
+        stats.append(ref[TOK:, 0:HD].astype(F32))
+    outs, _ = merge(parts, stats)
     for h in range(HEADS_DEV):
         att[:, h * HD : (h + 1) * HD] = outs[h].astype(BF16)
-    core = lax.axis_index("tensor") % 2
-    for z in range(4):
-        for out, c in ((give, 1 - core), (keep, core)):
-            part = w[:, pl.ds(pl.multiple_of((2 * z + c) * WIDTH, HD), WIDTH)]
-            out[z] = jnp.dot(att[...], part, preferred_element_type=F32).astype(out.dtype)
-
-
-def project(mine, theirs, out_weight):
+    for copy, (c, z) in zip(copies, order):
+        copy.wait()
+        out = keep if c else give
+        out[z] = jnp.dot(att[...], w[c, z], preferred_element_type=F32).astype(out.dtype)
+
+
+def project(mine, theirs, home, out_weight):
     full = pl.BlockSpec(memory_space=pltpu.VMEM)
     return pl.pallas_call(
         project_kernel,
@@ -322,12 +380,16 @@
             jax.ShapeDtypeStruct((4, TOK, WIDTH), F32),
             jax.ShapeDtypeStruct((4, TOK, WIDTH), BF16),
         ),
-        in_specs=[full] * 3,
+        in_specs=[full] * 3 + [pl.BlockSpec(memory_space=pltpu.HBM)],
         out_specs=(full, full),
-        scratch_shapes=[pltpu.VMEM((TOK, WIDTH), BF16)],
-        compiler_params=pltpu.CompilerParams(vmem_limit_bytes=16 * MIB),
+        scratch_shapes=[
+            pltpu.VMEM((TOK, WIDTH), BF16),
+            pltpu.VMEM((2, 4, WIDTH, WIDTH), BF16),
+            pltpu.SemaphoreType.DMA((8,)),
+        ],
+        compiler_params=pltpu.CompilerParams(vmem_limit_bytes=56 * MIB),
         name="project",
-    )(mine, theirs, out_weight)
+    )(mine, theirs, home, out_weight)
 
 
 def pair_kernel(keep, got, out):
@@ -383,14 +445,17 @@
     q, k_fresh = prepare(fresh_qkv, positions, query_gain, key_gain)
     pair_q = query_pair(q)
     stale_kv, q = lax.optimization_barrier((stale_kv, q))
-    kv_own = lax.all_gather(stale_kv, AXES, axis_index_groups=KEY_RINGS)
-    pair_q, pair_kv, kv_own = lax.optimization_barrier((pair_q, pair_kv, kv_own))
-    q_two = jnp.broadcast_to(jnp.stack([q, pair_q])[None], (4, 2, TOK, WIDTH))
-    q_all = exchange(q_two, AXES, QUERY_RINGS)
-    kv_pair = lax.all_gather(pair_kv, AXES, axis_index_groups=KEY_RINGS)
-    partial = attention(k_fresh, fresh_qkv, text_kv, stale_kv, kv_own, kv_pair, q_all)
-    keep, send = merge_first(exchange(partial, AXES, QUERY_RINGS))
-    keep, give = project(keep, query_pair(send), out_weight)
+    kv = key_square(stale_kv)
+    queries, pair_kv = lax.optimization_barrier((spread(q, pair_q), pair_kv))
+    q_all = exchange(queries, AXES, QUERY_GROUPS)
+    kv += key_square(pair_kv)
+    home = attend_home(q, k_fresh, fresh_qkv, text_kv)
+    paired = exchange(attention(1, kv, q_all), AXES, QUERY_GROUPS)
+    partial = attention(0, kv, q_all)
+    send, partial = lax.optimization_barrier((merge_first(paired), partial))
+    theirs = query_pair(send)
+    mine = exchange(partial, AXES, QUERY_GROUPS)
+    keep, give = project(mine, theirs, home, out_weight)
     parts = exchange(pair_sum(keep, swap_core(give)), "tensor", Z_RUNS)
     return finish(timestep, parts, gate_table, hidden_in, control)
 

time: 113 us -> 124 us (1.097)
  blocking collectives: 38.3 us -> 0 us
  starting transfers between devices: 37.5 us -> 75 us
  Pallas kernels: 12.3 us -> 17.8 us
  local copies, waits for them, and re-layouts: 2.12 us -> 6.9 us
  waiting for transfers between devices: 21 us -> 22.4 us
    all_gather x2 -> x0, blocking collectives: 26.3 us -> none  [the longest x1 14.4 us: body(): kv_pair = lax.all_gather(pair_kv, AXES, axis_index_groups=KEY_RINGS)]
    ppermute x4 -> x10, starting transfers between devices: 27.4 us -> 50.6 us  [permute(): return lax.ppermute(value, AXES, pairs)]
    all_to_all x2 -> x4, starting transfers between devices: 10.1 us -> 24.4 us  [exchange(): lax.all_to_all(value, axes, 0, 0, axis_index_groups=groups, tiled=True)]
    all_to_all x1 -> x0, blocking collectives: 12 us -> none  [exchange(): lax.all_to_all(value, axes, 0, 0, axis_index_groups=groups, tiled=True)]
    unnamed x16 -> x38, local copies, waits for them, and re-layouts: 1.16 us -> 6.9 us
    pallas_call x1, Pallas kernels: 0.97 us -> 4.82 us  [project(): pl.pallas_call(project_kernel, out_shape=(jax.ShapeDtypeStruct((4, TOK, W...]
    pallas_call x2 -> x5, Pallas kernels: 7.29 us -> 8.89 us  [the longest x2 6.68 us: attention(): pl.pallas_call(functools.partial(attn_kernel, half), out_shape=jax.ShapeD...]
    all_to_all x2 -> x4, waiting for transfers between devices: 10.6 us -> 11.6 us  [exchange(): lax.all_to_all(value, axes, 0, 0, axis_index_groups=groups, tiled=True)]
  transfers between devices with their start and end apart: 6 -> 14, of which waited for: 3 -> 7; matrix products, arithmetic and copies ran while one was open for 0% -> 0% of each run, Pallas kernels for 0% -> 6%
where the time goes in v2:
time: 124 us; the launch traced here: 123 us
  starting transfers between devices  75 us (60%)
  waiting for transfers between devices  22.4 us (18%)
  Pallas kernels  17.8 us (14%)
  local copies, waits for them, and re-layouts  6.9 us (6%)
    ppermute x10, starting transfers between devices, permute(): return lax.ppermute(value, AXES, pairs)  50.6 us
    all_to_all x4, starting transfers between devices, exchange(): lax.all_to_all(value, axes, 0, 0, axis_index_groups=groups, tiled=True)  24.4 us
    all_to_all x4, waiting for transfers between devices, exchange(): lax.all_to_all(value, axes, 0, 0, axis_index_groups=groups, tiled=True)  11.6 us
    ppermute x10, waiting for transfers between devices, permute(): return lax.ppermute(value, AXES, pairs)  10.8 us
    unnamed x38, local copies, waits for them, and re-layouts  6.9 us
    pallas_call x2, Pallas kernels, attention(): pl.pallas_call(functools.partial(attn_kernel, half), out_shape=jax.ShapeD...  6.68 us
    pallas_call x1, Pallas kernels, project(): pl.pallas_call(project_kernel, out_shape=(jax.ShapeDtypeStruct((4, TOK, W...  4.82 us
    pallas_call x1, Pallas kernels, prepare(): pl.pallas_call(prep_kernel, out_shape=(jax.ShapeDtypeStruct((TOK, WIDTH),...  2.54 us
  transfers between devices with their start and end apart: 14, of which 7 were waited for; matrix products, arithmetic and copies ran while one was open for 0% of the time, Pallas kernels for 6%

profile of v2, /device:TPU:1, one launch (start us, length us, event | category | flops | bytes accessed | tf_op | source)
XLA Modules:
  0.0 123.0 jit_solution(13566098026127872628)
XLA Ops:
  0.0 13.4 %collective-permute-start.4 = (bf16[2,128,384]{2,1,0:T(8,128)(2,1)}, bf16[2,128,384]{2,1,0:T(8,128)(2,1)S(1)}, u32[]{:S(2)}, u32[]{:S(2)}) collective-permute-start(bf16[2,128,384]{2,1,0:T(8,128)(2,1)} %refs_0_.1), channel_id=1, source_target_pairs={{0,32},{1,97},{2,34},{3,99},{4,36},{5,101},{6,38},{7,103},{8,40},{... | collective-permute-start | bytes 589832 | tf_op jit(solution)/shard_map/ppermute | solution.py:36
  13.4 2.5 %prep.1 = (bf16[128,384]{1,0:T(8,128)(2,1)}, bf16[128,384]{1,0:T(8,128)(2,1)}) custom-call(bf16[3,128,384]{2,1,0:T(8,128)(2,1)} %raw.1, s32[1,128]{1,0:T(1,128)} %bitcast.3, f32[8,128]{1,0:T(8,128)} %constant.2.clone.freq_hbm, f32[1,128]{1,0:T(1,128)} %bitcast.4, f32[1,128]{1,0:T(1,128)} %bitcast.5), custom_call_target="tpu_custom_call" | custom-call | tf_op jit(solution)/shard_map/prep/pallas_call | solution.py:160
  16.0 5.2 %collective-permute-start.3 = (bf16[128,384]{1,0:T(8,128)(2,1)}, bf16[128,384]{1,0:T(8,128)(2,1)S(1)}, u32[]{:S(2)}, u32[]{:S(2)}) collective-permute-start(bf16[128,384]{1,0:T(8,128)(2,1)} %get-tuple-element.17.refs_0_.q), channel_id=1, source_target_pairs={{0,96},{1,33},{2,98},{3,35},{4,100},{5,37},{6,102},{7,39},{8,104},... | collective-permute-start | bytes 294920 | tf_op jit(solution)/shard_map/ppermute | solution.py:36
  21.2 4.8 %collective-permute-done.3.refs_1_ = bf16[128,384]{1,0:T(8,128)(2,1)S(1)} collective-permute-done((bf16[128,384]{1,0:T(8,128)(2,1)}, bf16[128,384]{1,0:T(8,128)(2,1)S(1)}, u32[]{:S(2)}, u32[]{:S(2)}) %collective-permute-start.3) | collective-permute-done | bytes 98336 | tf_op jit(solution)/shard_map/ppermute | solution.py:36
  27.9 6.2 %all-to-all-start = ((bf16[4,2,128,384]{3,2,1,0:T(8,128)(2,1)}), bf16[4,2,128,384]{3,2,1,0:T(8,128)(2,1)S(1)}, u32[]{:S(2)}, u32[]{:S(2)}) async-start(bf16[4,2,128,384]{3,2,1,0:T(8,128)(2,1)} %spread.1), calls=%async_computation | async-start | bytes 1572864 | tf_op jit(solution)/shard_map/all_to_all | solution.py:55
  34.1 1.9 %collective-permute-start.2 = (bf16[2,128,384]{2,1,0:T(8,128)(2,1)S(1)}, bf16[2,128,384]{2,1,0:T(8,128)(2,1)S(1)}, u32[]{:S(2)}, u32[]{:S(2)}) collective-permute-start(bf16[2,128,384]{2,1,0:T(8,128)(2,1)S(1)} %copy-done.10), channel_id=1, source_target_pairs={{0,408},{1,137},{2,410},{3,139},{4,412},{5,141},{6,414},{7,143},{8... | collective-permute-start | bytes 589832 | tf_op jit(solution)/shard_map/ppermute | solution.py:36
  36.0 3.0 %collective-permute-start.1 = (bf16[2,128,384]{2,1,0:T(8,128)(2,1)S(1)}, bf16[2,128,384]{2,1,0:T(8,128)(2,1)S(1)}, u32[]{:S(2)}, u32[]{:S(2)}) collective-permute-start(bf16[2,128,384]{2,1,0:T(8,128)(2,1)S(1)} %copy-done.10), channel_id=1, source_target_pairs={{0,384},{1,129},{2,386},{3,131},{4,388},{5,133},{6,390},{7,135},{8... | collective-permute-start | bytes 589832 | tf_op jit(solution)/shard_map/ppermute | solution.py:36
  39.0 3.4 %collective-permute-start = (bf16[2,128,384]{2,1,0:T(8,128)(2,1)S(1)}, bf16[2,128,384]{2,1,0:T(8,128)(2,1)S(1)}, u32[]{:S(2)}, u32[]{:S(2)}) collective-permute-start(bf16[2,128,384]{2,1,0:T(8,128)(2,1)S(1)} %copy-done.10), channel_id=1, source_target_pairs={{0,24},{1,9},{2,26},{3,11},{4,28},{5,13},{6,30},{7,15},{8,16},{9,1... | collective-permute-start | bytes 589832 | tf_op jit(solution)/shard_map/ppermute | solution.py:36
  42.4 1.9 %collective-permute-start.7 = (bf16[2,128,384]{2,1,0:T(8,128)(2,1)S(1)}, bf16[2,128,384]{2,1,0:T(8,128)(2,1)S(1)}, u32[]{:S(2)}, u32[]{:S(2)}) collective-permute-start(bf16[2,128,384]{2,1,0:T(8,128)(2,1)S(1)} %collective-permute-done.4.refs_4_), channel_id=1, source_target_pairs={{0,408},{1,137},{2,410},{3,139},{4,412},{5,141},{6,414},{7,143},{8... | collective-permute-start | bytes 589832 | tf_op jit(solution)/shard_map/ppermute | solution.py:36
  44.4 3.1 %collective-permute-start.6 = (bf16[2,128,384]{2,1,0:T(8,128)(2,1)S(1)}, bf16[2,128,384]{2,1,0:T(8,128)(2,1)S(1)}, u32[]{:S(2)}, u32[]{:S(2)}) collective-permute-start(bf16[2,128,384]{2,1,0:T(8,128)(2,1)S(1)} %collective-permute-done.4.refs_4_), channel_id=1, source_target_pairs={{0,384},{1,129},{2,386},{3,131},{4,388},{5,133},{6,390},{7,135},{8... | collective-permute-start | bytes 589832 | tf_op jit(solution)/shard_map/ppermute | solution.py:36
  47.5 3.4 %collective-permute-start.5 = (bf16[2,128,384]{2,1,0:T(8,128)(2,1)S(1)}, bf16[2,128,384]{2,1,0:T(8,128)(2,1)S(1)}, u32[]{:S(2)}, u32[]{:S(2)}) collective-permute-start(bf16[2,128,384]{2,1,0:T(8,128)(2,1)S(1)} %collective-permute-done.4.refs_4_), channel_id=1, source_target_pairs={{0,24},{1,9},{2,26},{3,11},{4,28},{5,13},{6,30},{7,15},{8,16},{9,1... | collective-permute-start | bytes 589832 | tf_op jit(solution)/shard_map/ppermute | solution.py:36
  51.9 2.3 %collective-permute-done.5.refs_5_ = bf16[2,128,384]{2,1,0:T(8,128)(2,1)S(1)} collective-permute-done((bf16[2,128,384]{2,1,0:T(8,128)(2,1)S(1)}, bf16[2,128,384]{2,1,0:T(8,128)(2,1)S(1)}, u32[]{:S(2)}, u32[]{:S(2)}) %collective-permute-start.5) | collective-permute-done | bytes 196640 | tf_op jit(solution)/shard_map/ppermute | solution.py:36
  54.2 3.4 %attend_pair.1 = bf16[4,144,384]{2,1,0:T(8,128)(2,1)} custom-call(bf16[2,128,384]{2,1,0:T(8,128)(2,1)S(1)} %copy-done.10, bf16[2,128,384]{2,1,0:T(8,128)(2,1)S(1)} %collective-permute-done.refs_1_, bf16[2,128,384]{2,1,0:T(8,128)(2,1)S(1)} %collective-permute-done.1.refs_2_, bf16[2,128,384]{2,1,0:T(8,128)(2,1)S(1)} %collective-permute-done.2.refs_3_, ...), custom_call_target="tpu_custom_call" | custom-call | flops 805306368 | bytes 4194304 | tf_op jit(solution)/shard_map/attend_pair/pallas_call | solution.py:274
  57.6 6.1 %all-to-all-start.1 = ((bf16[4,144,384]{2,1,0:T(8,128)(2,1)}), bf16[4,144,384]{2,1,0:T(8,128)(2,1)S(1)}, u32[]{:S(2)}, u32[]{:S(2)}) async-start(bf16[4,144,384]{2,1,0:T(8,128)(2,1)} %attend_pair.1), calls=%async_computation.1 | async-start | bytes 884736 | tf_op jit(solution)/shard_map/all_to_all | solution.py:55
  66.4 3.3 %attend_own.1 = bf16[4,144,384]{2,1,0:T(8,128)(2,1)} custom-call(bf16[2,128,384]{2,1,0:T(8,128)(2,1)S(1)} %copy-done.10, bf16[2,128,384]{2,1,0:T(8,128)(2,1)S(1)} %collective-permute-done.refs_1_, bf16[2,128,384]{2,1,0:T(8,128)(2,1)S(1)} %collective-permute-done.1.refs_2_, bf16[2,128,384]{2,1,0:T(8,128)(2,1)S(1)} %collective-permute-done.2.refs_3_, ...), custom_call_target="tpu_custom_call" | custom-call | flops 805306368 | bytes 4194304 | tf_op jit(solution)/shard_map/attend_own/pallas_call | solution.py:274
  71.2 5.1 %all-to-all-start.2 = ((bf16[4,144,384]{2,1,0:T(8,128)(2,1)}), bf16[4,144,384]{2,1,0:T(8,128)(2,1)S(1)}, u32[]{:S(2)}, u32[]{:S(2)}) async-start(bf16[4,144,384]{2,1,0:T(8,128)(2,1)} %attend_own.1), calls=%async_computation.2 | async-start | bytes 884736 | tf_op jit(solution)/shard_map/all_to_all | solution.py:55
  76.2 6.7 %collective-permute-start.8 = (bf16[144,384]{1,0:T(8,128)(2,1)S(1)}, bf16[144,384]{1,0:T(8,128)(2,1)S(1)}, u32[]{:S(2)}, u32[]{:S(2)}) collective-permute-start(bf16[144,384]{1,0:T(8,128)(2,1)S(1)} %merge.1), channel_id=1, source_target_pairs={{0,96},{1,33},{2,98},{3,35},{4,100},{5,37},{6,102},{7,39},{8,104},... | collective-permute-start | bytes 331784 | tf_op jit(solution)/shard_map/ppermute | solution.py:36
  84.5 1.1 collective-permute-done.8.theirs
  87.1 4.8 %project.1 = (f32[4,128,384]{2,1,0:T(8,128)}, bf16[4,128,384]{2,1,0:T(8,128)(2,1)}) custom-call(bf16[4,144,384]{2,1,0:T(8,128)(2,1)} %copy-done.17, bf16[144,384]{1,0:T(8,128)(2,1)} %copy-done.18, bf16[144,384]{1,0:T(8,128)(2,1)} %copy-done.3, bf16[384,3072]{1,0:T(8,128)(2,1)} %w_hbm.1), custom_call_target="tpu_custom_call" | custom-call | tf_op jit(solution)/shard_map/project/pallas_call | solution.py:377
  91.9 8.6 %collective-permute-start.9 = (bf16[4,128,384]{2,1,0:T(8,128)(2,1)}, bf16[4,128,384]{2,1,0:T(8,128)(2,1)S(1)}, u32[]{:S(2)}, u32[]{:S(2)}) collective-permute-start(bf16[4,128,384]{2,1,0:T(8,128)(2,1)} %get-tuple-element.24), channel_id=1, source_target_pairs={{0,1},{1,0},{2,3},{3,2},{4,5},{5,4},{6,7},{7,6},{8,9},{9,8},{10,11... | collective-permute-start | bytes 1179656 | tf_op jit(solution)/shard_map/ppermute | solution.py:36
  100.5 1.5 %collective-permute-done.9.got = bf16[4,128,384]{2,1,0:T(8,128)(2,1)S(1)} collective-permute-done((bf16[4,128,384]{2,1,0:T(8,128)(2,1)}, bf16[4,128,384]{2,1,0:T(8,128)(2,1)S(1)}, u32[]{:S(2)}, u32[]{:S(2)}) %collective-permute-start.9) | collective-permute-done | bytes 393248 | tf_op jit(solution)/shard_map/ppermute | solution.py:36
  102.0 1.1 copy-done.1
  104.0 7.1 %all-to-all-start.3 = ((bf16[4,128,384]{2,1,0:T(8,128)(2,1)}), bf16[4,128,384]{2,1,0:T(8,128)(2,1)S(1)}, u32[]{:S(2)}, u32[]{:S(2)}) async-start(bf16[4,128,384]{2,1,0:T(8,128)(2,1)} %pair_sum.1), calls=%async_computation.3 | async-start | bytes 786432 | tf_op jit(solution)/shard_map/all_to_all | solution.py:55
  111.7 10.6 %all-to-all-done.3.got = bf16[4,128,384]{2,1,0:T(8,128)(2,1)S(1)} async-done(((bf16[4,128,384]{2,1,0:T(8,128)(2,1)}), bf16[4,128,384]{2,1,0:T(8,128)(2,1)S(1)}, u32[]{:S(2)}, u32[]{:S(2)}) %all-to-all-start.3) | async-done | bytes 393248 | tf_op jit(solution)/shard_map/all_to_all | solution.py:55
  (51 shorter events, 11.6 us)
Async XLA Ops:
  0.0 34.1 %copy-start.10 = (bf16[2,128,384]{2,1,0:T(8,128)(2,1)S(1)}, bf16[2,128,384]{2,1,0:T(8,128)(2,1)}, u32[]{:S(2)}) copy-start(bf16[2,128,384]{2,1,0:T(8,128)(2,1)} %refs_0_.1) | copy-start | bytes 589828
  0.0 27.9 %collective-permute-start.4 = (bf16[2,128,384]{2,1,0:T(8,128)(2,1)}, bf16[2,128,384]{2,1,0:T(8,128)(2,1)S(1)}, u32[]{:S(2)}, u32[]{:S(2)}) collective-permute-start(bf16[2,128,384]{2,1,0:T(8,128)(2,1)} %refs_0_.1), channel_id=1, source_target_pairs={{0,32},{1,97},{2,34},{3,99},{4,36},{5,101},{6,38},{7,103},{8,40},{... | collective-permute-start | bytes 589832 | tf_op jit(solution)/shard_map/ppermute | solution.py:36
  16.0 10.0 %collective-permute-start.3 = (bf16[128,384]{1,0:T(8,128)(2,1)}, bf16[128,384]{1,0:T(8,128)(2,1)S(1)}, u32[]{:S(2)}, u32[]{:S(2)}) collective-permute-start(bf16[128,384]{1,0:T(8,128)(2,1)} %get-tuple-element.17.refs_0_.q), channel_id=1, source_target_pairs={{0,96},{1,33},{2,98},{3,35},{4,100},{5,37},{6,102},{7,39},{8,104},... | collective-permute-start | bytes 294920 | tf_op jit(solution)/shard_map/ppermute | solution.py:36
  27.9 26.3 %all-to-all-start = ((bf16[4,2,128,384]{3,2,1,0:T(8,128)(2,1)}), bf16[4,2,128,384]{3,2,1,0:T(8,128)(2,1)S(1)}, u32[]{:S(2)}, u32[]{:S(2)}) async-start(bf16[4,2,128,384]{3,2,1,0:T(8,128)(2,1)} %spread.1), calls=%async_computation | async-start | bytes 1572864 | tf_op jit(solution)/shard_map/all_to_all | solution.py:55
  34.1 13.4 %collective-permute-start.2 = (bf16[2,128,384]{2,1,0:T(8,128)(2,1)S(1)}, bf16[2,128,384]{2,1,0:T(8,128)(2,1)S(1)}, u32[]{:S(2)}, u32[]{:S(2)}) collective-permute-start(bf16[2,128,384]{2,1,0:T(8,128)(2,1)S(1)} %copy-done.10), channel_id=1, source_target_pairs={{0,408},{1,137},{2,410},{3,139},{4,412},{5,141},{6,414},{7,143},{8... | collective-permute-start | bytes 589832 | tf_op jit(solution)/shard_map/ppermute | solution.py:36
  36.0 14.9 %collective-permute-start.1 = (bf16[2,128,384]{2,1,0:T(8,128)(2,1)S(1)}, bf16[2,128,384]{2,1,0:T(8,128)(2,1)S(1)}, u32[]{:S(2)}, u32[]{:S(2)}) collective-permute-start(bf16[2,128,384]{2,1,0:T(8,128)(2,1)S(1)} %copy-done.10), channel_id=1, source_target_pairs={{0,384},{1,129},{2,386},{3,131},{4,388},{5,133},{6,390},{7,135},{8... | collective-permute-start | bytes 589832 | tf_op jit(solution)/shard_map/ppermute | solution.py:36
  39.0 11.9 %collective-permute-start = (bf16[2,128,384]{2,1,0:T(8,128)(2,1)S(1)}, bf16[2,128,384]{2,1,0:T(8,128)(2,1)S(1)}, u32[]{:S(2)}, u32[]{:S(2)}) collective-permute-start(bf16[2,128,384]{2,1,0:T(8,128)(2,1)S(1)} %copy-done.10), channel_id=1, source_target_pairs={{0,24},{1,9},{2,26},{3,11},{4,28},{5,13},{6,30},{7,15},{8,16},{9,1... | collective-permute-start | bytes 589832 | tf_op jit(solution)/shard_map/ppermute | solution.py:36
  42.4 8.4 %collective-permute-start.7 = (bf16[2,128,384]{2,1,0:T(8,128)(2,1)S(1)}, bf16[2,128,384]{2,1,0:T(8,128)(2,1)S(1)}, u32[]{:S(2)}, u32[]{:S(2)}) collective-permute-start(bf16[2,128,384]{2,1,0:T(8,128)(2,1)S(1)} %collective-permute-done.4.refs_4_), channel_id=1, source_target_pairs={{0,408},{1,137},{2,410},{3,139},{4,412},{5,141},{6,414},{7,143},{8... | collective-permute-start | bytes 589832 | tf_op jit(solution)/shard_map/ppermute | solution.py:36
  44.4 7.5 %collective-permute-start.6 = (bf16[2,128,384]{2,1,0:T(8,128)(2,1)S(1)}, bf16[2,128,384]{2,1,0:T(8,128)(2,1)S(1)}, u32[]{:S(2)}, u32[]{:S(2)}) collective-permute-start(bf16[2,128,384]{2,1,0:T(8,128)(2,1)S(1)} %collective-permute-done.4.refs_4_), channel_id=1, source_target_pairs={{0,384},{1,129},{2,386},{3,131},{4,388},{5,133},{6,390},{7,135},{8... | collective-permute-start | bytes 589832 | tf_op jit(solution)/shard_map/ppermute | solution.py:36
  47.5 6.7 %collective-permute-start.5 = (bf16[2,128,384]{2,1,0:T(8,128)(2,1)S(1)}, bf16[2,128,384]{2,1,0:T(8,128)(2,1)S(1)}, u32[]{:S(2)}, u32[]{:S(2)}) collective-permute-start(bf16[2,128,384]{2,1,0:T(8,128)(2,1)S(1)} %collective-permute-done.4.refs_4_), channel_id=1, source_target_pairs={{0,24},{1,9},{2,26},{3,11},{4,28},{5,13},{6,30},{7,15},{8,16},{9,1... | collective-permute-start | bytes 589832 | tf_op jit(solution)/shard_map/ppermute | solution.py:36
  50.9 6.7 %copy-start.11 = (bf16[2,128,384]{2,1,0:T(8,128)(2,1)}, bf16[2,128,384]{2,1,0:T(8,128)(2,1)S(1)}, u32[]{:S(2)}) copy-start(bf16[2,128,384]{2,1,0:T(8,128)(2,1)S(1)} %collective-permute-done.7.refs_7_) | copy-start | bytes 589828
  51.9 5.7 %copy-start.13 = (bf16[2,128,384]{2,1,0:T(8,128)(2,1)}, bf16[2,128,384]{2,1,0:T(8,128)(2,1)S(1)}, u32[]{:S(2)}) copy-start(bf16[2,128,384]{2,1,0:T(8,128)(2,1)S(1)} %collective-permute-done.6.refs_6_) | copy-start | bytes 589828
  57.6 13.2 %all-to-all-start.1 = ((bf16[4,144,384]{2,1,0:T(8,128)(2,1)}), bf16[4,144,384]{2,1,0:T(8,128)(2,1)S(1)}, u32[]{:S(2)}, u32[]{:S(2)}) async-start(bf16[4,144,384]{2,1,0:T(8,128)(2,1)} %attend_pair.1), calls=%async_computation.1 | async-start | bytes 884736 | tf_op jit(solution)/shard_map/all_to_all | solution.py:55
  66.4 16.6 %copy-start = (bf16[3,128,384]{2,1,0:T(8,128)(2,1)S(1)}, bf16[3,128,384]{2,1,0:T(8,128)(2,1)}, u32[]{:S(2)}) copy-start(bf16[3,128,384]{2,1,0:T(8,128)(2,1)} %raw.1) | copy-start | bytes 884740
  66.4 16.6 %copy-start.2 = (bf16[2,512,384]{2,1,0:T(8,128)(2,1)S(1)}, bf16[2,512,384]{2,1,0:T(8,128)(2,1)}, u32[]{:S(2)}) copy-start(bf16[2,512,384]{2,1,0:T(8,128)(2,1)} %text.1) | copy-start | bytes 2359300
  66.4 16.6 %copy-start.5 = (bf16[128,384]{1,0:T(8,128)(2,1)S(1)}, bf16[128,384]{1,0:T(8,128)(2,1)}, u32[]{:S(2)}) copy-start(bf16[128,384]{1,0:T(8,128)(2,1)} %get-tuple-element.17.refs_0_.q) | copy-start | bytes 294916
  66.4 16.6 %copy-start.8 = (bf16[128,384]{1,0:T(8,128)(2,1)S(1)}, bf16[128,384]{1,0:T(8,128)(2,1)}, u32[]{:S(2)}) copy-start(bf16[128,384]{1,0:T(8,128)(2,1)} %get-tuple-element.22.k_fresh) | copy-start | bytes 294916
  71.2 14.4 %all-to-all-start.2 = ((bf16[4,144,384]{2,1,0:T(8,128)(2,1)}), bf16[4,144,384]{2,1,0:T(8,128)(2,1)S(1)}, u32[]{:S(2)}, u32[]{:S(2)}) async-start(bf16[4,144,384]{2,1,0:T(8,128)(2,1)} %attend_own.1), calls=%async_computation.2 | async-start | bytes 884736 | tf_op jit(solution)/shard_map/all_to_all | solution.py:55
  76.2 9.4 %collective-permute-start.8 = (bf16[144,384]{1,0:T(8,128)(2,1)S(1)}, bf16[144,384]{1,0:T(8,128)(2,1)S(1)}, u32[]{:S(2)}, u32[]{:S(2)}) collective-permute-start(bf16[144,384]{1,0:T(8,128)(2,1)S(1)} %merge.1), channel_id=1, source_target_pairs={{0,96},{1,33},{2,98},{3,35},{4,100},{5,37},{6,102},{7,39},{8,104},... | collective-permute-start | bytes 331784 | tf_op jit(solution)/shard_map/ppermute | solution.py:36
  84.5 37.8 %copy-start.6 = (bf16[128,384]{1,0:T(8,128)(2,1)S(1)}, bf16[128,384]{1,0:T(8,128)(2,1)}, u32[]{:S(2)}) copy-start(bf16[128,384]{1,0:T(8,128)(2,1)} %hidden.1) | copy-start | bytes 294916
  84.5 37.8 %copy-start.7 = (bf16[128,384]{1,0:T(8,128)(2,1)S(1)}, bf16[128,384]{1,0:T(8,128)(2,1)}, u32[]{:S(2)}) copy-start(bf16[128,384]{1,0:T(8,128)(2,1)} %control.1) | copy-start | bytes 294916
  84.5 37.8 %copy-start.9 = (f32[28,384]{1,0:T(8,128)S(1)}, f32[28,384]{1,0:T(8,128)}, u32[]{:S(2)}) copy-start(f32[28,384]{1,0:T(8,128)} %gate.1) | copy-start | bytes 129028
  91.9 10.1 %collective-permute-start.9 = (bf16[4,128,384]{2,1,0:T(8,128)(2,1)}, bf16[4,128,384]{2,1,0:T(8,128)(2,1)S(1)}, u32[]{:S(2)}, u32[]{:S(2)}) collective-permute-start(bf16[4,128,384]{2,1,0:T(8,128)(2,1)} %get-tuple-element.24), channel_id=1, source_target_pairs={{0,1},{1,0},{2,3},{3,2},{4,5},{5,4},{6,7},{7,6},{8,9},{9,8},{10,11... | collective-permute-start | bytes 1179656 | tf_op jit(solution)/shard_map/ppermute | solution.py:36
  104.0 18.3 %all-to-all-start.3 = ((bf16[4,128,384]{2,1,0:T(8,128)(2,1)}), bf16[4,128,384]{2,1,0:T(8,128)(2,1)S(1)}, u32[]{:S(2)}, u32[]{:S(2)}) async-start(bf16[4,128,384]{2,1,0:T(8,128)(2,1)} %pair_sum.1), calls=%async_computation.3 | async-start | bytes 786432 | tf_op jit(solution)/shard_map/all_to_all | solution.py:55
  (9 other events, 10.2 us)

commit v3 on v2

--- a/solution.py
+++ b/solution.py
@@ -48,7 +48,6 @@
 QUERY_FLIPS = (1, 3)
 QUERY_GROUPS = squares(QUERY_FLIPS)
 KEY_FLIPS = (3, 1)
-Z_RUNS = [[0, 2, 4, 6], [1, 3, 5, 7]]
 
 
 def exchange(value, axes, groups):
@@ -101,6 +100,10 @@
 
 def swap_core(value):
     return permute(value, lambda y, zh, x, zl, c: (y, zh, x, zl, 1 - c))
+
+
+def swap_z(value, d):
+    return permute(value, lambda y, zh, x, zl, c: (y, zh, x, zl ^ d, c))
 
 
 def frequencies():
@@ -180,6 +183,23 @@
     )
 
 
+def stack_kernel(a, b, out):
+    out[0] = a[...]
+    out[1] = b[...]
+
+
+def stack(a, b):
+    full = pl.BlockSpec(memory_space=pltpu.VMEM)
+    return pl.pallas_call(
+        stack_kernel,
+        out_shape=jax.ShapeDtypeStruct((2,) + a.shape, BF16),
+        in_specs=[full] * 2,
+        out_specs=full,
+        compiler_params=pltpu.CompilerParams(vmem_limit_bytes=16 * MIB),
+        name="stack",
+    )(a, b)
+
+
 def split3(v):
     hi = v.astype(BF16).astype(F32)
     rest = v - hi
@@ -191,17 +211,11 @@
     return lax.dot_general(q, k, (((1,), (1,)), ((), ())), preferred_element_type=F32)
 
 
-def attend(s, values):
-    top = jnp.max(s[0], axis=1, keepdims=True)
-    for t in s[1:]:
-        top = jnp.maximum(top, jnp.max(t, axis=1, keepdims=True))
-    top = top * SCALE2
-    acc = None
-    for t, v in zip(s, values):
-        p = jnp.exp2(t * SCALE2 - top).astype(BF16)
-        v = jnp.concatenate([v, jnp.ones(v.shape, BF16)], axis=1)
-        part = jnp.dot(p, v, preferred_element_type=F32)
-        acc = part if acc is None else acc + part
+def attend(q, k, v):
+    s = scores(q, k)
+    top = jnp.max(s, axis=1, keepdims=True) * SCALE2
+    p = jnp.exp2(s * SCALE2 - top).astype(BF16)
+    acc = jnp.dot(p, v, preferred_element_type=F32)
     total = acc[:, HD:]
     return acc[:, :HD] / total, top + jnp.log2(total)
 
@@ -223,7 +237,8 @@
         cut = slice(h * HD, (h + 1) * HD)
         keys = jnp.concatenate([k_fresh[:, cut], text[0, :, cut]], axis=0)
         values = jnp.concatenate([raw[2, :, cut], text[1, :, cut]], axis=0)
-        a, b = attend([scores(q[:, cut], keys)], [values])
+        values = jnp.concatenate([values, jnp.ones(values.shape, BF16)], axis=1)
+        a, b = attend(q[:, cut], keys, values)
         o.append(a)
         lse.append(b)
     put(out, o, lse)
@@ -244,43 +259,52 @@
     )(*args)
 
 
-def attn_kernel(half, *refs):
-    kv, q, out = refs[:8], refs[8], refs[9]
+def attn_kernel(a, b, c, d, q, out, kc, vc):
     at = query_place()
-    o = [[None] * HEADS_DEV for _ in range(4)]
-    lse = [[None] * HEADS_DEV for _ in range(4)]
+    kv = (a, b, c, d)
     for h in range(HEADS_DEV):
         cut = slice(h * HD, (h + 1) * HD)
-        keys = jnp.concatenate([r[0, :, cut] for r in kv], axis=0)
-        values = jnp.concatenate([r[1, :, cut] for r in kv], axis=0)
-        for pair in (0, 2):
-            rows = jnp.concatenate([q[at ^ pair, half, :, cut], q[at ^ (pair + 1), half, :, cut]], axis=0)
-            s = scores(rows, keys)
-            if half == 0 and pair == 0:
-                hidden = jnp.full((TOK, TOK), -jnp.inf, F32)
-                s = jnp.concatenate(
-                    [jnp.concatenate([hidden, s[:TOK, TOK:]], axis=1), s[TOK:]], axis=0
-                )
-            a, b = attend([s], [values])
-            for i in range(2):
-                o[pair + i][h] = a[i * TOK : (i + 1) * TOK]
-                lse[pair + i][h] = b[i * TOK : (i + 1) * TOK]
-    for d in range(4):
-        put(out.at[at ^ d], o[d], lse[d])
-
-
-def attention(half, kv, q):
-    full = pl.BlockSpec(memory_space=pltpu.VMEM)
-    return pl.pallas_call(
-        functools.partial(attn_kernel, half),
-        out_shape=jax.ShapeDtypeStruct((4, TOK + STAT, WIDTH), BF16),
-        in_specs=[full] * 9,
-        out_specs=full,
-        compiler_params=pltpu.CompilerParams(vmem_limit_bytes=32 * MIB),
+        for i in range(8):
+            rows = slice(i * TOK, (i + 1) * TOK)
+            kc[h, rows, :] = kv[i // 2][i % 2, 0, :, cut]
+            vc[h, rows, 0:HD] = kv[i // 2][i % 2, 1, :, cut]
+        vc[h, :, HD:] = jnp.ones((8 * TOK, HD), BF16)
+
+    def one(place, half, skip):
+        o, lse = [], []
+        for h in range(HEADS_DEV):
+            x, y = attend(q[place, half, :, h * HD : (h + 1) * HD], kc[h, skip:], vc[h, skip:])
+            o.append(x)
+            lse.append(y)
+        put(out.at[place, half], o, lse)
+
+    one(at, 0, TOK)
+    one(at, 1, 0)
+
+    def step(i, carry):
+        one(at ^ i, 0, 0)
+        one(at ^ i, 1, 0)
+        return carry
+
+    lax.fori_loop(1, 4, step, 0)
+
+
+def attention(kv, q):
+    full = pl.BlockSpec(memory_space=pltpu.VMEM)
+    return pl.pallas_call(
+        attn_kernel,
+        out_shape=jax.ShapeDtypeStruct((4, 2, TOK + STAT, WIDTH), BF16),
+        in_specs=[full] * 5,
+        out_specs=full,
+        scratch_shapes=[
+            pltpu.VMEM((HEADS_DEV, 8 * TOK, HD), BF16),
+            pltpu.VMEM((HEADS_DEV, 8 * TOK, 2 * HD), BF16),
+        ],
+        compiler_params=pltpu.CompilerParams(vmem_limit_bytes=24 * MIB),
         cost_estimate=pl.CostEstimate(
-            flops=4 * 4 * TOK * 8 * TOK * WIDTH, bytes_accessed=4 * MIB, transcendentals=2**21
+            flops=4 * 8 * TOK * 8 * TOK * WIDTH, bytes_accessed=4 * MIB, transcendentals=2**22
         ),
-        name="attend_own" if half == 0 else "attend_pair",
+        name="attend",
     )(*kv, q)
 
 
@@ -315,15 +339,15 @@
     return outs, lses
 
 
-def partials(ref):
+def partials(ref, half):
     return (
-        [lambda h, i=i: ref[i, 0:TOK, h * HD : (h + 1) * HD].astype(F32) for i in range(4)],
-        [ref[i, TOK:, 0:HD].astype(F32) for i in range(4)],
+        [lambda h, i=i: ref[i, half, 0:TOK, h * HD : (h + 1) * HD].astype(F32) for i in range(4)],
+        [ref[i, half, TOK:, 0:HD].astype(F32) for i in range(4)],
     )
 
 
 def merge_kernel(got, out):
-    outs, lses = merge(*partials(got))
+    outs, lses = merge(*partials(got, 1))
     sub = lax.broadcasted_iota(jnp.int32, (STAT, HD), 0)
     table = jnp.zeros((STAT, HD), F32)
     for h in range(HEADS_DEV):
@@ -346,30 +370,20 @@
     )(messages)
 
 
-def project_kernel(mine, theirs, home, w_hbm, keep, give, att, w, sem):
-    core = lax.axis_index("tensor") % 2
-    order = [(c, z) for c in range(2) for z in range(4)]
-
-    def columns(c, z):
-        return pl.ds(pl.multiple_of((2 * z + (core + 1 - c) % 2) * WIDTH, HD), WIDTH)
-
-    copies = [
-        pltpu.make_async_copy(w_hbm.at[:, columns(c, z)], w.at[c, z], sem.at[4 * c + z])
-        for c, z in order
-    ]
-    for c in copies:
-        c.start()
-    parts, stats = partials(mine)
+def project_kernel(mine, theirs, home, w, keep, give, att):
+    parts, stats = partials(mine, 0)
     for ref in (theirs, home):
         parts.append(lambda h, ref=ref: ref[0:TOK, h * HD : (h + 1) * HD].astype(F32))
         stats.append(ref[TOK:, 0:HD].astype(F32))
     outs, _ = merge(parts, stats)
     for h in range(HEADS_DEV):
         att[:, h * HD : (h + 1) * HD] = outs[h].astype(BF16)
-    for copy, (c, z) in zip(copies, order):
-        copy.wait()
-        out = keep if c else give
-        out[z] = jnp.dot(att[...], w[c, z], preferred_element_type=F32).astype(out.dtype)
+    t = lax.axis_index("tensor")
+    zl, core = t // 2, t % 2
+    for d in range(4):
+        for out, c in ((give, 1 - core), (keep, core)):
+            part = w[:, pl.ds(pl.multiple_of((2 * (zl ^ d) + c) * WIDTH, HD), WIDTH)]
+            out[d] = jnp.dot(att[...], part, preferred_element_type=F32).astype(out.dtype)
 
 
 def project(mine, theirs, home, out_weight):
@@ -380,52 +394,50 @@
             jax.ShapeDtypeStruct((4, TOK, WIDTH), F32),
             jax.ShapeDtypeStruct((4, TOK, WIDTH), BF16),
         ),
-        in_specs=[full] * 3 + [pl.BlockSpec(memory_space=pltpu.HBM)],
+        in_specs=[full] * 4,
         out_specs=(full, full),
-        scratch_shapes=[
-            pltpu.VMEM((TOK, WIDTH), BF16),
-            pltpu.VMEM((2, 4, WIDTH, WIDTH), BF16),
-            pltpu.SemaphoreType.DMA((8,)),
-        ],
-        compiler_params=pltpu.CompilerParams(vmem_limit_bytes=56 * MIB),
+        scratch_shapes=[pltpu.VMEM((TOK, WIDTH), BF16)],
+        compiler_params=pltpu.CompilerParams(vmem_limit_bytes=16 * MIB),
         name="project",
     )(mine, theirs, home, out_weight)
 
 
-def pair_kernel(keep, got, out):
-    out[...] = (keep[...] + got[...].astype(F32)).astype(BF16)
-
-
-def pair_sum(keep, got):
-    full = pl.BlockSpec(memory_space=pltpu.VMEM)
-    return pl.pallas_call(
-        pair_kernel,
-        out_shape=jax.ShapeDtypeStruct((4, TOK, WIDTH), BF16),
+def halve_kernel(keep, got, stay, send):
+    n = stay.shape[0]
+    for i in range(n):
+        stay[i] = keep[2 * i] + got[2 * i].astype(F32)
+        send[i] = (keep[2 * i + 1] + got[2 * i + 1].astype(F32)).astype(BF16)
+
+
+def halve(keep, got):
+    full = pl.BlockSpec(memory_space=pltpu.VMEM)
+    shape = (keep.shape[0] // 2, TOK, WIDTH)
+    return pl.pallas_call(
+        halve_kernel,
+        out_shape=(jax.ShapeDtypeStruct(shape, F32), jax.ShapeDtypeStruct(shape, BF16)),
         in_specs=[full] * 2,
-        out_specs=full,
-        compiler_params=pltpu.CompilerParams(vmem_limit_bytes=16 * MIB),
-        name="pair_sum",
+        out_specs=(full, full),
+        compiler_params=pltpu.CompilerParams(vmem_limit_bytes=16 * MIB),
+        name="halve",
     )(keep, got)
 
 
-def final_kernel(step, got, gate, hidden, control, out):
-    total = got[0].astype(F32)
-    for t in range(1, 4):
-        total = total + got[t].astype(F32)
+def final_kernel(step, own, got, gate, hidden, control, out):
+    total = own[0] + got[0].astype(F32)
     row = gate[pl.ds(step[0], 1), :]
     out[...] = (hidden[...].astype(F32) + row * total + control[...].astype(F32)).astype(BF16)
 
 
-def finish(timestep, got, gate_table, hidden_in, control):
+def finish(timestep, own, got, gate_table, hidden_in, control):
     full = pl.BlockSpec(memory_space=pltpu.VMEM)
     return pl.pallas_call(
         final_kernel,
         out_shape=jax.ShapeDtypeStruct((TOK, WIDTH), BF16),
-        in_specs=[pl.BlockSpec(memory_space=pltpu.SMEM)] + [full] * 4,
+        in_specs=[pl.BlockSpec(memory_space=pltpu.SMEM)] + [full] * 5,
         out_specs=full,
         compiler_params=pltpu.CompilerParams(vmem_limit_bytes=16 * MIB),
         name="finish",
-    )(timestep, got, gate_table, hidden_in, control)
+    )(timestep, own, got, gate_table, hidden_in, control)
 
 
 def body(
@@ -441,23 +453,20 @@
     hidden_in,
     control,
 ):
-    pair_kv = key_pair(stale_kv)
     q, k_fresh = prepare(fresh_qkv, positions, query_gain, key_gain)
     pair_q = query_pair(q)
     stale_kv, q = lax.optimization_barrier((stale_kv, q))
-    kv = key_square(stale_kv)
+    pair_kv = key_pair(stale_kv)
     queries, pair_kv = lax.optimization_barrier((spread(q, pair_q), pair_kv))
     q_all = exchange(queries, AXES, QUERY_GROUPS)
-    kv += key_square(pair_kv)
+    kv = key_square(stack(stale_kv, pair_kv))
     home = attend_home(q, k_fresh, fresh_qkv, text_kv)
-    paired = exchange(attention(1, kv, q_all), AXES, QUERY_GROUPS)
-    partial = attention(0, kv, q_all)
-    send, partial = lax.optimization_barrier((merge_first(paired), partial))
-    theirs = query_pair(send)
-    mine = exchange(partial, AXES, QUERY_GROUPS)
+    mine = exchange(attention(kv, q_all), AXES, QUERY_GROUPS)
+    theirs = query_pair(merge_first(mine))
     keep, give = project(mine, theirs, home, out_weight)
-    parts = exchange(pair_sum(keep, swap_core(give)), "tensor", Z_RUNS)
-    return finish(timestep, parts, gate_table, hidden_in, control)
+    keep, give = halve(keep, swap_core(give))
+    keep, give = halve(keep, swap_z(give, 1))
+    return finish(timestep, keep, swap_z(give, 2), gate_table, hidden_in, control)
 
 
 def solution(mesh):

time: 124 us -> 110 us (0.89)
  starting transfers between devices: 75 us -> 47.3 us
  blocking collectives: 0 us -> 15.9 us
  waiting for transfers between devices: 22.4 us -> 32 us
  local copies, waits for them, and re-layouts: 6.9 us -> 0.93 us
  Pallas kernels: 17.8 us -> 12.9 us
    ppermute x10 -> x9, waiting for transfers between devices: 10.8 us -> 31.9 us  [permute(): return lax.ppermute(value, AXES, pairs)]
    all_to_all x4 -> x1, starting transfers between devices: 24.4 us -> 6.2 us  [exchange(): lax.all_to_all(value, axes, 0, 0, axis_index_groups=groups, tiled=True)]
    all_to_all x0 -> x1, blocking collectives: none -> 15.9 us  [exchange(): lax.all_to_all(value, axes, 0, 0, axis_index_groups=groups, tiled=True)]
    all_to_all x4 -> x1, waiting for transfers between devices: 11.6 us -> 0.01 us  [exchange(): lax.all_to_all(value, axes, 0, 0, axis_index_groups=groups, tiled=True)]
    ppermute x10 -> x9, starting transfers between devices: 50.6 us -> 41.1 us  [permute(): return lax.ppermute(value, AXES, pairs)]
    unnamed x38 -> x20, local copies, waits for them, and re-layouts: 6.9 us -> 0.93 us
    pallas_call x1, Pallas kernels: 4.82 us -> 1.32 us  [project(): pl.pallas_call(project_kernel, out_shape=(jax.ShapeDtypeStruct((4, TOK, W...]
    pallas_call x3 -> x4, Pallas kernels: 7.51 us -> 6.09 us  [the longest x1 5.96 us: attention(): pl.pallas_call(attn_kernel, out_shape=jax.ShapeDtypeStruct((4, 2, TOK + S...]
  transfers between devices with their start and end apart: 14 -> 10, of which waited for: 7 -> 7; matrix products, arithmetic and copies ran while one was open for 0% -> 0% of each run, Pallas kernels for 6% -> 2%
where the time goes in v3:
time: 110 us
  starting transfers between devices  47.3 us (43%)
  waiting for transfers between devices  32 us (29%)
  blocking collectives  15.9 us (14%)
  Pallas kernels  12.9 us (12%)
    ppermute x9, starting transfers between devices, permute(): return lax.ppermute(value, AXES, pairs)  41.1 us
    ppermute x9, waiting for transfers between devices, permute(): return lax.ppermute(value, AXES, pairs)  31.9 us
    all_to_all x1, blocking collectives, exchange(): lax.all_to_all(value, axes, 0, 0, axis_index_groups=groups, tiled=True)  15.9 us
    all_to_all x1, starting transfers between devices, exchange(): lax.all_to_all(value, axes, 0, 0, axis_index_groups=groups, tiled=True)  6.2 us
    pallas_call x1, Pallas kernels, attention(): pl.pallas_call(attn_kernel, out_shape=jax.ShapeDtypeStruct((4, 2, TOK + S...  5.96 us
    pallas_call x1, Pallas kernels, prepare(): pl.pallas_call(prep_kernel, out_shape=(jax.ShapeDtypeStruct((TOK, WIDTH),...  2.57 us
  transfers between devices with their start and end apart: 10, of which 7 were waited for; matrix products, arithmetic and copies ran while one was open for 0% of the time, Pallas kernels for 2%

profile of v3, /device:TPU:1, one launch (start us, length us, event | category | flops | bytes accessed | tf_op | source)
XLA Modules:
  0.0 109.7 jit_solution(1127367043568232172)
XLA Ops:
  0.0 2.6 %prep.1 = (bf16[128,384]{1,0:T(8,128)(2,1)}, bf16[128,384]{1,0:T(8,128)(2,1)}) custom-call(bf16[3,128,384]{2,1,0:T(8,128)(2,1)} %raw.1, s32[1,128]{1,0:T(1,128)} %bitcast.3, f32[8,128]{1,0:T(8,128)} %constant.2.clone.freq_hbm, f32[1,128]{1,0:T(1,128)} %bitcast.4, f32[1,128]{1,0:T(1,128)} %bitcast.5), custom_call_target="tpu_custom_call" | custom-call | tf_op jit(solution)/shard_map/prep/pallas_call | solution.py:163
  2.6 13.3 %collective-permute-start.1 = (bf16[2,128,384]{2,1,0:T(8,128)(2,1)}, bf16[2,128,384]{2,1,0:T(8,128)(2,1)S(1)}, u32[]{:S(2)}, u32[]{:S(2)}) collective-permute-start(bf16[2,128,384]{2,1,0:T(8,128)(2,1)} %a), channel_id=1, source_target_pairs={{0,32},{1,97},{2,34},{3,99},{4,36},{5,101},{6,38},{7,103},{8,40},{... | collective-permute-start | bytes 589832 | tf_op jit(solution)/shard_map/ppermute | solution.py:36
  15.9 5.2 %collective-permute-start = (bf16[128,384]{1,0:T(8,128)(2,1)}, bf16[128,384]{1,0:T(8,128)(2,1)S(1)}, u32[]{:S(2)}, u32[]{:S(2)}) collective-permute-start(bf16[128,384]{1,0:T(8,128)(2,1)} %get-tuple-element.19.refs_0_.q), channel_id=1, source_target_pairs={{0,96},{1,33},{2,98},{3,35},{4,100},{5,37},{6,102},{7,39},{8,104},... | collective-permute-start | bytes 294920 | tf_op jit(solution)/shard_map/ppermute | solution.py:36
  21.1 6.3 %collective-permute-done.refs_1_ = bf16[128,384]{1,0:T(8,128)(2,1)S(1)} collective-permute-done((bf16[128,384]{1,0:T(8,128)(2,1)}, bf16[128,384]{1,0:T(8,128)(2,1)S(1)}, u32[]{:S(2)}, u32[]{:S(2)}) %collective-permute-start) | collective-permute-done | bytes 98336 | tf_op jit(solution)/shard_map/ppermute | solution.py:36
  27.4 0.9 copy-done.3
  28.3 0.9 spread.1
  29.2 6.2 %all-to-all-start = ((bf16[4,2,128,384]{3,2,1,0:T(8,128)(2,1)}), bf16[4,2,128,384]{3,2,1,0:T(8,128)(2,1)S(1)}, u32[]{:S(2)}, u32[]{:S(2)}) async-start(bf16[4,2,128,384]{3,2,1,0:T(8,128)(2,1)} %spread.1), calls=%async_computation | async-start | bytes 1572864 | tf_op jit(solution)/shard_map/all_to_all | solution.py:54
  35.5 1.9 %collective-permute-start.4 = (bf16[2,2,128,384]{3,2,1,0:T(8,128)(2,1)S(1)}, bf16[2,2,128,384]{3,2,1,0:T(8,128)(2,1)S(1)}, u32[]{:S(2)}, u32[]{:S(2)}) collective-permute-start(bf16[2,2,128,384]{3,2,1,0:T(8,128)(2,1)S(1)} %stack.1.a), channel_id=1, source_target_pairs={{0,408},{1,137},{2,410},{3,139},{4,412},{5,141},{6,414},{7,143},{8... | collective-permute-start | bytes 1179656 | tf_op jit(solution)/shard_map/ppermute | solution.py:36
  37.4 3.0 %collective-permute-start.3 = (bf16[2,2,128,384]{3,2,1,0:T(8,128)(2,1)S(1)}, bf16[2,2,128,384]{3,2,1,0:T(8,128)(2,1)S(1)}, u32[]{:S(2)}, u32[]{:S(2)}) collective-permute-start(bf16[2,2,128,384]{3,2,1,0:T(8,128)(2,1)S(1)} %stack.1.a), channel_id=1, source_target_pairs={{0,384},{1,129},{2,386},{3,131},{4,388},{5,133},{6,390},{7,135},{8... | collective-permute-start | bytes 1179656 | tf_op jit(solution)/shard_map/ppermute | solution.py:36
  40.4 3.4 %collective-permute-start.2 = (bf16[2,2,128,384]{3,2,1,0:T(8,128)(2,1)S(1)}, bf16[2,2,128,384]{3,2,1,0:T(8,128)(2,1)S(1)}, u32[]{:S(2)}, u32[]{:S(2)}) collective-permute-start(bf16[2,2,128,384]{3,2,1,0:T(8,128)(2,1)S(1)} %stack.1.a), channel_id=1, source_target_pairs={{0,24},{1,9},{2,26},{3,11},{4,28},{5,13},{6,30},{7,15},{8,16},{9,1... | collective-permute-start | bytes 1179656 | tf_op jit(solution)/shard_map/ppermute | solution.py:36
  43.9 4.2 %collective-permute-done.4.d = bf16[2,2,128,384]{3,2,1,0:T(8,128)(2,1)S(1)} collective-permute-done((bf16[2,2,128,384]{3,2,1,0:T(8,128)(2,1)S(1)}, bf16[2,2,128,384]{3,2,1,0:T(8,128)(2,1)S(1)}, u32[]{:S(2)}, u32[]{:S(2)}) %collective-permute-start.4) | collective-permute-done | bytes 393248 | tf_op jit(solution)/shard_map/ppermute | solution.py:36
  48.1 3.3 %collective-permute-done.3.c = bf16[2,2,128,384]{3,2,1,0:T(8,128)(2,1)S(1)} collective-permute-done((bf16[2,2,128,384]{3,2,1,0:T(8,128)(2,1)S(1)}, bf16[2,2,128,384]{3,2,1,0:T(8,128)(2,1)S(1)}, u32[]{:S(2)}, u32[]{:S(2)}) %collective-permute-start.3) | collective-permute-done | bytes 393248 | tf_op jit(solution)/shard_map/ppermute | solution.py:36
  51.4 6.0 %attend.1 = bf16[4,2,144,384]{3,2,1,0:T(8,128)(2,1)S(1)} custom-call(bf16[2,2,128,384]{3,2,1,0:T(8,128)(2,1)S(1)} %stack.1.a, bf16[2,2,128,384]{3,2,1,0:T(8,128)(2,1)S(1)} %collective-permute-done.2.b, bf16[2,2,128,384]{3,2,1,0:T(8,128)(2,1)S(1)} %collective-permute-done.3.c, bf16[2,2,128,384]{3,2,1,0:T(8,128)(2,1)S(1)} %collective-permute-done.4.d, ...), custom_call_target="tpu_custom_call" | custom-call | flops 1610612736 | bytes 4194304 | tf_op jit(solution)/shard_map/attend/pallas_call | solution.py:294
  57.4 15.9 %all_to_all.10.got.mine = bf16[4,2,144,384]{3,2,1,0:T(8,128)(2,1)S(1)} all-to-all(bf16[4,2,144,384]{3,2,1,0:T(8,128)(2,1)S(1)} %attend.1), channel_id=1, replica_groups={{0,8,128,136},{1,25,385,409},{2,10,130,138},{3,27,387,411},{4,12,132,14..., dimensions={0} | all-to-all | bytes 1769472 | tf_op jit(solution)/shard_map/all_to_all | solution.py:54
  73.7 5.4 %collective-permute-start.5 = (bf16[144,384]{1,0:T(8,128)(2,1)S(1)}, bf16[144,384]{1,0:T(8,128)(2,1)S(1)}, u32[]{:S(2)}, u32[]{:S(2)}) collective-permute-start(bf16[144,384]{1,0:T(8,128)(2,1)S(1)} %merge.1), channel_id=1, source_target_pairs={{0,96},{1,33},{2,98},{3,35},{4,100},{5,37},{6,102},{7,39},{8,104},... | collective-permute-start | bytes 331784 | tf_op jit(solution)/shard_map/ppermute | solution.py:36
  79.2 0.8 attend_home.1.home
  80.0 5.5 %collective-permute-done.5.theirs = bf16[144,384]{1,0:T(8,128)(2,1)S(1)} collective-permute-done((bf16[144,384]{1,0:T(8,128)(2,1)S(1)}, bf16[144,384]{1,0:T(8,128)(2,1)S(1)}, u32[]{:S(2)}, u32[]{:S(2)}) %collective-permute-start.5) | collective-permute-done | bytes 110624 | tf_op jit(solution)/shard_map/ppermute | solution.py:36
  85.6 1.3 %project.1 = (f32[4,128,384]{2,1,0:T(8,128)S(1)}, bf16[4,128,384]{2,1,0:T(8,128)(2,1)S(1)}) custom-call(bf16[4,2,144,384]{3,2,1,0:T(8,128)(2,1)S(1)} %all_to_all.10.got.mine, bf16[144,384]{1,0:T(8,128)(2,1)S(1)} %collective-permute-done.5.theirs, bf16[144,384]{1,0:T(8,128)(2,1)S(1)} %attend_home.1.home, bf16[384,3072]{1,0:T(8,128)(2,1)S(1)} %copy-done), custom_call_target="tpu_custom_call" | custom-call | tf_op jit(solution)/shard_map/project/pallas_call | solution.py:391
  86.9 3.6 %collective-permute-start.6 = (bf16[4,128,384]{2,1,0:T(8,128)(2,1)S(1)}, bf16[4,128,384]{2,1,0:T(8,128)(2,1)S(1)}, u32[]{:S(2)}, u32[]{:S(2)}) collective-permute-start(bf16[4,128,384]{2,1,0:T(8,128)(2,1)S(1)} %get-tuple-element.24), channel_id=1, source_target_pairs={{0,1},{1,0},{2,3},{3,2},{4,5},{5,4},{6,7},{7,6},{8,9},{9,8},{10,11... | collective-permute-start | bytes 1179656 | tf_op jit(solution)/shard_map/ppermute | solution.py:36
  90.5 1.3 %collective-permute-done.6.got = bf16[4,128,384]{2,1,0:T(8,128)(2,1)S(1)} collective-permute-done((bf16[4,128,384]{2,1,0:T(8,128)(2,1)S(1)}, bf16[4,128,384]{2,1,0:T(8,128)(2,1)S(1)}, u32[]{:S(2)}, u32[]{:S(2)}) %collective-permute-start.6) | collective-permute-done | bytes 393248 | tf_op jit(solution)/shard_map/ppermute | solution.py:36
  91.9 1.9 %collective-permute-start.7 = (bf16[2,128,384]{2,1,0:T(8,128)(2,1)S(1)}, bf16[2,128,384]{2,1,0:T(8,128)(2,1)S(1)}, u32[]{:S(2)}, u32[]{:S(2)}) collective-permute-start(bf16[2,128,384]{2,1,0:T(8,128)(2,1)S(1)} %get-tuple-element.26), channel_id=1, source_target_pairs={{0,2},{1,3},{2,0},{3,1},{4,6},{5,7},{6,4},{7,5},{8,10},{9,11},{10,... | collective-permute-start | bytes 589832 | tf_op jit(solution)/shard_map/ppermute | solution.py:36
  93.8 6.1 %collective-permute-done.7.got = bf16[2,128,384]{2,1,0:T(8,128)(2,1)S(1)} collective-permute-done((bf16[2,128,384]{2,1,0:T(8,128)(2,1)S(1)}, bf16[2,128,384]{2,1,0:T(8,128)(2,1)S(1)}, u32[]{:S(2)}, u32[]{:S(2)}) %collective-permute-start.7) | collective-permute-done | bytes 196640 | tf_op jit(solution)/shard_map/ppermute | solution.py:36
  99.9 3.3 %collective-permute-start.8 = (bf16[1,128,384]{2,1,0:T(8,128)(2,1)S(1)}, bf16[1,128,384]{2,1,0:T(8,128)(2,1)S(1)}, u32[]{:S(2)}, u32[]{:S(2)}) collective-permute-start(bf16[1,128,384]{2,1,0:T(8,128)(2,1)S(1)} %get-tuple-element.28), channel_id=1, source_target_pairs={{0,4},{1,5},{2,6},{3,7},{4,0},{5,1},{6,2},{7,3},{8,12},{9,13},{10,... | collective-permute-start | bytes 294920 | tf_op jit(solution)/shard_map/ppermute | solution.py:36
  103.9 5.1 %collective-permute-done.8.got = bf16[1,128,384]{2,1,0:T(8,128)(2,1)S(1)} collective-permute-done((bf16[1,128,384]{2,1,0:T(8,128)(2,1)S(1)}, bf16[1,128,384]{2,1,0:T(8,128)(2,1)S(1)}, u32[]{:S(2)}, u32[]{:S(2)}) %collective-permute-start.8) | collective-permute-done | bytes 98336 | tf_op jit(solution)/shard_map/ppermute | solution.py:36
  (27 shorter events, 1.4 us)
Async XLA Ops:
  0.0 35.4 %copy-start.5 = (bf16[2,128,384]{2,1,0:T(8,128)(2,1)S(1)}, bf16[2,128,384]{2,1,0:T(8,128)(2,1)}, u32[]{:S(2)}) copy-start(bf16[2,128,384]{2,1,0:T(8,128)(2,1)} %a) | copy-start | bytes 589828
  2.6 26.7 %collective-permute-start.1 = (bf16[2,128,384]{2,1,0:T(8,128)(2,1)}, bf16[2,128,384]{2,1,0:T(8,128)(2,1)S(1)}, u32[]{:S(2)}, u32[]{:S(2)}) collective-permute-start(bf16[2,128,384]{2,1,0:T(8,128)(2,1)} %a), channel_id=1, source_target_pairs={{0,32},{1,97},{2,34},{3,99},{4,36},{5,101},{6,38},{7,103},{8,40},{... | collective-permute-start | bytes 589832 | tf_op jit(solution)/shard_map/ppermute | solution.py:36
  15.9 11.5 %collective-permute-start = (bf16[128,384]{1,0:T(8,128)(2,1)}, bf16[128,384]{1,0:T(8,128)(2,1)S(1)}, u32[]{:S(2)}, u32[]{:S(2)}) collective-permute-start(bf16[128,384]{1,0:T(8,128)(2,1)} %get-tuple-element.19.refs_0_.q), channel_id=1, source_target_pairs={{0,96},{1,33},{2,98},{3,35},{4,100},{5,37},{6,102},{7,39},{8,104},... | collective-permute-start | bytes 294920 | tf_op jit(solution)/shard_map/ppermute | solution.py:36
  27.4 0.9 copy-start.3
  29.2 22.2 %all-to-all-start = ((bf16[4,2,128,384]{3,2,1,0:T(8,128)(2,1)}), bf16[4,2,128,384]{3,2,1,0:T(8,128)(2,1)S(1)}, u32[]{:S(2)}, u32[]{:S(2)}) async-start(bf16[4,2,128,384]{3,2,1,0:T(8,128)(2,1)} %spread.1), calls=%async_computation | async-start | bytes 1572864 | tf_op jit(solution)/shard_map/all_to_all | solution.py:54
  35.5 12.6 %collective-permute-start.4 = (bf16[2,2,128,384]{3,2,1,0:T(8,128)(2,1)S(1)}, bf16[2,2,128,384]{3,2,1,0:T(8,128)(2,1)S(1)}, u32[]{:S(2)}, u32[]{:S(2)}) collective-permute-start(bf16[2,2,128,384]{3,2,1,0:T(8,128)(2,1)S(1)} %stack.1.a), channel_id=1, source_target_pairs={{0,408},{1,137},{2,410},{3,139},{4,412},{5,141},{6,414},{7,143},{8... | collective-permute-start | bytes 1179656 | tf_op jit(solution)/shard_map/ppermute | solution.py:36
  37.4 14.0 %collective-permute-start.3 = (bf16[2,2,128,384]{3,2,1,0:T(8,128)(2,1)S(1)}, bf16[2,2,128,384]{3,2,1,0:T(8,128)(2,1)S(1)}, u32[]{:S(2)}, u32[]{:S(2)}) collective-permute-start(bf16[2,2,128,384]{3,2,1,0:T(8,128)(2,1)S(1)} %stack.1.a), channel_id=1, source_target_pairs={{0,384},{1,129},{2,386},{3,131},{4,388},{5,133},{6,390},{7,135},{8... | collective-permute-start | bytes 1179656 | tf_op jit(solution)/shard_map/ppermute | solution.py:36
  40.4 11.0 %collective-permute-start.2 = (bf16[2,2,128,384]{3,2,1,0:T(8,128)(2,1)S(1)}, bf16[2,2,128,384]{3,2,1,0:T(8,128)(2,1)S(1)}, u32[]{:S(2)}, u32[]{:S(2)}) collective-permute-start(bf16[2,2,128,384]{3,2,1,0:T(8,128)(2,1)S(1)} %stack.1.a), channel_id=1, source_target_pairs={{0,24},{1,9},{2,26},{3,11},{4,28},{5,13},{6,30},{7,15},{8,16},{9,1... | collective-permute-start | bytes 1179656 | tf_op jit(solution)/shard_map/ppermute | solution.py:36
  51.4 27.7 %copy-start.2 = (bf16[2,512,384]{2,1,0:T(8,128)(2,1)S(1)}, bf16[2,512,384]{2,1,0:T(8,128)(2,1)}, u32[]{:S(2)}) copy-start(bf16[2,512,384]{2,1,0:T(8,128)(2,1)} %text.1) | copy-start | bytes 2359300
  51.4 27.7 %copy-start.8 = (bf16[128,384]{1,0:T(8,128)(2,1)S(1)}, bf16[128,384]{1,0:T(8,128)(2,1)}, u32[]{:S(2)}) copy-start(bf16[128,384]{1,0:T(8,128)(2,1)} %get-tuple-element.22.k_fresh) | copy-start | bytes 294916
  57.4 21.8 %copy-start.1 = (bf16[3,128,384]{2,1,0:T(8,128)(2,1)S(1)}, bf16[3,128,384]{2,1,0:T(8,128)(2,1)}, u32[]{:S(2)}) copy-start(bf16[3,128,384]{2,1,0:T(8,128)(2,1)} %raw.1) | copy-start | bytes 884740
  57.4 21.8 %copy-start.4 = (bf16[128,384]{1,0:T(8,128)(2,1)S(1)}, bf16[128,384]{1,0:T(8,128)(2,1)}, u32[]{:S(2)}) copy-start(bf16[128,384]{1,0:T(8,128)(2,1)} %get-tuple-element.19.refs_0_.q) | copy-start | bytes 294916
  57.4 28.2 %copy-start = (bf16[384,3072]{1,0:T(8,128)(2,1)S(1)}, bf16[384,3072]{1,0:T(8,128)(2,1)}, u32[]{:S(2)}) copy-start(bf16[384,3072]{1,0:T(8,128)(2,1)} %w.1) | copy-start | bytes 7077892
  73.7 11.8 %collective-permute-start.5 = (bf16[144,384]{1,0:T(8,128)(2,1)S(1)}, bf16[144,384]{1,0:T(8,128)(2,1)S(1)}, u32[]{:S(2)}, u32[]{:S(2)}) collective-permute-start(bf16[144,384]{1,0:T(8,128)(2,1)S(1)} %merge.1), channel_id=1, source_target_pairs={{0,96},{1,33},{2,98},{3,35},{4,100},{5,37},{6,102},{7,39},{8,104},... | collective-permute-start | bytes 331784 | tf_op jit(solution)/shard_map/ppermute | solution.py:36
  80.0 29.0 %copy-start.6 = (bf16[128,384]{1,0:T(8,128)(2,1)S(1)}, bf16[128,384]{1,0:T(8,128)(2,1)}, u32[]{:S(2)}) copy-start(bf16[128,384]{1,0:T(8,128)(2,1)} %hidden.1) | copy-start | bytes 294916
  80.0 29.0 %copy-start.7 = (bf16[128,384]{1,0:T(8,128)(2,1)S(1)}, bf16[128,384]{1,0:T(8,128)(2,1)}, u32[]{:S(2)}) copy-start(bf16[128,384]{1,0:T(8,128)(2,1)} %control.1) | copy-start | bytes 294916
  80.0 29.0 %copy-start.9 = (f32[28,384]{1,0:T(8,128)S(1)}, f32[28,384]{1,0:T(8,128)}, u32[]{:S(2)}) copy-start(f32[28,384]{1,0:T(8,128)} %gate.1) | copy-start | bytes 129028
  86.9 4.9 %collective-permute-start.6 = (bf16[4,128,384]{2,1,0:T(8,128)(2,1)S(1)}, bf16[4,128,384]{2,1,0:T(8,128)(2,1)S(1)}, u32[]{:S(2)}, u32[]{:S(2)}) collective-permute-start(bf16[4,128,384]{2,1,0:T(8,128)(2,1)S(1)} %get-tuple-element.24), channel_id=1, source_target_pairs={{0,1},{1,0},{2,3},{3,2},{4,5},{5,4},{6,7},{7,6},{8,9},{9,8},{10,11... | collective-permute-start | bytes 1179656 | tf_op jit(solution)/shard_map/ppermute | solution.py:36
  91.9 8.0 %collective-permute-start.7 = (bf16[2,128,384]{2,1,0:T(8,128)(2,1)S(1)}, bf16[2,128,384]{2,1,0:T(8,128)(2,1)S(1)}, u32[]{:S(2)}, u32[]{:S(2)}) collective-permute-start(bf16[2,128,384]{2,1,0:T(8,128)(2,1)S(1)} %get-tuple-element.26), channel_id=1, source_target_pairs={{0,2},{1,3},{2,0},{3,1},{4,6},{5,7},{6,4},{7,5},{8,10},{9,11},{10,... | collective-permute-start | bytes 589832 | tf_op jit(solution)/shard_map/ppermute | solution.py:36
  99.9 9.1 %collective-permute-start.8 = (bf16[1,128,384]{2,1,0:T(8,128)(2,1)S(1)}, bf16[1,128,384]{2,1,0:T(8,128)(2,1)S(1)}, u32[]{:S(2)}, u32[]{:S(2)}) collective-permute-start(bf16[1,128,384]{2,1,0:T(8,128)(2,1)S(1)} %get-tuple-element.28), channel_id=1, source_target_pairs={{0,4},{1,5},{2,6},{3,7},{4,0},{5,1},{6,2},{7,3},{8,12},{9,13},{10,... | collective-permute-start | bytes 294920 | tf_op jit(solution)/shard_map/ppermute | solution.py:36

commit v4 on v3

--- a/solution.py
+++ b/solution.py
@@ -36,66 +36,57 @@
     return lax.ppermute(value, AXES, pairs)
 
 
-def squares(flip):
+def query_groups():
     groups = {}
     for i in range(512):
         y, zh, x, zl, c = coords(i)
-        f = flip[c]
-        groups.setdefault((min(x, x ^ f), min(y, y ^ f), zh, zl, c), []).append(i)
+        groups.setdefault((y // 2 if c else x // 2, zh, zl, c), []).append(i)
     return list(groups.values())
 
 
-QUERY_FLIPS = (1, 3)
-QUERY_GROUPS = squares(QUERY_FLIPS)
-KEY_FLIPS = (3, 1)
-
-
-def exchange(value, axes, groups):
-    return lax.all_to_all(value, axes, 0, 0, axis_index_groups=groups, tiled=True)
+QUERY_GROUPS = query_groups()
+
+
+def exchange(value):
+    return lax.all_to_all(value, AXES, 0, 0, axis_index_groups=QUERY_GROUPS, tiled=True)
 
 
 def query_place():
     patch = lax.axis_index("patch")
     x, y = patch % 4, patch // 16
-    first = lax.axis_index("tensor") % 2 == 0
-    return jnp.where(first, y % 2 * 2 + x % 2, y // 2 * 2 + x // 2)
-
-
-def key_square(value):
-    def move(dx, dy):
-        return permute(
-            value,
-            lambda y, zh, x, zl, c: (y ^ dy * KEY_FLIPS[c], zh, x ^ dx * KEY_FLIPS[c], zl, c),
-        )
-
-    return [value, move(1, 0), move(0, 1), move(1, 1)]
-
-
-def spread_kernel(*refs):
-    out = refs[-1]
-    for i in range(4):
-        for j, ref in enumerate(refs[:-1]):
-            out[i, j] = ref[...]
-
-
-def spread(*values):
+    return jnp.where(lax.axis_index("tensor") % 2 == 0, y * 2 + x % 2, y % 2 * 4 + x)
+
+
+def after(value, *others):
+    return lax.optimization_barrier((value,) + others)[0]
+
+
+def spread_kernel(ref, out):
+    for i in range(8):
+        out[i] = ref[...]
+
+
+def spread(value):
     full = pl.BlockSpec(memory_space=pltpu.VMEM)
     return pl.pallas_call(
         spread_kernel,
-        out_shape=jax.ShapeDtypeStruct((4, len(values)) + values[0].shape, BF16),
-        in_specs=[full] * len(values),
+        out_shape=jax.ShapeDtypeStruct((8,) + value.shape, BF16),
+        in_specs=[full],
         out_specs=full,
         compiler_params=pltpu.CompilerParams(vmem_limit_bytes=16 * MIB),
         name="spread",
-    )(*values)
-
-
-def key_pair(value):
-    return permute(value, lambda y, zh, x, zl, c: (y, zh ^ (1, 3)[c], x, zl, c))
-
-
-def query_pair(value):
-    return permute(value, lambda y, zh, x, zl, c: (y, zh ^ (3, 1)[c], x, zl, c))
+    )(value)
+
+
+def z_step(value, n):
+    flips = ((1, 3), (3, 1))[n]
+    return permute(value, lambda y, zh, x, zl, c: (y, zh ^ flips[c], x, zl, c))
+
+
+def plane_step(value):
+    return permute(
+        value, lambda y, zh, x, zl, c: (y ^ 3 * c, zh, x ^ 3 * (1 - c), zl, c)
+    )
 
 
 def swap_core(value):
@@ -183,23 +174,6 @@
     )
 
 
-def stack_kernel(a, b, out):
-    out[0] = a[...]
-    out[1] = b[...]
-
-
-def stack(a, b):
-    full = pl.BlockSpec(memory_space=pltpu.VMEM)
-    return pl.pallas_call(
-        stack_kernel,
-        out_shape=jax.ShapeDtypeStruct((2,) + a.shape, BF16),
-        in_specs=[full] * 2,
-        out_specs=full,
-        compiler_params=pltpu.CompilerParams(vmem_limit_bytes=16 * MIB),
-        name="stack",
-    )(a, b)
-
-
 def split3(v):
     hi = v.astype(BF16).astype(F32)
     rest = v - hi
@@ -259,42 +233,43 @@
     )(*args)
 
 
-def attn_kernel(a, b, c, d, q, out, kc, vc):
+def attn_kernel(*refs):
+    kv = refs[:8]
+    q, out, kc, vc = refs[8:]
     at = query_place()
-    kv = (a, b, c, d)
     for h in range(HEADS_DEV):
         cut = slice(h * HD, (h + 1) * HD)
         for i in range(8):
             rows = slice(i * TOK, (i + 1) * TOK)
-            kc[h, rows, :] = kv[i // 2][i % 2, 0, :, cut]
-            vc[h, rows, 0:HD] = kv[i // 2][i % 2, 1, :, cut]
+            kc[h, rows, :] = kv[i][0, :, cut]
+            vc[h, rows, 0:HD] = kv[i][1, :, cut]
         vc[h, :, HD:] = jnp.ones((8 * TOK, HD), BF16)
 
-    def one(place, half, skip):
+    def one(place, skip):
         o, lse = [], []
         for h in range(HEADS_DEV):
-            x, y = attend(q[place, half, :, h * HD : (h + 1) * HD], kc[h, skip:], vc[h, skip:])
+            x, y = attend(q[place, :, h * HD : (h + 1) * HD], kc[h, skip:], vc[h, skip:])
             o.append(x)
             lse.append(y)
-        put(out.at[place, half], o, lse)
-
-    one(at, 0, TOK)
-    one(at, 1, 0)
+        put(out.at[place], o, lse)
+
+    one(at, TOK)
+    one(at ^ 1, 0)
 
     def step(i, carry):
-        one(at ^ i, 0, 0)
-        one(at ^ i, 1, 0)
+        one(at ^ (2 * i), 0)
+        one(at ^ (2 * i + 1), 0)
         return carry
 
     lax.fori_loop(1, 4, step, 0)
 
 
-def attention(kv, q):
+def attention(*args):
     full = pl.BlockSpec(memory_space=pltpu.VMEM)
     return pl.pallas_call(
         attn_kernel,
-        out_shape=jax.ShapeDtypeStruct((4, 2, TOK + STAT, WIDTH), BF16),
-        in_specs=[full] * 5,
+        out_shape=jax.ShapeDtypeStruct((8, TOK + STAT, WIDTH), BF16),
+        in_specs=[full] * 9,
         out_specs=full,
         scratch_shapes=[
             pltpu.VMEM((HEADS_DEV, 8 * TOK, HD), BF16),
@@ -305,7 +280,7 @@
             flops=4 * 8 * TOK * 8 * TOK * WIDTH, bytes_accessed=4 * MIB, transcendentals=2**22
         ),
         name="attend",
-    )(*kv, q)
+    )(*args)
 
 
 def merge(parts, stats):
@@ -315,7 +290,6 @@
                      for h in range(HEADS_DEV)])
     sub = lax.broadcasted_iota(jnp.int32, (TOK, HD), 0)
     table = jnp.zeros((TOK, HD), F32)
-    lses = []
     for h in range(HEADS_DEV):
         top = rows[0][h]
         for r in rows[1:]:
@@ -324,7 +298,6 @@
         total = weights[0]
         for w in weights[1:]:
             total = total + w
-        lses.append(top + jnp.log2(total))
         for i, w in enumerate(weights):
             table = jnp.where(sub == len(rows) * h + i, w / total, table)
     table = table.T
@@ -336,46 +309,18 @@
             term = part(h) * w
             acc = term if acc is None else acc + term
         outs.append(acc)
-    return outs, lses
-
-
-def partials(ref, half):
+    return outs
+
+
+def partials(refs):
     return (
-        [lambda h, i=i: ref[i, half, 0:TOK, h * HD : (h + 1) * HD].astype(F32) for i in range(4)],
-        [ref[i, half, TOK:, 0:HD].astype(F32) for i in range(4)],
+        [lambda h, r=r: r[0:TOK, h * HD : (h + 1) * HD].astype(F32) for r in refs],
+        [r[TOK:, 0:HD].astype(F32) for r in refs],
     )
 
 
-def merge_kernel(got, out):
-    outs, lses = merge(*partials(got, 1))
-    sub = lax.broadcasted_iota(jnp.int32, (STAT, HD), 0)
-    table = jnp.zeros((STAT, HD), F32)
-    for h in range(HEADS_DEV):
-        out[0:TOK, h * HD : (h + 1) * HD] = outs[h].astype(BF16)
-        for part, v in enumerate(split3(lses[h])):
-            table = jnp.where(sub == 3 * h + part, v, table)
-    out[TOK:, :] = jnp.zeros((STAT, WIDTH), BF16)
-    out[TOK:, 0:HD] = table.astype(BF16)
-
-
-def merge_first(messages):
-    full = pl.BlockSpec(memory_space=pltpu.VMEM)
-    return pl.pallas_call(
-        merge_kernel,
-        out_shape=jax.ShapeDtypeStruct((TOK + STAT, WIDTH), BF16),
-        in_specs=[full],
-        out_specs=full,
-        compiler_params=pltpu.CompilerParams(vmem_limit_bytes=16 * MIB),
-        name="merge",
-    )(messages)
-
-
-def project_kernel(mine, theirs, home, w, keep, give, att):
-    parts, stats = partials(mine, 0)
-    for ref in (theirs, home):
-        parts.append(lambda h, ref=ref: ref[0:TOK, h * HD : (h + 1) * HD].astype(F32))
-        stats.append(ref[TOK:, 0:HD].astype(F32))
-    outs, _ = merge(parts, stats)
+def project_kernel(got, home, w, keep, give, att):
+    outs = merge(*partials([got.at[i] for i in range(8)] + [home]))
     for h in range(HEADS_DEV):
         att[:, h * HD : (h + 1) * HD] = outs[h].astype(BF16)
     t = lax.axis_index("tensor")
@@ -386,7 +331,7 @@
             out[d] = jnp.dot(att[...], part, preferred_element_type=F32).astype(out.dtype)
 
 
-def project(mine, theirs, home, out_weight):
+def project(*args):
     full = pl.BlockSpec(memory_space=pltpu.VMEM)
     return pl.pallas_call(
         project_kernel,
@@ -394,12 +339,12 @@
             jax.ShapeDtypeStruct((4, TOK, WIDTH), F32),
             jax.ShapeDtypeStruct((4, TOK, WIDTH), BF16),
         ),
-        in_specs=[full] * 4,
+        in_specs=[full] * 3,
         out_specs=(full, full),
         scratch_shapes=[pltpu.VMEM((TOK, WIDTH), BF16)],
         compiler_params=pltpu.CompilerParams(vmem_limit_bytes=16 * MIB),
         name="project",
-    )(mine, theirs, home, out_weight)
+    )(*args)
 
 
 def halve_kernel(keep, got, stay, send):
@@ -453,17 +398,17 @@
     hidden_in,
     control,
 ):
+    z1 = z_step(stale_kv, 0)
     q, k_fresh = prepare(fresh_qkv, positions, query_gain, key_gain)
-    pair_q = query_pair(q)
-    stale_kv, q = lax.optimization_barrier((stale_kv, q))
-    pair_kv = key_pair(stale_kv)
-    queries, pair_kv = lax.optimization_barrier((spread(q, pair_q), pair_kv))
-    q_all = exchange(queries, AXES, QUERY_GROUPS)
-    kv = key_square(stack(stale_kv, pair_kv))
+    stale = after(stale_kv, q)
+    z2 = z_step(stale, 1)
+    plane = plane_step(stale)
+    q_all = exchange(spread(q))
+    z1, z2 = after(z1, q_all), after(z2, q_all)
+    z3 = z_step(z1, 1)
+    kv = [stale_kv, plane, z1, plane_step(z1), z2, plane_step(z2), z3, plane_step(z3)]
     home = attend_home(q, k_fresh, fresh_qkv, text_kv)
-    mine = exchange(attention(kv, q_all), AXES, QUERY_GROUPS)
-    theirs = query_pair(merge_first(mine))
-    keep, give = project(mine, theirs, home, out_weight)
+    keep, give = project(exchange(attention(*kv, q_all)), home, out_weight)
     keep, give = halve(keep, swap_core(give))
     keep, give = halve(keep, swap_z(give, 1))
     return finish(timestep, keep, swap_z(give, 2), gate_table, hidden_in, control)

time: 110 us -> 116 us (1.055); the launches traced: 110 us -> 114 us
  starting transfers between devices: 47.3 us -> 72.5 us
  blocking collectives: 15.9 us -> 0 us
  waiting for transfers between devices: 32 us -> 22.1 us
  local copies, waits for them, and re-layouts: 0.93 us -> 6.3 us
    ppermute x9 -> x10, starting transfers between devices: 41.1 us -> 62.5 us  [permute(): return lax.ppermute(value, AXES, pairs)]
    all_to_all x1 -> x0, blocking collectives: 15.9 us -> none  [exchange(): lax.all_to_all(value, axes, 0, 0, axis_index_groups=groups, tiled=True)]
    ppermute x9 -> x10, waiting for transfers between devices: 31.9 us -> 17 us  [permute(): return lax.ppermute(value, AXES, pairs)]
    unnamed x20 -> x26, local copies, waits for them, and re-layouts: 0.93 us -> 6.3 us
    all_to_all x1 -> x2, waiting for transfers between devices: 0.01 us -> 5.17 us  [exchange(): lax.all_to_all(value, AXES, 0, 0, axis_index_groups=QUERY_GROUPS, tiled=T...]
    all_to_all x1 -> x2, starting transfers between devices: 6.2 us -> 10 us  [exchange(): lax.all_to_all(value, AXES, 0, 0, axis_index_groups=QUERY_GROUPS, tiled=T...]
    pallas_call x4 -> x2, Pallas kernels: 7.37 us -> 7.01 us  [the longest x1 6.04 us: attention(): pl.pallas_call(attn_kernel, out_shape=jax.ShapeDtypeStruct((8, TOK + STAT...]
  transfers between devices with their start and end apart: 10 -> 12, of which waited for: 7 -> 7; matrix products, arithmetic and copies ran while one was open for 0% -> 0% of each run, Pallas kernels for 2% -> 1%
where the time goes in v4:
time: 116 us; the launch traced here: 114 us
  starting transfers between devices  72.5 us (62%)
  waiting for transfers between devices  22.1 us (19%)
  Pallas kernels  12.7 us (11%)
  local copies, waits for them, and re-layouts  6.3 us (5%)
    ppermute x10, starting transfers between devices, permute(): return lax.ppermute(value, AXES, pairs)  62.5 us
    ppermute x10, waiting for transfers between devices, permute(): return lax.ppermute(value, AXES, pairs)  17 us
    all_to_all x2, starting transfers between devices, exchange(): lax.all_to_all(value, AXES, 0, 0, axis_index_groups=QUERY_GROUPS, tiled=T...  10 us
    unnamed x26, local copies, waits for them, and re-layouts  6.3 us
    pallas_call x1, Pallas kernels, attention(): pl.pallas_call(attn_kernel, out_shape=jax.ShapeDtypeStruct((8, TOK + STAT...  6.04 us
    all_to_all x2, waiting for transfers between devices, exchange(): lax.all_to_all(value, AXES, 0, 0, axis_index_groups=QUERY_GROUPS, tiled=T...  5.17 us
    pallas_call x1, Pallas kernels, prepare(): pl.pallas_call(prep_kernel, out_shape=(jax.ShapeDtypeStruct((TOK, WIDTH),...  2.58 us
  transfers between devices with their start and end apart: 12, of which 7 were waited for; matrix products, arithmetic and copies ran while one was open for 0% of the time, Pallas kernels for 1%

profile of v4, /device:TPU:1, one launch (start us, length us, event | category | flops | bytes accessed | tf_op | source)
XLA Modules:
  0.0 114.5 jit_solution(5939396000854863454)
XLA Ops:
  0.0 2.6 %prep.1 = (bf16[128,384]{1,0:T(8,128)(2,1)}, bf16[128,384]{1,0:T(8,128)(2,1)}) custom-call(bf16[3,128,384]{2,1,0:T(8,128)(2,1)} %raw.1, s32[1,128]{1,0:T(1,128)} %bitcast.3, f32[8,128]{1,0:T(8,128)} %constant.2.clone.freq_hbm, f32[1,128]{1,0:T(1,128)} %bitcast.4, f32[1,128]{1,0:T(1,128)} %bitcast.5), custom_call_target="tpu_custom_call" | custom-call | tf_op jit(solution)/shard_map/prep/pallas_call | solution.py:154
  3.5 1.0 spread.1
  4.5 5.9 %all-to-all-start = ((bf16[8,128,384]{2,1,0:T(8,128)(2,1)}), bf16[8,128,384]{2,1,0:T(8,128)(2,1)S(1)}, u32[]{:S(2)}, u32[]{:S(2)}) async-start(bf16[8,128,384]{2,1,0:T(8,128)(2,1)} %spread.1), calls=%async_computation | async-start | bytes 1572864 | tf_op jit(solution)/shard_map/all_to_all | solution.py:51
  10.3 12.6 %collective-permute-start.1 = (bf16[2,128,384]{2,1,0:T(8,128)(2,1)S(1)}, bf16[2,128,384]{2,1,0:T(8,128)(2,1)S(1)}, u32[]{:S(2)}, u32[]{:S(2)}) collective-permute-start(bf16[2,128,384]{2,1,0:T(8,128)(2,1)S(1)} %copy-done.12), channel_id=1, source_target_pairs={{0,32},{1,97},{2,34},{3,99},{4,36},{5,101},{6,38},{7,103},{8,40},{... | collective-permute-start | bytes 589832 | tf_op jit(solution)/shard_map/ppermute | solution.py:36
  22.9 5.2 %collective-permute-start.3 = (bf16[2,128,384]{2,1,0:T(8,128)(2,1)S(1)}, bf16[2,128,384]{2,1,0:T(8,128)(2,1)S(1)}, u32[]{:S(2)}, u32[]{:S(2)}) collective-permute-start(bf16[2,128,384]{2,1,0:T(8,128)(2,1)S(1)} %copy-done.12), channel_id=1, source_target_pairs={{0,96},{1,33},{2,98},{3,35},{4,100},{5,37},{6,102},{7,39},{8,104},... | collective-permute-start | bytes 589832 | tf_op jit(solution)/shard_map/ppermute | solution.py:36
  28.1 2.2 %collective-permute-done.1.refs_2_ = bf16[2,128,384]{2,1,0:T(8,128)(2,1)S(1)} collective-permute-done((bf16[2,128,384]{2,1,0:T(8,128)(2,1)S(1)}, bf16[2,128,384]{2,1,0:T(8,128)(2,1)S(1)}, u32[]{:S(2)}, u32[]{:S(2)}) %collective-permute-start.1) | collective-permute-done | bytes 196640 | tf_op jit(solution)/shard_map/ppermute | solution.py:36
  30.3 15.2 %collective-permute-start.5 = (bf16[2,128,384]{2,1,0:T(8,128)(2,1)S(1)}, bf16[2,128,384]{2,1,0:T(8,128)(2,1)S(1)}, u32[]{:S(2)}, u32[]{:S(2)}) collective-permute-start(bf16[2,128,384]{2,1,0:T(8,128)(2,1)S(1)} %collective-permute-done.1.refs_2_), channel_id=1, source_target_pairs={{0,96},{1,33},{2,98},{3,35},{4,100},{5,37},{6,102},{7,39},{8,104},... | collective-permute-start | bytes 589832 | tf_op jit(solution)/shard_map/ppermute | solution.py:36
  45.5 4.8 %collective-permute-start = (bf16[2,128,384]{2,1,0:T(8,128)(2,1)S(1)}, bf16[2,128,384]{2,1,0:T(8,128)(2,1)S(1)}, u32[]{:S(2)}, u32[]{:S(2)}) collective-permute-start(bf16[2,128,384]{2,1,0:T(8,128)(2,1)S(1)} %copy-done.12), channel_id=1, source_target_pairs={{0,24},{1,385},{2,26},{3,387},{4,28},{5,389},{6,30},{7,391},{8,16}... | collective-permute-start | bytes 589832 | tf_op jit(solution)/shard_map/ppermute | solution.py:36
  50.3 1.9 %collective-permute-start.2 = (bf16[2,128,384]{2,1,0:T(8,128)(2,1)S(1)}, bf16[2,128,384]{2,1,0:T(8,128)(2,1)S(1)}, u32[]{:S(2)}, u32[]{:S(2)}) collective-permute-start(bf16[2,128,384]{2,1,0:T(8,128)(2,1)S(1)} %collective-permute-done.1.refs_2_), channel_id=1, source_target_pairs={{0,24},{1,385},{2,26},{3,387},{4,28},{5,389},{6,30},{7,391},{8,16}... | collective-permute-start | bytes 589832 | tf_op jit(solution)/shard_map/ppermute | solution.py:36
  52.2 4.6 %collective-permute-start.4 = (bf16[2,128,384]{2,1,0:T(8,128)(2,1)S(1)}, bf16[2,128,384]{2,1,0:T(8,128)(2,1)S(1)}, u32[]{:S(2)}, u32[]{:S(2)}) collective-permute-start(bf16[2,128,384]{2,1,0:T(8,128)(2,1)S(1)} %collective-permute-done.3.refs_4_), channel_id=1, source_target_pairs={{0,24},{1,385},{2,26},{3,387},{4,28},{5,389},{6,30},{7,391},{8,16}... | collective-permute-start | bytes 589832 | tf_op jit(solution)/shard_map/ppermute | solution.py:36
  56.8 1.9 %collective-permute-start.6 = (bf16[2,128,384]{2,1,0:T(8,128)(2,1)S(1)}, bf16[2,128,384]{2,1,0:T(8,128)(2,1)S(1)}, u32[]{:S(2)}, u32[]{:S(2)}) collective-permute-start(bf16[2,128,384]{2,1,0:T(8,128)(2,1)S(1)} %collective-permute-done.5.refs_6_), channel_id=1, source_target_pairs={{0,24},{1,385},{2,26},{3,387},{4,28},{5,389},{6,30},{7,391},{8,16}... | collective-permute-start | bytes 589832 | tf_op jit(solution)/shard_map/ppermute | solution.py:36
  58.8 1.5 %collective-permute-done.4.refs_5_ = bf16[2,128,384]{2,1,0:T(8,128)(2,1)S(1)} collective-permute-done((bf16[2,128,384]{2,1,0:T(8,128)(2,1)S(1)}, bf16[2,128,384]{2,1,0:T(8,128)(2,1)S(1)}, u32[]{:S(2)}, u32[]{:S(2)}) %collective-permute-start.4) | collective-permute-done | bytes 196640 | tf_op jit(solution)/shard_map/ppermute | solution.py:36
  60.3 4.1 %collective-permute-done.6.refs_7_ = bf16[2,128,384]{2,1,0:T(8,128)(2,1)S(1)} collective-permute-done((bf16[2,128,384]{2,1,0:T(8,128)(2,1)S(1)}, bf16[2,128,384]{2,1,0:T(8,128)(2,1)S(1)}, u32[]{:S(2)}, u32[]{:S(2)}) %collective-permute-start.6) | collective-permute-done | bytes 196640 | tf_op jit(solution)/shard_map/ppermute | solution.py:36
  64.4 6.0 %attend.1 = bf16[8,144,384]{2,1,0:T(8,128)(2,1)S(1)} custom-call(bf16[2,128,384]{2,1,0:T(8,128)(2,1)S(1)} %copy-done.12, bf16[2,128,384]{2,1,0:T(8,128)(2,1)S(1)} %collective-permute-done.refs_1_, bf16[2,128,384]{2,1,0:T(8,128)(2,1)S(1)} %collective-permute-done.1.refs_2_, bf16[2,128,384]{2,1,0:T(8,128)(2,1)S(1)} %collective-permute-done.2.refs_3_, ...), custom_call_target="tpu_custom_call" | custom-call | flops 1610612736 | bytes 4194304 | tf_op jit(solution)/shard_map/attend/pallas_call | solution.py:269
  71.4 4.1 %all-to-all-start.1 = ((bf16[8,144,384]{2,1,0:T(8,128)(2,1)}), bf16[8,144,384]{2,1,0:T(8,128)(2,1)S(1)}, u32[]{:S(2)}, u32[]{:S(2)}) async-start(bf16[8,144,384]{2,1,0:T(8,128)(2,1)} %copy-done.2), calls=%async_computation.1 | async-start | bytes 1769472 | tf_op jit(solution)/shard_map/all_to_all | solution.py:51
  75.6 1.1 copy-done.3
  80.0 5.2 %all-to-all-done.1.got = bf16[8,144,384]{2,1,0:T(8,128)(2,1)S(1)} async-done(((bf16[8,144,384]{2,1,0:T(8,128)(2,1)}), bf16[8,144,384]{2,1,0:T(8,128)(2,1)S(1)}, u32[]{:S(2)}, u32[]{:S(2)}) %all-to-all-start.1) | async-done | bytes 884768 | tf_op jit(solution)/shard_map/all_to_all | solution.py:51
  86.1 1.5 %project.1 = (f32[4,128,384]{2,1,0:T(8,128)S(1)}, bf16[4,128,384]{2,1,0:T(8,128)(2,1)S(1)}) custom-call(bf16[8,144,384]{2,1,0:T(8,128)(2,1)S(1)} %all-to-all-done.1.got, bf16[144,384]{1,0:T(8,128)(2,1)S(1)} %copy-done.5, bf16[384,3072]{1,0:T(8,128)(2,1)S(1)} %copy-done), custom_call_target="tpu_custom_call" | custom-call | tf_op jit(solution)/shard_map/project/pallas_call | solution.py:336
  87.6 7.8 %collective-permute-start.7 = (bf16[4,128,384]{2,1,0:T(8,128)(2,1)S(1)}, bf16[4,128,384]{2,1,0:T(8,128)(2,1)S(1)}, u32[]{:S(2)}, u32[]{:S(2)}) collective-permute-start(bf16[4,128,384]{2,1,0:T(8,128)(2,1)S(1)} %get-tuple-element.22), channel_id=1, source_target_pairs={{0,1},{1,0},{2,3},{3,2},{4,5},{5,4},{6,7},{7,6},{8,9},{9,8},{10,11... | collective-permute-start | bytes 1179656 | tf_op jit(solution)/shard_map/ppermute | solution.py:36
  95.5 1.3 %collective-permute-done.7.got = bf16[4,128,384]{2,1,0:T(8,128)(2,1)S(1)} collective-permute-done((bf16[4,128,384]{2,1,0:T(8,128)(2,1)S(1)}, bf16[4,128,384]{2,1,0:T(8,128)(2,1)S(1)}, u32[]{:S(2)}, u32[]{:S(2)}) %collective-permute-start.7) | collective-permute-done | bytes 393248 | tf_op jit(solution)/shard_map/ppermute | solution.py:36
  96.9 3.7 %collective-permute-start.8 = (bf16[2,128,384]{2,1,0:T(8,128)(2,1)S(1)}, bf16[2,128,384]{2,1,0:T(8,128)(2,1)S(1)}, u32[]{:S(2)}, u32[]{:S(2)}) collective-permute-start(bf16[2,128,384]{2,1,0:T(8,128)(2,1)S(1)} %get-tuple-element.24), channel_id=1, source_target_pairs={{0,2},{1,3},{2,0},{3,1},{4,6},{5,7},{6,4},{7,5},{8,10},{9,11},{10,... | collective-permute-start | bytes 589832 | tf_op jit(solution)/shard_map/ppermute | solution.py:36
  100.6 5.0 %collective-permute-done.8.got = bf16[2,128,384]{2,1,0:T(8,128)(2,1)S(1)} collective-permute-done((bf16[2,128,384]{2,1,0:T(8,128)(2,1)S(1)}, bf16[2,128,384]{2,1,0:T(8,128)(2,1)S(1)}, u32[]{:S(2)}, u32[]{:S(2)}) %collective-permute-start.8) | collective-permute-done | bytes 196640 | tf_op jit(solution)/shard_map/ppermute | solution.py:36
  105.6 4.7 %collective-permute-start.9 = (bf16[1,128,384]{2,1,0:T(8,128)(2,1)S(1)}, bf16[1,128,384]{2,1,0:T(8,128)(2,1)S(1)}, u32[]{:S(2)}, u32[]{:S(2)}) collective-permute-start(bf16[1,128,384]{2,1,0:T(8,128)(2,1)S(1)} %get-tuple-element.26), channel_id=1, source_target_pairs={{0,4},{1,5},{2,6},{3,7},{4,0},{5,1},{6,2},{7,3},{8,12},{9,13},{10,... | collective-permute-start | bytes 294920 | tf_op jit(solution)/shard_map/ppermute | solution.py:36
  111.0 2.8 %collective-permute-done.9.got = bf16[1,128,384]{2,1,0:T(8,128)(2,1)S(1)} collective-permute-done((bf16[1,128,384]{2,1,0:T(8,128)(2,1)S(1)}, bf16[1,128,384]{2,1,0:T(8,128)(2,1)S(1)}, u32[]{:S(2)}, u32[]{:S(2)}) %collective-permute-start.9) | collective-permute-done | bytes 98336 | tf_op jit(solution)/shard_map/ppermute | solution.py:36
  (34 shorter events, 6.8 us)
Async XLA Ops:
  0.0 10.3 %copy-start.12 = (bf16[2,128,384]{2,1,0:T(8,128)(2,1)S(1)}, bf16[2,128,384]{2,1,0:T(8,128)(2,1)}, u32[]{:S(2)}) copy-start(bf16[2,128,384]{2,1,0:T(8,128)(2,1)} %refs_0_.1) | copy-start | bytes 589828
  2.6 0.9 copy-start.6
  4.5 25.9 %all-to-all-start = ((bf16[8,128,384]{2,1,0:T(8,128)(2,1)}), bf16[8,128,384]{2,1,0:T(8,128)(2,1)S(1)}, u32[]{:S(2)}, u32[]{:S(2)}) async-start(bf16[8,128,384]{2,1,0:T(8,128)(2,1)} %spread.1), calls=%async_computation | async-start | bytes 1572864 | tf_op jit(solution)/shard_map/all_to_all | solution.py:51
  10.3 65.3 %copy-start.1 = (bf16[3,128,384]{2,1,0:T(8,128)(2,1)S(1)}, bf16[3,128,384]{2,1,0:T(8,128)(2,1)}, u32[]{:S(2)}) copy-start(bf16[3,128,384]{2,1,0:T(8,128)(2,1)} %raw.1) | copy-start | bytes 884740
  10.3 20.0 %collective-permute-start.1 = (bf16[2,128,384]{2,1,0:T(8,128)(2,1)S(1)}, bf16[2,128,384]{2,1,0:T(8,128)(2,1)S(1)}, u32[]{:S(2)}, u32[]{:S(2)}) collective-permute-start(bf16[2,128,384]{2,1,0:T(8,128)(2,1)S(1)} %copy-done.12), channel_id=1, source_target_pairs={{0,32},{1,97},{2,34},{3,99},{4,36},{5,101},{6,38},{7,103},{8,40},{... | collective-permute-start | bytes 589832 | tf_op jit(solution)/shard_map/ppermute | solution.py:36
  22.9 29.3 %collective-permute-start.3 = (bf16[2,128,384]{2,1,0:T(8,128)(2,1)S(1)}, bf16[2,128,384]{2,1,0:T(8,128)(2,1)S(1)}, u32[]{:S(2)}, u32[]{:S(2)}) collective-permute-start(bf16[2,128,384]{2,1,0:T(8,128)(2,1)S(1)} %copy-done.12), channel_id=1, source_target_pairs={{0,96},{1,33},{2,98},{3,35},{4,100},{5,37},{6,102},{7,39},{8,104},... | collective-permute-start | bytes 589832 | tf_op jit(solution)/shard_map/ppermute | solution.py:36
  30.3 26.5 %collective-permute-start.5 = (bf16[2,128,384]{2,1,0:T(8,128)(2,1)S(1)}, bf16[2,128,384]{2,1,0:T(8,128)(2,1)S(1)}, u32[]{:S(2)}, u32[]{:S(2)}) collective-permute-start(bf16[2,128,384]{2,1,0:T(8,128)(2,1)S(1)} %collective-permute-done.1.refs_2_), channel_id=1, source_target_pairs={{0,96},{1,33},{2,98},{3,35},{4,100},{5,37},{6,102},{7,39},{8,104},... | collective-permute-start | bytes 589832 | tf_op jit(solution)/shard_map/ppermute | solution.py:36
  45.5 13.2 %collective-permute-start = (bf16[2,128,384]{2,1,0:T(8,128)(2,1)S(1)}, bf16[2,128,384]{2,1,0:T(8,128)(2,1)S(1)}, u32[]{:S(2)}, u32[]{:S(2)}) collective-permute-start(bf16[2,128,384]{2,1,0:T(8,128)(2,1)S(1)} %copy-done.12), channel_id=1, source_target_pairs={{0,24},{1,385},{2,26},{3,387},{4,28},{5,389},{6,30},{7,391},{8,16}... | collective-permute-start | bytes 589832 | tf_op jit(solution)/shard_map/ppermute | solution.py:36
  50.3 8.5 %collective-permute-start.2 = (bf16[2,128,384]{2,1,0:T(8,128)(2,1)S(1)}, bf16[2,128,384]{2,1,0:T(8,128)(2,1)S(1)}, u32[]{:S(2)}, u32[]{:S(2)}) collective-permute-start(bf16[2,128,384]{2,1,0:T(8,128)(2,1)S(1)} %collective-permute-done.1.refs_2_), channel_id=1, source_target_pairs={{0,24},{1,385},{2,26},{3,387},{4,28},{5,389},{6,30},{7,391},{8,16}... | collective-permute-start | bytes 589832 | tf_op jit(solution)/shard_map/ppermute | solution.py:36
  52.2 8.1 %collective-permute-start.4 = (bf16[2,128,384]{2,1,0:T(8,128)(2,1)S(1)}, bf16[2,128,384]{2,1,0:T(8,128)(2,1)S(1)}, u32[]{:S(2)}, u32[]{:S(2)}) collective-permute-start(bf16[2,128,384]{2,1,0:T(8,128)(2,1)S(1)} %collective-permute-done.3.refs_4_), channel_id=1, source_target_pairs={{0,24},{1,385},{2,26},{3,387},{4,28},{5,389},{6,30},{7,391},{8,16}... | collective-permute-start | bytes 589832 | tf_op jit(solution)/shard_map/ppermute | solution.py:36
  56.8 7.6 %collective-permute-start.6 = (bf16[2,128,384]{2,1,0:T(8,128)(2,1)S(1)}, bf16[2,128,384]{2,1,0:T(8,128)(2,1)S(1)}, u32[]{:S(2)}, u32[]{:S(2)}) collective-permute-start(bf16[2,128,384]{2,1,0:T(8,128)(2,1)S(1)} %collective-permute-done.5.refs_6_), channel_id=1, source_target_pairs={{0,24},{1,385},{2,26},{3,387},{4,28},{5,389},{6,30},{7,391},{8,16}... | collective-permute-start | bytes 589832 | tf_op jit(solution)/shard_map/ppermute | solution.py:36
  70.5 0.9 copy-start.2
  71.4 13.7 %copy-start = (bf16[384,3072]{1,0:T(8,128)(2,1)S(1)}, bf16[384,3072]{1,0:T(8,128)(2,1)}, u32[]{:S(2)}) copy-start(bf16[384,3072]{1,0:T(8,128)(2,1)} %w.1) | copy-start | bytes 7077892
  71.4 13.7 %all-to-all-start.1 = ((bf16[8,144,384]{2,1,0:T(8,128)(2,1)}), bf16[8,144,384]{2,1,0:T(8,128)(2,1)S(1)}, u32[]{:S(2)}, u32[]{:S(2)}) async-start(bf16[8,144,384]{2,1,0:T(8,128)(2,1)} %copy-done.2), calls=%async_computation.1 | async-start | bytes 1769472 | tf_op jit(solution)/shard_map/all_to_all | solution.py:51
  75.6 1.1 copy-start.3
  76.7 0.9 copy-start.7
  77.6 0.9 copy-start.10
  85.2 0.9 copy-start.5
  86.1 27.7 %copy-start.8 = (bf16[128,384]{1,0:T(8,128)(2,1)S(1)}, bf16[128,384]{1,0:T(8,128)(2,1)}, u32[]{:S(2)}) copy-start(bf16[128,384]{1,0:T(8,128)(2,1)} %hidden.1) | copy-start | bytes 294916
  86.1 27.7 %copy-start.9 = (bf16[128,384]{1,0:T(8,128)(2,1)S(1)}, bf16[128,384]{1,0:T(8,128)(2,1)}, u32[]{:S(2)}) copy-start(bf16[128,384]{1,0:T(8,128)(2,1)} %control.1) | copy-start | bytes 294916
  86.1 27.7 %copy-start.11 = (f32[28,384]{1,0:T(8,128)S(1)}, f32[28,384]{1,0:T(8,128)}, u32[]{:S(2)}) copy-start(f32[28,384]{1,0:T(8,128)} %gate.1) | copy-start | bytes 129028
  87.6 9.2 %collective-permute-start.7 = (bf16[4,128,384]{2,1,0:T(8,128)(2,1)S(1)}, bf16[4,128,384]{2,1,0:T(8,128)(2,1)S(1)}, u32[]{:S(2)}, u32[]{:S(2)}) collective-permute-start(bf16[4,128,384]{2,1,0:T(8,128)(2,1)S(1)} %get-tuple-element.22), channel_id=1, source_target_pairs={{0,1},{1,0},{2,3},{3,2},{4,5},{5,4},{6,7},{7,6},{8,9},{9,8},{10,11... | collective-permute-start | bytes 1179656 | tf_op jit(solution)/shard_map/ppermute | solution.py:36
  96.9 8.7 %collective-permute-start.8 = (bf16[2,128,384]{2,1,0:T(8,128)(2,1)S(1)}, bf16[2,128,384]{2,1,0:T(8,128)(2,1)S(1)}, u32[]{:S(2)}, u32[]{:S(2)}) collective-permute-start(bf16[2,128,384]{2,1,0:T(8,128)(2,1)S(1)} %get-tuple-element.24), channel_id=1, source_target_pairs={{0,2},{1,3},{2,0},{3,1},{4,6},{5,7},{6,4},{7,5},{8,10},{9,11},{10,... | collective-permute-start | bytes 589832 | tf_op jit(solution)/shard_map/ppermute | solution.py:36
  105.6 8.2 %collective-permute-start.9 = (bf16[1,128,384]{2,1,0:T(8,128)(2,1)S(1)}, bf16[1,128,384]{2,1,0:T(8,128)(2,1)S(1)}, u32[]{:S(2)}, u32[]{:S(2)}) collective-permute-start(bf16[1,128,384]{2,1,0:T(8,128)(2,1)S(1)} %get-tuple-element.26), channel_id=1, source_target_pairs={{0,4},{1,5},{2,6},{3,7},{4,0},{5,1},{6,2},{7,3},{8,12},{9,13},{10,... | collective-permute-start | bytes 294920 | tf_op jit(solution)/shard_map/ppermute | solution.py:36
  (1 other events, 0.7 us)

commit v5 on v3

--- a/solution.py
+++ b/solution.py
@@ -61,14 +61,13 @@
     return jnp.where(first, y % 2 * 2 + x % 2, y // 2 * 2 + x // 2)
 
 
-def key_square(value):
-    def move(dx, dy):
+def square(values, flips):
+    def move(value, dx, dy):
         return permute(
-            value,
-            lambda y, zh, x, zl, c: (y ^ dy * KEY_FLIPS[c], zh, x ^ dx * KEY_FLIPS[c], zl, c),
+            value, lambda y, zh, x, zl, c: (y ^ dy * flips[c], zh, x ^ dx * flips[c], zl, c)
         )
 
-    return [value, move(1, 0), move(0, 1), move(1, 1)]
+    return [values[0], move(values[1], 1, 0), move(values[2], 0, 1), move(values[3], 1, 1)]
 
 
 def spread_kernel(*refs):
@@ -259,9 +258,9 @@
     )(*args)
 
 
-def attn_kernel(a, b, c, d, q, out, kc, vc):
+def attn_kernel(*refs):
     at = query_place()
-    kv = (a, b, c, d)
+    kv, q, outs, kc, vc = refs[:4], refs[4], refs[5:9], refs[9], refs[10]
     for h in range(HEADS_DEV):
         cut = slice(h * HD, (h + 1) * HD)
         for i in range(8):
@@ -270,32 +269,25 @@
             vc[h, rows, 0:HD] = kv[i // 2][i % 2, 1, :, cut]
         vc[h, :, HD:] = jnp.ones((8 * TOK, HD), BF16)
 
-    def one(place, half, skip):
-        o, lse = [], []
-        for h in range(HEADS_DEV):
-            x, y = attend(q[place, half, :, h * HD : (h + 1) * HD], kc[h, skip:], vc[h, skip:])
-            o.append(x)
-            lse.append(y)
-        put(out.at[place, half], o, lse)
-
-    one(at, 0, TOK)
-    one(at, 1, 0)
-
-    def step(i, carry):
-        one(at ^ i, 0, 0)
-        one(at ^ i, 1, 0)
-        return carry
-
-    lax.fori_loop(1, 4, step, 0)
+    for d in range(4):
+        for half in range(2):
+            skip = TOK if d == 0 and half == 0 else 0
+            o, lse = [], []
+            for h in range(HEADS_DEV):
+                rows = q[at ^ d, half, :, h * HD : (h + 1) * HD]
+                x, y = attend(rows, kc[h, skip:], vc[h, skip:])
+                o.append(x)
+                lse.append(y)
+            put(outs[d].at[half], o, lse)
 
 
 def attention(kv, q):
     full = pl.BlockSpec(memory_space=pltpu.VMEM)
     return pl.pallas_call(
         attn_kernel,
-        out_shape=jax.ShapeDtypeStruct((4, 2, TOK + STAT, WIDTH), BF16),
+        out_shape=(jax.ShapeDtypeStruct((2, TOK + STAT, WIDTH), BF16),) * 4,
         in_specs=[full] * 5,
-        out_specs=full,
+        out_specs=(full,) * 4,
         scratch_shapes=[
             pltpu.VMEM((HEADS_DEV, 8 * TOK, HD), BF16),
             pltpu.VMEM((HEADS_DEV, 8 * TOK, 2 * HD), BF16),
@@ -339,15 +331,15 @@
     return outs, lses
 
 
-def partials(ref, half):
+def partials(refs, half):
     return (
-        [lambda h, i=i: ref[i, half, 0:TOK, h * HD : (h + 1) * HD].astype(F32) for i in range(4)],
-        [ref[i, half, TOK:, 0:HD].astype(F32) for i in range(4)],
+        [lambda h, r=r: r[half, 0:TOK, h * HD : (h + 1) * HD].astype(F32) for r in refs],
+        [r[half, TOK:, 0:HD].astype(F32) for r in refs],
     )
 
 
-def merge_kernel(got, out):
-    outs, lses = merge(*partials(got, 1))
+def merge_kernel(a, b, c, d, out):
+    outs, lses = merge(*partials((a, b, c, d), 1))
     sub = lax.broadcasted_iota(jnp.int32, (STAT, HD), 0)
     table = jnp.zeros((STAT, HD), F32)
     for h in range(HEADS_DEV):
@@ -358,20 +350,20 @@
     out[TOK:, 0:HD] = table.astype(BF16)
 
 
-def merge_first(messages):
+def merge_first(*messages):
     full = pl.BlockSpec(memory_space=pltpu.VMEM)
     return pl.pallas_call(
         merge_kernel,
         out_shape=jax.ShapeDtypeStruct((TOK + STAT, WIDTH), BF16),
-        in_specs=[full],
+        in_specs=[full] * 4,
         out_specs=full,
         compiler_params=pltpu.CompilerParams(vmem_limit_bytes=16 * MIB),
         name="merge",
-    )(messages)
-
-
-def project_kernel(mine, theirs, home, w, keep, give, att):
-    parts, stats = partials(mine, 0)
+    )(*messages)
+
+
+def project_kernel(a, b, c, d, theirs, home, w, keep, give, att):
+    parts, stats = partials((a, b, c, d), 0)
     for ref in (theirs, home):
         parts.append(lambda h, ref=ref: ref[0:TOK, h * HD : (h + 1) * HD].astype(F32))
         stats.append(ref[TOK:, 0:HD].astype(F32))
@@ -380,13 +372,13 @@
         att[:, h * HD : (h + 1) * HD] = outs[h].astype(BF16)
     t = lax.axis_index("tensor")
     zl, core = t // 2, t % 2
-    for d in range(4):
+    for slot in range(4):
         for out, c in ((give, 1 - core), (keep, core)):
-            part = w[:, pl.ds(pl.multiple_of((2 * (zl ^ d) + c) * WIDTH, HD), WIDTH)]
-            out[d] = jnp.dot(att[...], part, preferred_element_type=F32).astype(out.dtype)
-
-
-def project(mine, theirs, home, out_weight):
+            part = w[:, pl.ds(pl.multiple_of((2 * (zl ^ slot) + c) * WIDTH, HD), WIDTH)]
+            out[slot] = jnp.dot(att[...], part, preferred_element_type=F32).astype(out.dtype)
+
+
+def project(*args):
     full = pl.BlockSpec(memory_space=pltpu.VMEM)
     return pl.pallas_call(
         project_kernel,
@@ -394,50 +386,49 @@
             jax.ShapeDtypeStruct((4, TOK, WIDTH), F32),
             jax.ShapeDtypeStruct((4, TOK, WIDTH), BF16),
         ),
-        in_specs=[full] * 4,
+        in_specs=[full] * 7,
         out_specs=(full, full),
         scratch_shapes=[pltpu.VMEM((TOK, WIDTH), BF16)],
         compiler_params=pltpu.CompilerParams(vmem_limit_bytes=16 * MIB),
         name="project",
-    )(mine, theirs, home, out_weight)
-
-
-def halve_kernel(keep, got, stay, send):
-    n = stay.shape[0]
-    for i in range(n):
-        stay[i] = keep[2 * i] + got[2 * i].astype(F32)
-        send[i] = (keep[2 * i + 1] + got[2 * i + 1].astype(F32)).astype(BF16)
-
-
-def halve(keep, got):
-    full = pl.BlockSpec(memory_space=pltpu.VMEM)
-    shape = (keep.shape[0] // 2, TOK, WIDTH)
-    return pl.pallas_call(
-        halve_kernel,
-        out_shape=(jax.ShapeDtypeStruct(shape, F32), jax.ShapeDtypeStruct(shape, BF16)),
+    )(*args)
+
+
+def core_kernel(keep, got, own, *outs):
+    own[...] = keep[0] + got[0].astype(F32)
+    for d in range(1, 4):
+        outs[d - 1][...] = (keep[d] + got[d].astype(F32)).astype(BF16)
+
+
+def core_sum(keep, got):
+    full = pl.BlockSpec(memory_space=pltpu.VMEM)
+    return pl.pallas_call(
+        core_kernel,
+        out_shape=(jax.ShapeDtypeStruct((TOK, WIDTH), F32),)
+        + (jax.ShapeDtypeStruct((TOK, WIDTH), BF16),) * 3,
         in_specs=[full] * 2,
-        out_specs=(full, full),
-        compiler_params=pltpu.CompilerParams(vmem_limit_bytes=16 * MIB),
-        name="halve",
+        out_specs=(full,) * 4,
+        compiler_params=pltpu.CompilerParams(vmem_limit_bytes=16 * MIB),
+        name="core_sum",
     )(keep, got)
 
 
-def final_kernel(step, own, got, gate, hidden, control, out):
-    total = own[0] + got[0].astype(F32)
+def final_kernel(step, own, a, b, c, gate, hidden, control, out):
+    total = own[...] + a[...].astype(F32) + b[...].astype(F32) + c[...].astype(F32)
     row = gate[pl.ds(step[0], 1), :]
     out[...] = (hidden[...].astype(F32) + row * total + control[...].astype(F32)).astype(BF16)
 
 
-def finish(timestep, own, got, gate_table, hidden_in, control):
+def finish(timestep, *args):
     full = pl.BlockSpec(memory_space=pltpu.VMEM)
     return pl.pallas_call(
         final_kernel,
         out_shape=jax.ShapeDtypeStruct((TOK, WIDTH), BF16),
-        in_specs=[pl.BlockSpec(memory_space=pltpu.SMEM)] + [full] * 5,
+        in_specs=[pl.BlockSpec(memory_space=pltpu.SMEM)] + [full] * 7,
         out_specs=full,
         compiler_params=pltpu.CompilerParams(vmem_limit_bytes=16 * MIB),
         name="finish",
-    )(timestep, own, got, gate_table, hidden_in, control)
+    )(timestep, *args)
 
 
 def body(
@@ -459,14 +450,14 @@
     pair_kv = key_pair(stale_kv)
     queries, pair_kv = lax.optimization_barrier((spread(q, pair_q), pair_kv))
     q_all = exchange(queries, AXES, QUERY_GROUPS)
-    kv = key_square(stack(stale_kv, pair_kv))
+    kv = square([stack(stale_kv, pair_kv)] * 4, KEY_FLIPS)
     home = attend_home(q, k_fresh, fresh_qkv, text_kv)
-    mine = exchange(attention(kv, q_all), AXES, QUERY_GROUPS)
-    theirs = query_pair(merge_first(mine))
-    keep, give = project(mine, theirs, home, out_weight)
-    keep, give = halve(keep, swap_core(give))
-    keep, give = halve(keep, swap_z(give, 1))
-    return finish(timestep, keep, swap_z(give, 2), gate_table, hidden_in, control)
+    mine = square(attention(kv, q_all), QUERY_FLIPS)
+    theirs = query_pair(merge_first(*mine))
+    keep, give = project(*mine, theirs, home, out_weight)
+    own, *parts = core_sum(keep, swap_core(give))
+    parts = [swap_z(p, d + 1) for d, p in enumerate(parts)]
+    return finish(timestep, own, *parts, gate_table, hidden_in, control)
 
 
 def solution(mesh):

time: 110 us -> 111 us (level)
  the two profiles are of different devices: /device:TPU:1 before, /device:TPU:18 now
where the time goes in v5:
time: 111 us; the launch traced here: 110 us
  starting transfers between devices  64.1 us (58%)
  waiting for transfers between devices  31.2 us (28%)
  Pallas kernels  11.5 us (10%)
  local copies, waits for them, and re-layouts  2.69 us (2%)
    ppermute x13, starting transfers between devices, permute(): return lax.ppermute(value, AXES, pairs)  60.1 us
    ppermute x13, waiting for transfers between devices, permute(): return lax.ppermute(value, AXES, pairs)  31.2 us
    pallas_call x1, Pallas kernels, attention(): pl.pallas_call(attn_kernel, out_shape=(jax.ShapeDtypeStruct((2, TOK + STA...  4.55 us
    all_to_all x1, starting transfers between devices, exchange(): lax.all_to_all(value, axes, 0, 0, axis_index_groups=groups, tiled=True)  4.01 us
    unnamed x24, local copies, waits for them, and re-layouts  2.69 us
    pallas_call x1, Pallas kernels, prepare(): pl.pallas_call(prep_kernel, out_shape=(jax.ShapeDtypeStruct((TOK, WIDTH),...  2.57 us
  transfers between devices with their start and end apart: 14, of which 10 were waited for; matrix products, arithmetic and copies ran while one was open for 0% of the time, Pallas kernels for 2%

profile of v5, /device:TPU:18, one launch (start us, length us, event | category | flops | bytes accessed | tf_op | source)
XLA Modules:
  0.0 110.3 jit_solution(11553923313854194131)
XLA Ops:
  0.0 2.6 %prep.1 = (bf16[128,384]{1,0:T(8,128)(2,1)}, bf16[128,384]{1,0:T(8,128)(2,1)}) custom-call(bf16[3,128,384]{2,1,0:T(8,128)(2,1)} %raw.1, s32[1,128]{1,0:T(1,128)} %bitcast.3, f32[8,128]{1,0:T(8,128)} %constant.2.clone.freq_hbm, f32[1,128]{1,0:T(1,128)} %bitcast.4, f32[1,128]{1,0:T(1,128)} %bitcast.5), custom_call_target="tpu_custom_call" | custom-call | tf_op jit(solution)/shard_map/prep/pallas_call | solution.py:162
  2.6 9.1 %collective-permute-start.1 = (bf16[2,128,384]{2,1,0:T(8,128)(2,1)}, bf16[2,128,384]{2,1,0:T(8,128)(2,1)S(1)}, u32[]{:S(2)}, u32[]{:S(2)}) collective-permute-start(bf16[2,128,384]{2,1,0:T(8,128)(2,1)} %a), channel_id=1, source_target_pairs={{0,32},{1,97},{2,34},{3,99},{4,36},{5,101},{6,38},{7,103},{8,40},{... | collective-permute-start | bytes 589832 | tf_op jit(solution)/shard_map/ppermute | solution.py:36
  11.7 9.1 %collective-permute-start = (bf16[128,384]{1,0:T(8,128)(2,1)}, bf16[128,384]{1,0:T(8,128)(2,1)S(1)}, u32[]{:S(2)}, u32[]{:S(2)}) collective-permute-start(bf16[128,384]{1,0:T(8,128)(2,1)} %get-tuple-element.23.refs_0_.q), channel_id=1, source_target_pairs={{0,96},{1,33},{2,98},{3,35},{4,100},{5,37},{6,102},{7,39},{8,104},... | collective-permute-start | bytes 294920 | tf_op jit(solution)/shard_map/ppermute | solution.py:36
  20.8 7.4 %collective-permute-done.refs_1_ = bf16[128,384]{1,0:T(8,128)(2,1)S(1)} collective-permute-done((bf16[128,384]{1,0:T(8,128)(2,1)}, bf16[128,384]{1,0:T(8,128)(2,1)S(1)}, u32[]{:S(2)}, u32[]{:S(2)}) %collective-permute-start) | collective-permute-done | bytes 98336 | tf_op jit(solution)/shard_map/ppermute | solution.py:36
  30.1 4.0 %all-to-all-start = ((bf16[4,2,128,384]{3,2,1,0:T(8,128)(2,1)}), bf16[4,2,128,384]{3,2,1,0:T(8,128)(2,1)S(1)}, u32[]{:S(2)}, u32[]{:S(2)}) async-start(bf16[4,2,128,384]{3,2,1,0:T(8,128)(2,1)} %spread.1), calls=%async_computation | async-start | bytes 1572864 | tf_op jit(solution)/shard_map/all_to_all | solution.py:54
  34.2 3.3 %collective-permute-start.4 = (bf16[2,2,128,384]{3,2,1,0:T(8,128)(2,1)S(1)}, bf16[2,2,128,384]{3,2,1,0:T(8,128)(2,1)S(1)}, u32[]{:S(2)}, u32[]{:S(2)}) collective-permute-start(bf16[2,2,128,384]{3,2,1,0:T(8,128)(2,1)S(1)} %stack.1.refs_0_), channel_id=1, source_target_pairs={{0,408},{1,137},{2,410},{3,139},{4,412},{5,141},{6,414},{7,143},{8... | collective-permute-start | bytes 1179656 | tf_op jit(solution)/shard_map/ppermute | solution.py:36
  37.6 3.1 %collective-permute-start.3 = (bf16[2,2,128,384]{3,2,1,0:T(8,128)(2,1)S(1)}, bf16[2,2,128,384]{3,2,1,0:T(8,128)(2,1)S(1)}, u32[]{:S(2)}, u32[]{:S(2)}) collective-permute-start(bf16[2,2,128,384]{3,2,1,0:T(8,128)(2,1)S(1)} %stack.1.refs_0_), channel_id=1, source_target_pairs={{0,384},{1,129},{2,386},{3,131},{4,388},{5,133},{6,390},{7,135},{8... | collective-permute-start | bytes 1179656 | tf_op jit(solution)/shard_map/ppermute | solution.py:36
  40.6 2.9 %collective-permute-start.2 = (bf16[2,2,128,384]{3,2,1,0:T(8,128)(2,1)S(1)}, bf16[2,2,128,384]{3,2,1,0:T(8,128)(2,1)S(1)}, u32[]{:S(2)}, u32[]{:S(2)}) collective-permute-start(bf16[2,2,128,384]{3,2,1,0:T(8,128)(2,1)S(1)} %stack.1.refs_0_), channel_id=1, source_target_pairs={{0,24},{1,9},{2,26},{3,11},{4,28},{5,13},{6,30},{7,15},{8,16},{9,1... | collective-permute-start | bytes 1179656 | tf_op jit(solution)/shard_map/ppermute | solution.py:36
  45.0 4.1 %collective-permute-done.3.refs_2_ = bf16[2,2,128,384]{3,2,1,0:T(8,128)(2,1)S(1)} collective-permute-done((bf16[2,2,128,384]{3,2,1,0:T(8,128)(2,1)S(1)}, bf16[2,2,128,384]{3,2,1,0:T(8,128)(2,1)S(1)}, u32[]{:S(2)}, u32[]{:S(2)}) %collective-permute-start.3) | collective-permute-done | bytes 393248 | tf_op jit(solution)/shard_map/ppermute | solution.py:36
  52.1 4.5 %attend.1 = (bf16[2,144,384]{2,1,0:T(8,128)(2,1)S(1)}, bf16[2,144,384]{2,1,0:T(8,128)(2,1)S(1)}, bf16[2,144,384]{2,1,0:T(8,128)(2,1)S(1)}, bf16[2,144,384]{2,1,0:T(8,128)(2,1)S(1)}) custom-call(bf16[2,2,128,384]{3,2,1,0:T(8,128)(2,1)S(1)} %stack.1.refs_0_, bf16[2,2,128,384]{3,2,1,0:T(8,128)(2,1)S(1)} %copy-done.11, ...), custom_call_target="tpu_custom_call" | custom-call | flops 1610612736 | bytes 4194304 | tf_op jit(solution)/shard_map/attend/pallas_call | solution.py:286
  56.6 5.8 %collective-permute-start.5 = (bf16[2,144,384]{2,1,0:T(8,128)(2,1)S(1)}, bf16[2,144,384]{2,1,0:T(8,128)(2,1)S(1)}, u32[]{:S(2)}, u32[]{:S(2)}) collective-permute-start(bf16[2,144,384]{2,1,0:T(8,128)(2,1)S(1)} %get-tuple-element.27), channel_id=1, source_target_pairs={{0,8},{1,25},{2,10},{3,27},{4,12},{5,29},{6,14},{7,31},{8,0},{9,17... | collective-permute-start | bytes 663560 | tf_op jit(solution)/shard_map/ppermute | solution.py:36
  62.4 4.6 %collective-permute-start.6 = (bf16[2,144,384]{2,1,0:T(8,128)(2,1)S(1)}, bf16[2,144,384]{2,1,0:T(8,128)(2,1)S(1)}, u32[]{:S(2)}, u32[]{:S(2)}) collective-permute-start(bf16[2,144,384]{2,1,0:T(8,128)(2,1)S(1)} %get-tuple-element.28), channel_id=1, source_target_pairs={{0,128},{1,385},{2,130},{3,387},{4,132},{5,389},{6,134},{7,391},{8... | collective-permute-start | bytes 663560 | tf_op jit(solution)/shard_map/ppermute | solution.py:36
  67.0 1.9 %collective-permute-start.7 = (bf16[2,144,384]{2,1,0:T(8,128)(2,1)S(1)}, bf16[2,144,384]{2,1,0:T(8,128)(2,1)S(1)}, u32[]{:S(2)}, u32[]{:S(2)}) collective-permute-start(bf16[2,144,384]{2,1,0:T(8,128)(2,1)S(1)} %get-tuple-element.29), channel_id=1, source_target_pairs={{0,136},{1,409},{2,138},{3,411},{4,140},{5,413},{6,142},{7,415},{8... | collective-permute-start | bytes 663560 | tf_op jit(solution)/shard_map/ppermute | solution.py:36
  69.0 2.0 %collective-permute-done.6.c = bf16[2,144,384]{2,1,0:T(8,128)(2,1)S(1)} collective-permute-done((bf16[2,144,384]{2,1,0:T(8,128)(2,1)S(1)}, bf16[2,144,384]{2,1,0:T(8,128)(2,1)S(1)}, u32[]{:S(2)}, u32[]{:S(2)}) %collective-permute-start.6) | collective-permute-done | bytes 221216 | tf_op jit(solution)/shard_map/ppermute | solution.py:36
  70.9 4.8 %collective-permute-done.7.d = bf16[2,144,384]{2,1,0:T(8,128)(2,1)S(1)} collective-permute-done((bf16[2,144,384]{2,1,0:T(8,128)(2,1)S(1)}, bf16[2,144,384]{2,1,0:T(8,128)(2,1)S(1)}, u32[]{:S(2)}, u32[]{:S(2)}) %collective-permute-start.7) | collective-permute-done | bytes 221216 | tf_op jit(solution)/shard_map/ppermute | solution.py:36
  76.2 8.2 %collective-permute-start.8 = (bf16[144,384]{1,0:T(8,128)(2,1)S(1)}, bf16[144,384]{1,0:T(8,128)(2,1)S(1)}, u32[]{:S(2)}, u32[]{:S(2)}) collective-permute-start(bf16[144,384]{1,0:T(8,128)(2,1)S(1)} %merge.1), channel_id=1, source_target_pairs={{0,96},{1,33},{2,98},{3,35},{4,100},{5,37},{6,102},{7,39},{8,104},... | collective-permute-start | bytes 331784 | tf_op jit(solution)/shard_map/ppermute | solution.py:36
  85.2 3.5 %collective-permute-done.8.theirs = bf16[144,384]{1,0:T(8,128)(2,1)S(1)} collective-permute-done((bf16[144,384]{1,0:T(8,128)(2,1)S(1)}, bf16[144,384]{1,0:T(8,128)(2,1)S(1)}, u32[]{:S(2)}, u32[]{:S(2)}) %collective-permute-start.8) | collective-permute-done | bytes 110624 | tf_op jit(solution)/shard_map/ppermute | solution.py:36
  90.1 1.9 %collective-permute-start.9 = (bf16[4,128,384]{2,1,0:T(8,128)(2,1)S(1)}, bf16[4,128,384]{2,1,0:T(8,128)(2,1)S(1)}, u32[]{:S(2)}, u32[]{:S(2)}) collective-permute-start(bf16[4,128,384]{2,1,0:T(8,128)(2,1)S(1)} %get-tuple-element.32), channel_id=1, source_target_pairs={{0,1},{1,0},{2,3},{3,2},{4,5},{5,4},{6,7},{7,6},{8,9},{9,8},{10,11... | collective-permute-start | bytes 1179656 | tf_op jit(solution)/shard_map/ppermute | solution.py:36
  92.1 1.7 %collective-permute-done.9.got = bf16[4,128,384]{2,1,0:T(8,128)(2,1)S(1)} collective-permute-done((bf16[4,128,384]{2,1,0:T(8,128)(2,1)S(1)}, bf16[4,128,384]{2,1,0:T(8,128)(2,1)S(1)}, u32[]{:S(2)}, u32[]{:S(2)}) %collective-permute-start.9) | collective-permute-done | bytes 393248 | tf_op jit(solution)/shard_map/ppermute | solution.py:36
  93.8 1.9 %collective-permute-start.10 = (bf16[128,384]{1,0:T(8,128)(2,1)S(1)}, bf16[128,384]{1,0:T(8,128)(2,1)S(1)}, u32[]{:S(2)}, u32[]{:S(2)}) collective-permute-start(bf16[128,384]{1,0:T(8,128)(2,1)S(1)} %get-tuple-element.34), channel_id=1, source_target_pairs={{0,2},{1,3},{2,0},{3,1},{4,6},{5,7},{6,4},{7,5},{8,10},{9,11},{10,... | collective-permute-start | bytes 294920 | tf_op jit(solution)/shard_map/ppermute | solution.py:36
  95.8 5.5 %collective-permute-start.11 = (bf16[128,384]{1,0:T(8,128)(2,1)S(1)}, bf16[128,384]{1,0:T(8,128)(2,1)S(1)}, u32[]{:S(2)}, u32[]{:S(2)}) collective-permute-start(bf16[128,384]{1,0:T(8,128)(2,1)S(1)} %get-tuple-element.35), channel_id=1, source_target_pairs={{0,4},{1,5},{2,6},{3,7},{4,0},{5,1},{6,2},{7,3},{8,12},{9,13},{10,... | collective-permute-start | bytes 294920 | tf_op jit(solution)/shard_map/ppermute | solution.py:36
  101.2 2.7 %collective-permute-start.12 = (bf16[128,384]{1,0:T(8,128)(2,1)S(1)}, bf16[128,384]{1,0:T(8,128)(2,1)S(1)}, u32[]{:S(2)}, u32[]{:S(2)}) collective-permute-start(bf16[128,384]{1,0:T(8,128)(2,1)S(1)} %get-tuple-element.36), channel_id=1, source_target_pairs={{0,6},{1,7},{2,4},{3,5},{4,2},{5,3},{6,0},{7,1},{8,14},{9,15},{10,... | collective-permute-start | bytes 294920 | tf_op jit(solution)/shard_map/ppermute | solution.py:36
  104.6 2.1 %collective-permute-done.11.b = bf16[128,384]{1,0:T(8,128)(2,1)S(1)} collective-permute-done((bf16[128,384]{1,0:T(8,128)(2,1)S(1)}, bf16[128,384]{1,0:T(8,128)(2,1)S(1)}, u32[]{:S(2)}, u32[]{:S(2)}) %collective-permute-start.11) | collective-permute-done | bytes 98336 | tf_op jit(solution)/shard_map/ppermute | solution.py:36
  106.7 2.9 %collective-permute-done.12.c = bf16[128,384]{1,0:T(8,128)(2,1)S(1)} collective-permute-done((bf16[128,384]{1,0:T(8,128)(2,1)S(1)}, bf16[128,384]{1,0:T(8,128)(2,1)S(1)}, u32[]{:S(2)}, u32[]{:S(2)}) %collective-permute-start.12) | collective-permute-done | bytes 98336 | tf_op jit(solution)/shard_map/ppermute | solution.py:36
  (37 shorter events, 9.7 us)
Async XLA Ops:
  0.0 34.1 %copy-start.5 = (bf16[2,128,384]{2,1,0:T(8,128)(2,1)S(1)}, bf16[2,128,384]{2,1,0:T(8,128)(2,1)}, u32[]{:S(2)}) copy-start(bf16[2,128,384]{2,1,0:T(8,128)(2,1)} %a) | copy-start | bytes 589828
  2.6 27.5 %collective-permute-start.1 = (bf16[2,128,384]{2,1,0:T(8,128)(2,1)}, bf16[2,128,384]{2,1,0:T(8,128)(2,1)S(1)}, u32[]{:S(2)}, u32[]{:S(2)}) collective-permute-start(bf16[2,128,384]{2,1,0:T(8,128)(2,1)} %a), channel_id=1, source_target_pairs={{0,32},{1,97},{2,34},{3,99},{4,36},{5,101},{6,38},{7,103},{8,40},{... | collective-permute-start | bytes 589832 | tf_op jit(solution)/shard_map/ppermute | solution.py:36
  11.7 16.6 %collective-permute-start = (bf16[128,384]{1,0:T(8,128)(2,1)}, bf16[128,384]{1,0:T(8,128)(2,1)S(1)}, u32[]{:S(2)}, u32[]{:S(2)}) collective-permute-start(bf16[128,384]{1,0:T(8,128)(2,1)} %get-tuple-element.23.refs_0_.q), channel_id=1, source_target_pairs={{0,96},{1,33},{2,98},{3,35},{4,100},{5,37},{6,102},{7,39},{8,104},... | collective-permute-start | bytes 294920 | tf_op jit(solution)/shard_map/ppermute | solution.py:36
  30.1 21.0 %all-to-all-start = ((bf16[4,2,128,384]{3,2,1,0:T(8,128)(2,1)}), bf16[4,2,128,384]{3,2,1,0:T(8,128)(2,1)S(1)}, u32[]{:S(2)}, u32[]{:S(2)}) async-start(bf16[4,2,128,384]{3,2,1,0:T(8,128)(2,1)} %spread.1), calls=%async_computation | async-start | bytes 1572864 | tf_op jit(solution)/shard_map/all_to_all | solution.py:54
  34.2 50.2 %copy-start.1 = (bf16[3,128,384]{2,1,0:T(8,128)(2,1)S(1)}, bf16[3,128,384]{2,1,0:T(8,128)(2,1)}, u32[]{:S(2)}) copy-start(bf16[3,128,384]{2,1,0:T(8,128)(2,1)} %raw.1) | copy-start | bytes 884740
  34.2 50.2 %copy-start.2 = (bf16[2,512,384]{2,1,0:T(8,128)(2,1)S(1)}, bf16[2,512,384]{2,1,0:T(8,128)(2,1)}, u32[]{:S(2)}) copy-start(bf16[2,512,384]{2,1,0:T(8,128)(2,1)} %text.1) | copy-start | bytes 2359300
  34.2 50.2 %copy-start.4 = (bf16[128,384]{1,0:T(8,128)(2,1)S(1)}, bf16[128,384]{1,0:T(8,128)(2,1)}, u32[]{:S(2)}) copy-start(bf16[128,384]{1,0:T(8,128)(2,1)} %get-tuple-element.23.refs_0_.q) | copy-start | bytes 294916
  34.2 50.2 %copy-start.8 = (bf16[128,384]{1,0:T(8,128)(2,1)S(1)}, bf16[128,384]{1,0:T(8,128)(2,1)}, u32[]{:S(2)}) copy-start(bf16[128,384]{1,0:T(8,128)(2,1)} %get-tuple-element.30.k_fresh) | copy-start | bytes 294916
  34.2 10.8 %collective-permute-start.4 = (bf16[2,2,128,384]{3,2,1,0:T(8,128)(2,1)S(1)}, bf16[2,2,128,384]{3,2,1,0:T(8,128)(2,1)S(1)}, u32[]{:S(2)}, u32[]{:S(2)}) collective-permute-start(bf16[2,2,128,384]{3,2,1,0:T(8,128)(2,1)S(1)} %stack.1.refs_0_), channel_id=1, source_target_pairs={{0,408},{1,137},{2,410},{3,139},{4,412},{5,141},{6,414},{7,143},{8... | collective-permute-start | bytes 1179656 | tf_op jit(solution)/shard_map/ppermute | solution.py:36
  37.6 11.6 %collective-permute-start.3 = (bf16[2,2,128,384]{3,2,1,0:T(8,128)(2,1)S(1)}, bf16[2,2,128,384]{3,2,1,0:T(8,128)(2,1)S(1)}, u32[]{:S(2)}, u32[]{:S(2)}) collective-permute-start(bf16[2,2,128,384]{3,2,1,0:T(8,128)(2,1)S(1)} %stack.1.refs_0_), channel_id=1, source_target_pairs={{0,384},{1,129},{2,386},{3,131},{4,388},{5,133},{6,390},{7,135},{8... | collective-permute-start | bytes 1179656 | tf_op jit(solution)/shard_map/ppermute | solution.py:36
  40.6 9.7 %collective-permute-start.2 = (bf16[2,2,128,384]{3,2,1,0:T(8,128)(2,1)S(1)}, bf16[2,2,128,384]{3,2,1,0:T(8,128)(2,1)S(1)}, u32[]{:S(2)}, u32[]{:S(2)}) collective-permute-start(bf16[2,2,128,384]{3,2,1,0:T(8,128)(2,1)S(1)} %stack.1.refs_0_), channel_id=1, source_target_pairs={{0,24},{1,9},{2,26},{3,11},{4,28},{5,13},{6,30},{7,15},{8,16},{9,1... | collective-permute-start | bytes 1179656 | tf_op jit(solution)/shard_map/ppermute | solution.py:36
  51.1 1.0 copy-start.11
  56.6 32.2 %copy-start = (bf16[384,3072]{1,0:T(8,128)(2,1)S(1)}, bf16[384,3072]{1,0:T(8,128)(2,1)}, u32[]{:S(2)}) copy-start(bf16[384,3072]{1,0:T(8,128)(2,1)} %w.1) | copy-start | bytes 7077892
  56.6 12.4 %collective-permute-start.5 = (bf16[2,144,384]{2,1,0:T(8,128)(2,1)S(1)}, bf16[2,144,384]{2,1,0:T(8,128)(2,1)S(1)}, u32[]{:S(2)}, u32[]{:S(2)}) collective-permute-start(bf16[2,144,384]{2,1,0:T(8,128)(2,1)S(1)} %get-tuple-element.27), channel_id=1, source_target_pairs={{0,8},{1,25},{2,10},{3,27},{4,12},{5,29},{6,14},{7,31},{8,0},{9,17... | collective-permute-start | bytes 663560 | tf_op jit(solution)/shard_map/ppermute | solution.py:36
  62.4 8.5 %collective-permute-start.6 = (bf16[2,144,384]{2,1,0:T(8,128)(2,1)S(1)}, bf16[2,144,384]{2,1,0:T(8,128)(2,1)S(1)}, u32[]{:S(2)}, u32[]{:S(2)}) collective-permute-start(bf16[2,144,384]{2,1,0:T(8,128)(2,1)S(1)} %get-tuple-element.28), channel_id=1, source_target_pairs={{0,128},{1,385},{2,130},{3,387},{4,132},{5,389},{6,134},{7,391},{8... | collective-permute-start | bytes 663560 | tf_op jit(solution)/shard_map/ppermute | solution.py:36
  67.0 8.7 %collective-permute-start.7 = (bf16[2,144,384]{2,1,0:T(8,128)(2,1)S(1)}, bf16[2,144,384]{2,1,0:T(8,128)(2,1)S(1)}, u32[]{:S(2)}, u32[]{:S(2)}) collective-permute-start(bf16[2,144,384]{2,1,0:T(8,128)(2,1)S(1)} %get-tuple-element.29), channel_id=1, source_target_pairs={{0,136},{1,409},{2,138},{3,411},{4,140},{5,413},{6,142},{7,415},{8... | collective-permute-start | bytes 663560 | tf_op jit(solution)/shard_map/ppermute | solution.py:36
  76.2 12.6 %collective-permute-start.8 = (bf16[144,384]{1,0:T(8,128)(2,1)S(1)}, bf16[144,384]{1,0:T(8,128)(2,1)S(1)}, u32[]{:S(2)}, u32[]{:S(2)}) collective-permute-start(bf16[144,384]{1,0:T(8,128)(2,1)S(1)} %merge.1), channel_id=1, source_target_pairs={{0,96},{1,33},{2,98},{3,35},{4,100},{5,37},{6,102},{7,39},{8,104},... | collective-permute-start | bytes 331784 | tf_op jit(solution)/shard_map/ppermute | solution.py:36
  85.2 24.4 %copy-start.6 = (bf16[128,384]{1,0:T(8,128)(2,1)S(1)}, bf16[128,384]{1,0:T(8,128)(2,1)}, u32[]{:S(2)}) copy-start(bf16[128,384]{1,0:T(8,128)(2,1)} %hidden.1) | copy-start | bytes 294916
  85.2 24.4 %copy-start.7 = (bf16[128,384]{1,0:T(8,128)(2,1)S(1)}, bf16[128,384]{1,0:T(8,128)(2,1)}, u32[]{:S(2)}) copy-start(bf16[128,384]{1,0:T(8,128)(2,1)} %control.1) | copy-start | bytes 294916
  85.2 24.4 %copy-start.9 = (f32[28,384]{1,0:T(8,128)S(1)}, f32[28,384]{1,0:T(8,128)}, u32[]{:S(2)}) copy-start(f32[28,384]{1,0:T(8,128)} %gate.1) | copy-start | bytes 129028
  90.1 3.6 %collective-permute-start.9 = (bf16[4,128,384]{2,1,0:T(8,128)(2,1)S(1)}, bf16[4,128,384]{2,1,0:T(8,128)(2,1)S(1)}, u32[]{:S(2)}, u32[]{:S(2)}) collective-permute-start(bf16[4,128,384]{2,1,0:T(8,128)(2,1)S(1)} %get-tuple-element.32), channel_id=1, source_target_pairs={{0,1},{1,0},{2,3},{3,2},{4,5},{5,4},{6,7},{7,6},{8,9},{9,8},{10,11... | collective-permute-start | bytes 1179656 | tf_op jit(solution)/shard_map/ppermute | solution.py:36
  93.8 10.8 %collective-permute-start.10 = (bf16[128,384]{1,0:T(8,128)(2,1)S(1)}, bf16[128,384]{1,0:T(8,128)(2,1)S(1)}, u32[]{:S(2)}, u32[]{:S(2)}) collective-permute-start(bf16[128,384]{1,0:T(8,128)(2,1)S(1)} %get-tuple-element.34), channel_id=1, source_target_pairs={{0,2},{1,3},{2,0},{3,1},{4,6},{5,7},{6,4},{7,5},{8,10},{9,11},{10,... | collective-permute-start | bytes 294920 | tf_op jit(solution)/shard_map/ppermute | solution.py:36
  95.8 11.0 %collective-permute-start.11 = (bf16[128,384]{1,0:T(8,128)(2,1)S(1)}, bf16[128,384]{1,0:T(8,128)(2,1)S(1)}, u32[]{:S(2)}, u32[]{:S(2)}) collective-permute-start(bf16[128,384]{1,0:T(8,128)(2,1)S(1)} %get-tuple-element.35), channel_id=1, source_target_pairs={{0,4},{1,5},{2,6},{3,7},{4,0},{5,1},{6,2},{7,3},{8,12},{9,13},{10,... | collective-permute-start | bytes 294920 | tf_op jit(solution)/shard_map/ppermute | solution.py:36
  101.2 8.4 %collective-permute-start.12 = (bf16[128,384]{1,0:T(8,128)(2,1)S(1)}, bf16[128,384]{1,0:T(8,128)(2,1)S(1)}, u32[]{:S(2)}, u32[]{:S(2)}) collective-permute-start(bf16[128,384]{1,0:T(8,128)(2,1)S(1)} %get-tuple-element.36), channel_id=1, source_target_pairs={{0,6},{1,7},{2,4},{3,5},{4,2},{5,3},{6,0},{7,1},{8,14},{9,15},{10,... | collective-permute-start | bytes 294920 | tf_op jit(solution)/shard_map/ppermute | solution.py:36
  (2 other events, 1.7 us)

commit v6 on v3

--- a/solution.py
+++ b/solution.py
@@ -278,15 +278,9 @@
             lse.append(y)
         put(out.at[place, half], o, lse)
 
-    one(at, 0, TOK)
-    one(at, 1, 0)
-
-    def step(i, carry):
-        one(at ^ i, 0, 0)
-        one(at ^ i, 1, 0)
-        return carry
-
-    lax.fori_loop(1, 4, step, 0)
+    for d in range(4):
+        one(at ^ d, 0, 0 if d else TOK)
+        one(at ^ d, 1, 0)
 
 
 def attention(kv, q):
@@ -402,42 +396,41 @@
     )(mine, theirs, home, out_weight)
 
 
-def halve_kernel(keep, got, stay, send):
-    n = stay.shape[0]
-    for i in range(n):
-        stay[i] = keep[2 * i] + got[2 * i].astype(F32)
-        send[i] = (keep[2 * i + 1] + got[2 * i + 1].astype(F32)).astype(BF16)
-
-
-def halve(keep, got):
-    full = pl.BlockSpec(memory_space=pltpu.VMEM)
-    shape = (keep.shape[0] // 2, TOK, WIDTH)
-    return pl.pallas_call(
-        halve_kernel,
-        out_shape=(jax.ShapeDtypeStruct(shape, F32), jax.ShapeDtypeStruct(shape, BF16)),
+def core_kernel(keep, got, own, *outs):
+    own[...] = keep[0] + got[0].astype(F32)
+    for d in range(1, 4):
+        outs[d - 1][...] = (keep[d] + got[d].astype(F32)).astype(BF16)
+
+
+def core_sum(keep, got):
+    full = pl.BlockSpec(memory_space=pltpu.VMEM)
+    return pl.pallas_call(
+        core_kernel,
+        out_shape=(jax.ShapeDtypeStruct((TOK, WIDTH), F32),)
+        + (jax.ShapeDtypeStruct((TOK, WIDTH), BF16),) * 3,
         in_specs=[full] * 2,
-        out_specs=(full, full),
-        compiler_params=pltpu.CompilerParams(vmem_limit_bytes=16 * MIB),
-        name="halve",
+        out_specs=(full,) * 4,
+        compiler_params=pltpu.CompilerParams(vmem_limit_bytes=16 * MIB),
+        name="core_sum",
     )(keep, got)
 
 
-def final_kernel(step, own, got, gate, hidden, control, out):
-    total = own[0] + got[0].astype(F32)
+def final_kernel(step, own, a, b, c, gate, hidden, control, out):
+    total = own[...] + a[...].astype(F32) + b[...].astype(F32) + c[...].astype(F32)
     row = gate[pl.ds(step[0], 1), :]
     out[...] = (hidden[...].astype(F32) + row * total + control[...].astype(F32)).astype(BF16)
 
 
-def finish(timestep, own, got, gate_table, hidden_in, control):
+def finish(timestep, *args):
     full = pl.BlockSpec(memory_space=pltpu.VMEM)
     return pl.pallas_call(
         final_kernel,
         out_shape=jax.ShapeDtypeStruct((TOK, WIDTH), BF16),
-        in_specs=[pl.BlockSpec(memory_space=pltpu.SMEM)] + [full] * 5,
+        in_specs=[pl.BlockSpec(memory_space=pltpu.SMEM)] + [full] * 7,
         out_specs=full,
         compiler_params=pltpu.CompilerParams(vmem_limit_bytes=16 * MIB),
         name="finish",
-    )(timestep, own, got, gate_table, hidden_in, control)
+    )(timestep, *args)
 
 
 def body(
@@ -464,9 +457,9 @@
     mine = exchange(attention(kv, q_all), AXES, QUERY_GROUPS)
     theirs = query_pair(merge_first(mine))
     keep, give = project(mine, theirs, home, out_weight)
-    keep, give = halve(keep, swap_core(give))
-    keep, give = halve(keep, swap_z(give, 1))
-    return finish(timestep, keep, swap_z(give, 2), gate_table, hidden_in, control)
+    own, *parts = core_sum(keep, swap_core(give))
+    parts = [swap_z(p, d + 1) for d, p in enumerate(parts)]
+    return finish(timestep, own, *parts, gate_table, hidden_in, control)
 
 
 def solution(mesh):

time: 110 us -> 106 us (0.964)
  waiting for transfers between devices: 32 us -> 24.4 us
  starting transfers between devices: 47.3 us -> 51.3 us
  Pallas kernels: 12.9 us -> 11.6 us
    ppermute x9 -> x10, waiting for transfers between devices: 31.9 us -> 24.4 us  [permute(): return lax.ppermute(value, AXES, pairs)]
    ppermute x9 -> x10, starting transfers between devices: 41.1 us -> 45.1 us  [permute(): return lax.ppermute(value, AXES, pairs)]
    pallas_call x1, Pallas kernels: 5.96 us -> 4.63 us  [attention(): pl.pallas_call(attn_kernel, out_shape=jax.ShapeDtypeStruct((4, 2, TOK + S...]
  transfers between devices with their start and end apart: 10 -> 11, of which waited for: 7 -> 7; matrix products, arithmetic and copies ran while one was open for 0% -> 0% of each run, Pallas kernels for 2% -> 2%
where the time goes in v6:
time: 106 us; the launch traced here: 105 us
  starting transfers between devices  51.3 us (48%)
  waiting for transfers between devices  24.4 us (23%)
  blocking collectives  15.9 us (15%)
  Pallas kernels  11.6 us (11%)
    ppermute x10, starting transfers between devices, permute(): return lax.ppermute(value, AXES, pairs)  45.1 us
    ppermute x10, waiting for transfers between devices, permute(): return lax.ppermute(value, AXES, pairs)  24.4 us
    all_to_all x1, blocking collectives, exchange(): lax.all_to_all(value, axes, 0, 0, axis_index_groups=groups, tiled=True)  15.9 us
    all_to_all x1, starting transfers between devices, exchange(): lax.all_to_all(value, axes, 0, 0, axis_index_groups=groups, tiled=True)  6.2 us
    pallas_call x1, Pallas kernels, attention(): pl.pallas_call(attn_kernel, out_shape=jax.ShapeDtypeStruct((4, 2, TOK + S...  4.63 us
    pallas_call x1, Pallas kernels, prepare(): pl.pallas_call(prep_kernel, out_shape=(jax.ShapeDtypeStruct((TOK, WIDTH),...  2.57 us
  transfers between devices with their start and end apart: 11, of which 7 were waited for; matrix products, arithmetic and copies ran while one was open for 0% of the time, Pallas kernels for 2%

profile of v6, /device:TPU:1, one launch (start us, length us, event | category | flops | bytes accessed | tf_op | source)
XLA Modules:
  0.0 104.9 jit_solution(10528728586582062186)
XLA Ops:
  0.0 2.6 %prep.1 = (bf16[128,384]{1,0:T(8,128)(2,1)}, bf16[128,384]{1,0:T(8,128)(2,1)}) custom-call(bf16[3,128,384]{2,1,0:T(8,128)(2,1)} %raw.1, s32[1,128]{1,0:T(1,128)} %bitcast.3, f32[8,128]{1,0:T(8,128)} %constant.2.clone.freq_hbm, f32[1,128]{1,0:T(1,128)} %bitcast.4, f32[1,128]{1,0:T(1,128)} %bitcast.5), custom_call_target="tpu_custom_call" | custom-call | tf_op jit(solution)/shard_map/prep/pallas_call | solution.py:163
  2.6 13.3 %collective-permute-start.1 = (bf16[2,128,384]{2,1,0:T(8,128)(2,1)}, bf16[2,128,384]{2,1,0:T(8,128)(2,1)S(1)}, u32[]{:S(2)}, u32[]{:S(2)}) collective-permute-start(bf16[2,128,384]{2,1,0:T(8,128)(2,1)} %a), channel_id=1, source_target_pairs={{0,32},{1,97},{2,34},{3,99},{4,36},{5,101},{6,38},{7,103},{8,40},{... | collective-permute-start | bytes 589832 | tf_op jit(solution)/shard_map/ppermute | solution.py:36
  15.9 5.2 %collective-permute-start = (bf16[128,384]{1,0:T(8,128)(2,1)}, bf16[128,384]{1,0:T(8,128)(2,1)S(1)}, u32[]{:S(2)}, u32[]{:S(2)}) collective-permute-start(bf16[128,384]{1,0:T(8,128)(2,1)} %get-tuple-element.19.refs_0_.q), channel_id=1, source_target_pairs={{0,96},{1,33},{2,98},{3,35},{4,100},{5,37},{6,102},{7,39},{8,104},... | collective-permute-start | bytes 294920 | tf_op jit(solution)/shard_map/ppermute | solution.py:36
  21.1 6.3 %collective-permute-done.refs_1_ = bf16[128,384]{1,0:T(8,128)(2,1)S(1)} collective-permute-done((bf16[128,384]{1,0:T(8,128)(2,1)}, bf16[128,384]{1,0:T(8,128)(2,1)S(1)}, u32[]{:S(2)}, u32[]{:S(2)}) %collective-permute-start) | collective-permute-done | bytes 98336 | tf_op jit(solution)/shard_map/ppermute | solution.py:36
  27.4 0.9 copy-done.3
  28.3 0.9 spread.1
  29.2 6.2 %all-to-all-start = ((bf16[4,2,128,384]{3,2,1,0:T(8,128)(2,1)}), bf16[4,2,128,384]{3,2,1,0:T(8,128)(2,1)S(1)}, u32[]{:S(2)}, u32[]{:S(2)}) async-start(bf16[4,2,128,384]{3,2,1,0:T(8,128)(2,1)} %spread.1), calls=%async_computation | async-start | bytes 1572864 | tf_op jit(solution)/shard_map/all_to_all | solution.py:54
  35.5 1.9 %collective-permute-start.4 = (bf16[2,2,128,384]{3,2,1,0:T(8,128)(2,1)S(1)}, bf16[2,2,128,384]{3,2,1,0:T(8,128)(2,1)S(1)}, u32[]{:S(2)}, u32[]{:S(2)}) collective-permute-start(bf16[2,2,128,384]{3,2,1,0:T(8,128)(2,1)S(1)} %stack.1.a), channel_id=1, source_target_pairs={{0,408},{1,137},{2,410},{3,139},{4,412},{5,141},{6,414},{7,143},{8... | collective-permute-start | bytes 1179656 | tf_op jit(solution)/shard_map/ppermute | solution.py:36
  37.4 3.0 %collective-permute-start.3 = (bf16[2,2,128,384]{3,2,1,0:T(8,128)(2,1)S(1)}, bf16[2,2,128,384]{3,2,1,0:T(8,128)(2,1)S(1)}, u32[]{:S(2)}, u32[]{:S(2)}) collective-permute-start(bf16[2,2,128,384]{3,2,1,0:T(8,128)(2,1)S(1)} %stack.1.a), channel_id=1, source_target_pairs={{0,384},{1,129},{2,386},{3,131},{4,388},{5,133},{6,390},{7,135},{8... | collective-permute-start | bytes 1179656 | tf_op jit(solution)/shard_map/ppermute | solution.py:36
  40.4 3.4 %collective-permute-start.2 = (bf16[2,2,128,384]{3,2,1,0:T(8,128)(2,1)S(1)}, bf16[2,2,128,384]{3,2,1,0:T(8,128)(2,1)S(1)}, u32[]{:S(2)}, u32[]{:S(2)}) collective-permute-start(bf16[2,2,128,384]{3,2,1,0:T(8,128)(2,1)S(1)} %stack.1.a), channel_id=1, source_target_pairs={{0,24},{1,9},{2,26},{3,11},{4,28},{5,13},{6,30},{7,15},{8,16},{9,1... | collective-permute-start | bytes 1179656 | tf_op jit(solution)/shard_map/ppermute | solution.py:36
  43.9 4.2 %collective-permute-done.4.d = bf16[2,2,128,384]{3,2,1,0:T(8,128)(2,1)S(1)} collective-permute-done((bf16[2,2,128,384]{3,2,1,0:T(8,128)(2,1)S(1)}, bf16[2,2,128,384]{3,2,1,0:T(8,128)(2,1)S(1)}, u32[]{:S(2)}, u32[]{:S(2)}) %collective-permute-start.4) | collective-permute-done | bytes 393248 | tf_op jit(solution)/shard_map/ppermute | solution.py:36
  48.1 3.3 %collective-permute-done.3.c = bf16[2,2,128,384]{3,2,1,0:T(8,128)(2,1)S(1)} collective-permute-done((bf16[2,2,128,384]{3,2,1,0:T(8,128)(2,1)S(1)}, bf16[2,2,128,384]{3,2,1,0:T(8,128)(2,1)S(1)}, u32[]{:S(2)}, u32[]{:S(2)}) %collective-permute-start.3) | collective-permute-done | bytes 393248 | tf_op jit(solution)/shard_map/ppermute | solution.py:36
  51.4 4.6 %attend.1 = bf16[4,2,144,384]{3,2,1,0:T(8,128)(2,1)S(1)} custom-call(bf16[2,2,128,384]{3,2,1,0:T(8,128)(2,1)S(1)} %stack.1.a, bf16[2,2,128,384]{3,2,1,0:T(8,128)(2,1)S(1)} %collective-permute-done.2.b, bf16[2,2,128,384]{3,2,1,0:T(8,128)(2,1)S(1)} %collective-permute-done.3.c, bf16[2,2,128,384]{3,2,1,0:T(8,128)(2,1)S(1)} %collective-permute-done.4.d, ...), custom_call_target="tpu_custom_call" | custom-call | flops 1610612736 | bytes 4194304 | tf_op jit(solution)/shard_map/attend/pallas_call | solution.py:288
  56.1 15.9 %all_to_all.10.got.mine = bf16[4,2,144,384]{3,2,1,0:T(8,128)(2,1)S(1)} all-to-all(bf16[4,2,144,384]{3,2,1,0:T(8,128)(2,1)S(1)} %attend.1), channel_id=1, replica_groups={{0,8,128,136},{1,25,385,409},{2,10,130,138},{3,27,387,411},{4,12,132,14..., dimensions={0} | all-to-all | bytes 1769472 | tf_op jit(solution)/shard_map/all_to_all | solution.py:54
  72.4 5.4 %collective-permute-start.5 = (bf16[144,384]{1,0:T(8,128)(2,1)S(1)}, bf16[144,384]{1,0:T(8,128)(2,1)S(1)}, u32[]{:S(2)}, u32[]{:S(2)}) collective-permute-start(bf16[144,384]{1,0:T(8,128)(2,1)S(1)} %merge.1), channel_id=1, source_target_pairs={{0,96},{1,33},{2,98},{3,35},{4,100},{5,37},{6,102},{7,39},{8,104},... | collective-permute-start | bytes 331784 | tf_op jit(solution)/shard_map/ppermute | solution.py:36
  78.7 5.5 %collective-permute-done.5.theirs = bf16[144,384]{1,0:T(8,128)(2,1)S(1)} collective-permute-done((bf16[144,384]{1,0:T(8,128)(2,1)S(1)}, bf16[144,384]{1,0:T(8,128)(2,1)S(1)}, u32[]{:S(2)}, u32[]{:S(2)}) %collective-permute-start.5) | collective-permute-done | bytes 110624 | tf_op jit(solution)/shard_map/ppermute | solution.py:36
  84.2 1.3 %project.1 = (f32[4,128,384]{2,1,0:T(8,128)S(1)}, bf16[4,128,384]{2,1,0:T(8,128)(2,1)S(1)}) custom-call(bf16[4,2,144,384]{3,2,1,0:T(8,128)(2,1)S(1)} %all_to_all.10.got.mine, bf16[144,384]{1,0:T(8,128)(2,1)S(1)} %collective-permute-done.5.theirs, bf16[144,384]{1,0:T(8,128)(2,1)S(1)} %attend_home.1.home, bf16[384,3072]{1,0:T(8,128)(2,1)S(1)} %copy-done), custom_call_target="tpu_custom_call" | custom-call | tf_op jit(solution)/shard_map/project/pallas_call | solution.py:385
  85.6 3.6 %collective-permute-start.6 = (bf16[4,128,384]{2,1,0:T(8,128)(2,1)S(1)}, bf16[4,128,384]{2,1,0:T(8,128)(2,1)S(1)}, u32[]{:S(2)}, u32[]{:S(2)}) collective-permute-start(bf16[4,128,384]{2,1,0:T(8,128)(2,1)S(1)} %get-tuple-element.24), channel_id=1, source_target_pairs={{0,1},{1,0},{2,3},{3,2},{4,5},{5,4},{6,7},{7,6},{8,9},{9,8},{10,11... | collective-permute-start | bytes 1179656 | tf_op jit(solution)/shard_map/ppermute | solution.py:36
  89.2 1.3 %collective-permute-done.6.got = bf16[4,128,384]{2,1,0:T(8,128)(2,1)S(1)} collective-permute-done((bf16[4,128,384]{2,1,0:T(8,128)(2,1)S(1)}, bf16[4,128,384]{2,1,0:T(8,128)(2,1)S(1)}, u32[]{:S(2)}, u32[]{:S(2)}) %collective-permute-start.6) | collective-permute-done | bytes 393248 | tf_op jit(solution)/shard_map/ppermute | solution.py:36
  90.6 1.9 %collective-permute-start.7 = (bf16[128,384]{1,0:T(8,128)(2,1)S(1)}, bf16[128,384]{1,0:T(8,128)(2,1)S(1)}, u32[]{:S(2)}, u32[]{:S(2)}) collective-permute-start(bf16[128,384]{1,0:T(8,128)(2,1)S(1)} %get-tuple-element.26), channel_id=1, source_target_pairs={{0,2},{1,3},{2,0},{3,1},{4,6},{5,7},{6,4},{7,5},{8,10},{9,11},{10,... | collective-permute-start | bytes 294920 | tf_op jit(solution)/shard_map/ppermute | solution.py:36
  92.5 4.4 %collective-permute-start.8 = (bf16[128,384]{1,0:T(8,128)(2,1)S(1)}, bf16[128,384]{1,0:T(8,128)(2,1)S(1)}, u32[]{:S(2)}, u32[]{:S(2)}) collective-permute-start(bf16[128,384]{1,0:T(8,128)(2,1)S(1)} %get-tuple-element.27), channel_id=1, source_target_pairs={{0,4},{1,5},{2,6},{3,7},{4,0},{5,1},{6,2},{7,3},{8,12},{9,13},{10,... | collective-permute-start | bytes 294920 | tf_op jit(solution)/shard_map/ppermute | solution.py:36
  96.9 2.9 %collective-permute-start.9 = (bf16[128,384]{1,0:T(8,128)(2,1)S(1)}, bf16[128,384]{1,0:T(8,128)(2,1)S(1)}, u32[]{:S(2)}, u32[]{:S(2)}) collective-permute-start(bf16[128,384]{1,0:T(8,128)(2,1)S(1)} %get-tuple-element.28), channel_id=1, source_target_pairs={{0,6},{1,7},{2,4},{3,5},{4,2},{5,3},{6,0},{7,1},{8,14},{9,15},{10,... | collective-permute-start | bytes 294920 | tf_op jit(solution)/shard_map/ppermute | solution.py:36
  100.5 1.0 collective-permute-done.8.b
  101.6 2.6 %collective-permute-done.9.c = bf16[128,384]{1,0:T(8,128)(2,1)S(1)} collective-permute-done((bf16[128,384]{1,0:T(8,128)(2,1)S(1)}, bf16[128,384]{1,0:T(8,128)(2,1)S(1)}, u32[]{:S(2)}, u32[]{:S(2)}) %collective-permute-start.9) | collective-permute-done | bytes 98336 | tf_op jit(solution)/shard_map/ppermute | solution.py:36
  (28 shorter events, 2.2 us)
Async XLA Ops:
  0.0 35.4 %copy-start.5 = (bf16[2,128,384]{2,1,0:T(8,128)(2,1)S(1)}, bf16[2,128,384]{2,1,0:T(8,128)(2,1)}, u32[]{:S(2)}) copy-start(bf16[2,128,384]{2,1,0:T(8,128)(2,1)} %a) | copy-start | bytes 589828
  2.6 26.7 %collective-permute-start.1 = (bf16[2,128,384]{2,1,0:T(8,128)(2,1)}, bf16[2,128,384]{2,1,0:T(8,128)(2,1)S(1)}, u32[]{:S(2)}, u32[]{:S(2)}) collective-permute-start(bf16[2,128,384]{2,1,0:T(8,128)(2,1)} %a), channel_id=1, source_target_pairs={{0,32},{1,97},{2,34},{3,99},{4,36},{5,101},{6,38},{7,103},{8,40},{... | collective-permute-start | bytes 589832 | tf_op jit(solution)/shard_map/ppermute | solution.py:36
  15.9 11.5 %collective-permute-start = (bf16[128,384]{1,0:T(8,128)(2,1)}, bf16[128,384]{1,0:T(8,128)(2,1)S(1)}, u32[]{:S(2)}, u32[]{:S(2)}) collective-permute-start(bf16[128,384]{1,0:T(8,128)(2,1)} %get-tuple-element.19.refs_0_.q), channel_id=1, source_target_pairs={{0,96},{1,33},{2,98},{3,35},{4,100},{5,37},{6,102},{7,39},{8,104},... | collective-permute-start | bytes 294920 | tf_op jit(solution)/shard_map/ppermute | solution.py:36
  27.4 0.9 copy-start.3
  29.2 22.2 %all-to-all-start = ((bf16[4,2,128,384]{3,2,1,0:T(8,128)(2,1)}), bf16[4,2,128,384]{3,2,1,0:T(8,128)(2,1)S(1)}, u32[]{:S(2)}, u32[]{:S(2)}) async-start(bf16[4,2,128,384]{3,2,1,0:T(8,128)(2,1)} %spread.1), calls=%async_computation | async-start | bytes 1572864 | tf_op jit(solution)/shard_map/all_to_all | solution.py:54
  35.5 12.6 %collective-permute-start.4 = (bf16[2,2,128,384]{3,2,1,0:T(8,128)(2,1)S(1)}, bf16[2,2,128,384]{3,2,1,0:T(8,128)(2,1)S(1)}, u32[]{:S(2)}, u32[]{:S(2)}) collective-permute-start(bf16[2,2,128,384]{3,2,1,0:T(8,128)(2,1)S(1)} %stack.1.a), channel_id=1, source_target_pairs={{0,408},{1,137},{2,410},{3,139},{4,412},{5,141},{6,414},{7,143},{8... | collective-permute-start | bytes 1179656 | tf_op jit(solution)/shard_map/ppermute | solution.py:36
  37.4 14.0 %collective-permute-start.3 = (bf16[2,2,128,384]{3,2,1,0:T(8,128)(2,1)S(1)}, bf16[2,2,128,384]{3,2,1,0:T(8,128)(2,1)S(1)}, u32[]{:S(2)}, u32[]{:S(2)}) collective-permute-start(bf16[2,2,128,384]{3,2,1,0:T(8,128)(2,1)S(1)} %stack.1.a), channel_id=1, source_target_pairs={{0,384},{1,129},{2,386},{3,131},{4,388},{5,133},{6,390},{7,135},{8... | collective-permute-start | bytes 1179656 | tf_op jit(solution)/shard_map/ppermute | solution.py:36
  40.4 11.0 %collective-permute-start.2 = (bf16[2,2,128,384]{3,2,1,0:T(8,128)(2,1)S(1)}, bf16[2,2,128,384]{3,2,1,0:T(8,128)(2,1)S(1)}, u32[]{:S(2)}, u32[]{:S(2)}) collective-permute-start(bf16[2,2,128,384]{3,2,1,0:T(8,128)(2,1)S(1)} %stack.1.a), channel_id=1, source_target_pairs={{0,24},{1,9},{2,26},{3,11},{4,28},{5,13},{6,30},{7,15},{8,16},{9,1... | collective-permute-start | bytes 1179656 | tf_op jit(solution)/shard_map/ppermute | solution.py:36
  51.4 26.4 %copy-start.2 = (bf16[2,512,384]{2,1,0:T(8,128)(2,1)S(1)}, bf16[2,512,384]{2,1,0:T(8,128)(2,1)}, u32[]{:S(2)}) copy-start(bf16[2,512,384]{2,1,0:T(8,128)(2,1)} %text.1) | copy-start | bytes 2359300
  51.4 26.4 %copy-start.8 = (bf16[128,384]{1,0:T(8,128)(2,1)S(1)}, bf16[128,384]{1,0:T(8,128)(2,1)}, u32[]{:S(2)}) copy-start(bf16[128,384]{1,0:T(8,128)(2,1)} %get-tuple-element.22.k_fresh) | copy-start | bytes 294916
  56.1 21.8 %copy-start.1 = (bf16[3,128,384]{2,1,0:T(8,128)(2,1)S(1)}, bf16[3,128,384]{2,1,0:T(8,128)(2,1)}, u32[]{:S(2)}) copy-start(bf16[3,128,384]{2,1,0:T(8,128)(2,1)} %raw.1) | copy-start | bytes 884740
  56.1 21.8 %copy-start.4 = (bf16[128,384]{1,0:T(8,128)(2,1)S(1)}, bf16[128,384]{1,0:T(8,128)(2,1)}, u32[]{:S(2)}) copy-start(bf16[128,384]{1,0:T(8,128)(2,1)} %get-tuple-element.19.refs_0_.q) | copy-start | bytes 294916
  56.1 28.2 %copy-start = (bf16[384,3072]{1,0:T(8,128)(2,1)S(1)}, bf16[384,3072]{1,0:T(8,128)(2,1)}, u32[]{:S(2)}) copy-start(bf16[384,3072]{1,0:T(8,128)(2,1)} %w.1) | copy-start | bytes 7077892
  72.4 11.8 %collective-permute-start.5 = (bf16[144,384]{1,0:T(8,128)(2,1)S(1)}, bf16[144,384]{1,0:T(8,128)(2,1)S(1)}, u32[]{:S(2)}, u32[]{:S(2)}) collective-permute-start(bf16[144,384]{1,0:T(8,128)(2,1)S(1)} %merge.1), channel_id=1, source_target_pairs={{0,96},{1,33},{2,98},{3,35},{4,100},{5,37},{6,102},{7,39},{8,104},... | collective-permute-start | bytes 331784 | tf_op jit(solution)/shard_map/ppermute | solution.py:36
  78.7 25.5 %copy-start.6 = (bf16[128,384]{1,0:T(8,128)(2,1)S(1)}, bf16[128,384]{1,0:T(8,128)(2,1)}, u32[]{:S(2)}) copy-start(bf16[128,384]{1,0:T(8,128)(2,1)} %hidden.1) | copy-start | bytes 294916
  78.7 25.5 %copy-start.7 = (bf16[128,384]{1,0:T(8,128)(2,1)S(1)}, bf16[128,384]{1,0:T(8,128)(2,1)}, u32[]{:S(2)}) copy-start(bf16[128,384]{1,0:T(8,128)(2,1)} %control.1) | copy-start | bytes 294916
  78.7 25.5 %copy-start.9 = (f32[28,384]{1,0:T(8,128)S(1)}, f32[28,384]{1,0:T(8,128)}, u32[]{:S(2)}) copy-start(f32[28,384]{1,0:T(8,128)} %gate.1) | copy-start | bytes 129028
  85.6 4.9 %collective-permute-start.6 = (bf16[4,128,384]{2,1,0:T(8,128)(2,1)S(1)}, bf16[4,128,384]{2,1,0:T(8,128)(2,1)S(1)}, u32[]{:S(2)}, u32[]{:S(2)}) collective-permute-start(bf16[4,128,384]{2,1,0:T(8,128)(2,1)S(1)} %get-tuple-element.24), channel_id=1, source_target_pairs={{0,1},{1,0},{2,3},{3,2},{4,5},{5,4},{6,7},{7,6},{8,9},{9,8},{10,11... | collective-permute-start | bytes 1179656 | tf_op jit(solution)/shard_map/ppermute | solution.py:36
  90.6 9.9 %collective-permute-start.7 = (bf16[128,384]{1,0:T(8,128)(2,1)S(1)}, bf16[128,384]{1,0:T(8,128)(2,1)S(1)}, u32[]{:S(2)}, u32[]{:S(2)}) collective-permute-start(bf16[128,384]{1,0:T(8,128)(2,1)S(1)} %get-tuple-element.26), channel_id=1, source_target_pairs={{0,2},{1,3},{2,0},{3,1},{4,6},{5,7},{6,4},{7,5},{8,10},{9,11},{10,... | collective-permute-start | bytes 294920 | tf_op jit(solution)/shard_map/ppermute | solution.py:36
  92.5 9.1 %collective-permute-start.8 = (bf16[128,384]{1,0:T(8,128)(2,1)S(1)}, bf16[128,384]{1,0:T(8,128)(2,1)S(1)}, u32[]{:S(2)}, u32[]{:S(2)}) collective-permute-start(bf16[128,384]{1,0:T(8,128)(2,1)S(1)} %get-tuple-element.27), channel_id=1, source_target_pairs={{0,4},{1,5},{2,6},{3,7},{4,0},{5,1},{6,2},{7,3},{8,12},{9,13},{10,... | collective-permute-start | bytes 294920 | tf_op jit(solution)/shard_map/ppermute | solution.py:36
  96.9 7.3 %collective-permute-start.9 = (bf16[128,384]{1,0:T(8,128)(2,1)S(1)}, bf16[128,384]{1,0:T(8,128)(2,1)S(1)}, u32[]{:S(2)}, u32[]{:S(2)}) collective-permute-start(bf16[128,384]{1,0:T(8,128)(2,1)S(1)} %get-tuple-element.28), channel_id=1, source_target_pairs={{0,6},{1,7},{2,4},{3,5},{4,2},{5,3},{6,0},{7,1},{8,14},{9,15},{10,... | collective-permute-start | bytes 294920 | tf_op jit(solution)/shard_map/ppermute | solution.py:36

commit v7 on v6

--- a/solution.py
+++ b/solution.py
@@ -76,6 +76,23 @@
     for i in range(4):
         for j, ref in enumerate(refs[:-1]):
             out[i, j] = ref[...]
+
+
+def hold_kernel(ref, out):
+    out[...] = ref[...]
+
+
+def hold(value):
+    full = pl.BlockSpec(memory_space=pltpu.VMEM)
+    return pl.pallas_call(
+        hold_kernel,
+        out_shape=jax.ShapeDtypeStruct(value.shape, value.dtype),
+        in_specs=[full],
+        out_specs=full,
+        compiler_params=pltpu.CompilerParams(vmem_limit_bytes=16 * MIB),
+        cost_estimate=pl.CostEstimate(flops=2**30, bytes_accessed=MIB, transcendentals=0),
+        name="hold",
+    )(value)
 
 
 def spread(*values):
@@ -364,7 +381,11 @@
     )(messages)
 
 
-def project_kernel(mine, theirs, home, w, keep, give, att):
+def columns(zl, slot, core):
+    return pl.ds(pl.multiple_of((2 * (zl ^ slot) + core) * WIDTH, HD), WIDTH)
+
+
+def give_kernel(mine, theirs, home, w, att, give):
     parts, stats = partials(mine, 0)
     for ref in (theirs, home):
         parts.append(lambda h, ref=ref: ref[0:TOK, h * HD : (h + 1) * HD].astype(F32))
@@ -373,27 +394,41 @@
     for h in range(HEADS_DEV):
         att[:, h * HD : (h + 1) * HD] = outs[h].astype(BF16)
     t = lax.axis_index("tensor")
-    zl, core = t // 2, t % 2
-    for d in range(4):
-        for out, c in ((give, 1 - core), (keep, core)):
-            part = w[:, pl.ds(pl.multiple_of((2 * (zl ^ d) + c) * WIDTH, HD), WIDTH)]
-            out[d] = jnp.dot(att[...], part, preferred_element_type=F32).astype(out.dtype)
+    for slot in range(4):
+        part = w[:, columns(t // 2, slot, 1 - t % 2)]
+        give[slot] = jnp.dot(att[...], part, preferred_element_type=F32).astype(BF16)
+
+
+def keep_kernel(att, w, keep):
+    t = lax.axis_index("tensor")
+    for slot in range(4):
+        part = w[:, columns(t // 2, slot, t % 2)]
+        keep[slot] = jnp.dot(att[...], part, preferred_element_type=F32)
 
 
 def project(mine, theirs, home, out_weight):
     full = pl.BlockSpec(memory_space=pltpu.VMEM)
-    return pl.pallas_call(
-        project_kernel,
+    params = pltpu.CompilerParams(vmem_limit_bytes=16 * MIB)
+    att, give = pl.pallas_call(
+        give_kernel,
         out_shape=(
-            jax.ShapeDtypeStruct((4, TOK, WIDTH), F32),
+            jax.ShapeDtypeStruct((TOK, WIDTH), BF16),
             jax.ShapeDtypeStruct((4, TOK, WIDTH), BF16),
         ),
         in_specs=[full] * 4,
         out_specs=(full, full),
-        scratch_shapes=[pltpu.VMEM((TOK, WIDTH), BF16)],
-        compiler_params=pltpu.CompilerParams(vmem_limit_bytes=16 * MIB),
-        name="project",
+        compiler_params=params,
+        name="project_give",
     )(mine, theirs, home, out_weight)
+    keep = pl.pallas_call(
+        keep_kernel,
+        out_shape=jax.ShapeDtypeStruct((4, TOK, WIDTH), F32),
+        in_specs=[full] * 2,
+        out_specs=full,
+        compiler_params=params,
+        name="project_keep",
+    )(att, out_weight)
+    return keep, give
 
 
 def core_kernel(keep, got, own, *outs):
@@ -450,7 +485,7 @@
     pair_q = query_pair(q)
     stale_kv, q = lax.optimization_barrier((stale_kv, q))
     pair_kv = key_pair(stale_kv)
-    queries, pair_kv = lax.optimization_barrier((spread(q, pair_q), pair_kv))
+    queries, pair_kv = lax.optimization_barrier((spread(hold(q), pair_q), pair_kv))
     q_all = exchange(queries, AXES, QUERY_GROUPS)
     kv = key_square(stack(stale_kv, pair_kv))
     home = attend_home(q, k_fresh, fresh_qkv, text_kv)

time: 106 us -> 105 us (level)
  waiting for transfers between devices: 24.4 us -> 22.4 us
    ppermute x10, waiting for transfers between devices: 24.4 us -> 22.4 us  [permute(): return lax.ppermute(value, AXES, pairs)]
where the time goes in v7:
time: 105 us; the launch traced here: 104 us
  starting transfers between devices  52 us (50%)
  waiting for transfers between devices  22.4 us (21%)
  blocking collectives  15.9 us (15%)
  Pallas kernels  11.7 us (11%)
    ppermute x10, starting transfers between devices, permute(): return lax.ppermute(value, AXES, pairs)  45.1 us
    ppermute x10, waiting for transfers between devices, permute(): return lax.ppermute(value, AXES, pairs)  22.4 us
    all_to_all x1, blocking collectives, exchange(): lax.all_to_all(value, axes, 0, 0, axis_index_groups=groups, tiled=True)  15.9 us
    all_to_all x1, starting transfers between devices, exchange(): lax.all_to_all(value, axes, 0, 0, axis_index_groups=groups, tiled=True)  6.87 us
    pallas_call x1, Pallas kernels, attention(): pl.pallas_call(attn_kernel, out_shape=jax.ShapeDtypeStruct((4, 2, TOK + S...  4.63 us
    pallas_call x1, Pallas kernels, prepare(): pl.pallas_call(prep_kernel, out_shape=(jax.ShapeDtypeStruct((TOK, WIDTH),...  2.53 us
  transfers between devices with their start and end apart: 11, of which 7 were waited for; matrix products, arithmetic and copies ran while one was open for 0% of the time, Pallas kernels for 2%

profile of v7, /device:TPU:1, one launch (start us, length us, event | category | flops | bytes accessed | tf_op | source)
XLA Modules:
  0.0 103.8 jit_solution(9524525724685354430)
XLA Ops:
  0.0 2.5 %prep.1 = (bf16[128,384]{1,0:T(8,128)(2,1)}, bf16[128,384]{1,0:T(8,128)(2,1)}) custom-call(bf16[3,128,384]{2,1,0:T(8,128)(2,1)} %raw.1, s32[1,128]{1,0:T(1,128)} %bitcast.3, f32[8,128]{1,0:T(8,128)} %constant.2.clone.freq_hbm, f32[1,128]{1,0:T(1,128)} %bitcast.4, f32[1,128]{1,0:T(1,128)} %bitcast.5), custom_call_target="tpu_custom_call" | custom-call | tf_op jit(solution)/shard_map/prep/pallas_call | solution.py:180
  2.5 13.4 %collective-permute-start.1 = (bf16[2,128,384]{2,1,0:T(8,128)(2,1)}, bf16[2,128,384]{2,1,0:T(8,128)(2,1)S(1)}, u32[]{:S(2)}, u32[]{:S(2)}) collective-permute-start(bf16[2,128,384]{2,1,0:T(8,128)(2,1)} %a), channel_id=1, source_target_pairs={{0,32},{1,97},{2,34},{3,99},{4,36},{5,101},{6,38},{7,103},{8,40},{... | collective-permute-start | bytes 589832 | tf_op jit(solution)/shard_map/ppermute | solution.py:36
  16.0 5.2 %collective-permute-start = (bf16[128,384]{1,0:T(8,128)(2,1)}, bf16[128,384]{1,0:T(8,128)(2,1)S(1)}, u32[]{:S(2)}, u32[]{:S(2)}) collective-permute-start(bf16[128,384]{1,0:T(8,128)(2,1)} %get-tuple-element.19.ref.q), channel_id=1, source_target_pairs={{0,96},{1,33},{2,98},{3,35},{4,100},{5,37},{6,102},{7,39},{8,104},... | collective-permute-start | bytes 294920 | tf_op jit(solution)/shard_map/ppermute | solution.py:36
  21.2 0.9 copy-done.6
  22.1 5.4 %collective-permute-done.refs_1_ = bf16[128,384]{1,0:T(8,128)(2,1)S(1)} collective-permute-done((bf16[128,384]{1,0:T(8,128)(2,1)}, bf16[128,384]{1,0:T(8,128)(2,1)S(1)}, u32[]{:S(2)}, u32[]{:S(2)}) %collective-permute-start) | collective-permute-done | bytes 98336 | tf_op jit(solution)/shard_map/ppermute | solution.py:36
  27.5 0.9 spread.1
  28.4 6.9 %all-to-all-start = ((bf16[4,2,128,384]{3,2,1,0:T(8,128)(2,1)}), bf16[4,2,128,384]{3,2,1,0:T(8,128)(2,1)S(1)}, u32[]{:S(2)}, u32[]{:S(2)}) async-start(bf16[4,2,128,384]{3,2,1,0:T(8,128)(2,1)} %spread.1), calls=%async_computation | async-start | bytes 1572864 | tf_op jit(solution)/shard_map/all_to_all | solution.py:54
  35.4 1.9 %collective-permute-start.4 = (bf16[2,2,128,384]{3,2,1,0:T(8,128)(2,1)S(1)}, bf16[2,2,128,384]{3,2,1,0:T(8,128)(2,1)S(1)}, u32[]{:S(2)}, u32[]{:S(2)}) collective-permute-start(bf16[2,2,128,384]{3,2,1,0:T(8,128)(2,1)S(1)} %stack.1.a), channel_id=1, source_target_pairs={{0,408},{1,137},{2,410},{3,139},{4,412},{5,141},{6,414},{7,143},{8... | collective-permute-start | bytes 1179656 | tf_op jit(solution)/shard_map/ppermute | solution.py:36
  37.3 3.0 %collective-permute-start.3 = (bf16[2,2,128,384]{3,2,1,0:T(8,128)(2,1)S(1)}, bf16[2,2,128,384]{3,2,1,0:T(8,128)(2,1)S(1)}, u32[]{:S(2)}, u32[]{:S(2)}) collective-permute-start(bf16[2,2,128,384]{3,2,1,0:T(8,128)(2,1)S(1)} %stack.1.a), channel_id=1, source_target_pairs={{0,384},{1,129},{2,386},{3,131},{4,388},{5,133},{6,390},{7,135},{8... | collective-permute-start | bytes 1179656 | tf_op jit(solution)/shard_map/ppermute | solution.py:36
  40.3 3.4 %collective-permute-start.2 = (bf16[2,2,128,384]{3,2,1,0:T(8,128)(2,1)S(1)}, bf16[2,2,128,384]{3,2,1,0:T(8,128)(2,1)S(1)}, u32[]{:S(2)}, u32[]{:S(2)}) collective-permute-start(bf16[2,2,128,384]{3,2,1,0:T(8,128)(2,1)S(1)} %stack.1.a), channel_id=1, source_target_pairs={{0,24},{1,9},{2,26},{3,11},{4,28},{5,13},{6,30},{7,15},{8,16},{9,1... | collective-permute-start | bytes 1179656 | tf_op jit(solution)/shard_map/ppermute | solution.py:36
  43.7 3.6 %collective-permute-done.4.d = bf16[2,2,128,384]{3,2,1,0:T(8,128)(2,1)S(1)} collective-permute-done((bf16[2,2,128,384]{3,2,1,0:T(8,128)(2,1)S(1)}, bf16[2,2,128,384]{3,2,1,0:T(8,128)(2,1)S(1)}, u32[]{:S(2)}, u32[]{:S(2)}) %collective-permute-start.4) | collective-permute-done | bytes 393248 | tf_op jit(solution)/shard_map/ppermute | solution.py:36
  47.3 3.3 %collective-permute-done.3.c = bf16[2,2,128,384]{3,2,1,0:T(8,128)(2,1)S(1)} collective-permute-done((bf16[2,2,128,384]{3,2,1,0:T(8,128)(2,1)S(1)}, bf16[2,2,128,384]{3,2,1,0:T(8,128)(2,1)S(1)}, u32[]{:S(2)}, u32[]{:S(2)}) %collective-permute-start.3) | collective-permute-done | bytes 393248 | tf_op jit(solution)/shard_map/ppermute | solution.py:36
  50.6 4.6 %attend.1 = bf16[4,2,144,384]{3,2,1,0:T(8,128)(2,1)S(1)} custom-call(bf16[2,2,128,384]{3,2,1,0:T(8,128)(2,1)S(1)} %stack.1.a, bf16[2,2,128,384]{3,2,1,0:T(8,128)(2,1)S(1)} %collective-permute-done.2.b, bf16[2,2,128,384]{3,2,1,0:T(8,128)(2,1)S(1)} %collective-permute-done.3.c, bf16[2,2,128,384]{3,2,1,0:T(8,128)(2,1)S(1)} %collective-permute-done.4.d, ...), custom_call_target="tpu_custom_call" | custom-call | flops 1610612736 | bytes 4194304 | tf_op jit(solution)/shard_map/attend/pallas_call | solution.py:305
  55.3 15.9 %all_to_all.10.got.mine = bf16[4,2,144,384]{3,2,1,0:T(8,128)(2,1)S(1)} all-to-all(bf16[4,2,144,384]{3,2,1,0:T(8,128)(2,1)S(1)} %attend.1), channel_id=1, replica_groups={{0,8,128,136},{1,25,385,409},{2,10,130,138},{3,27,387,411},{4,12,132,14..., dimensions={0} | all-to-all | bytes 1769472 | tf_op jit(solution)/shard_map/all_to_all | solution.py:54
  71.6 5.4 %collective-permute-start.5 = (bf16[144,384]{1,0:T(8,128)(2,1)S(1)}, bf16[144,384]{1,0:T(8,128)(2,1)S(1)}, u32[]{:S(2)}, u32[]{:S(2)}) collective-permute-start(bf16[144,384]{1,0:T(8,128)(2,1)S(1)} %merge.1), channel_id=1, source_target_pairs={{0,96},{1,33},{2,98},{3,35},{4,100},{5,37},{6,102},{7,39},{8,104},... | collective-permute-start | bytes 331784 | tf_op jit(solution)/shard_map/ppermute | solution.py:36
  77.9 6.0 %collective-permute-done.5.theirs = bf16[144,384]{1,0:T(8,128)(2,1)S(1)} collective-permute-done((bf16[144,384]{1,0:T(8,128)(2,1)S(1)}, bf16[144,384]{1,0:T(8,128)(2,1)S(1)}, u32[]{:S(2)}, u32[]{:S(2)}) %collective-permute-start.5) | collective-permute-done | bytes 110624 | tf_op jit(solution)/shard_map/ppermute | solution.py:36
  83.9 1.0 project_give.1
  85.0 3.5 %collective-permute-start.6 = (bf16[4,128,384]{2,1,0:T(8,128)(2,1)S(1)}, bf16[4,128,384]{2,1,0:T(8,128)(2,1)S(1)}, u32[]{:S(2)}, u32[]{:S(2)}) collective-permute-start(bf16[4,128,384]{2,1,0:T(8,128)(2,1)S(1)} %get-tuple-element.24), channel_id=1, source_target_pairs={{0,1},{1,0},{2,3},{3,2},{4,5},{5,4},{6,7},{7,6},{8,9},{9,8},{10,11... | collective-permute-start | bytes 1179656 | tf_op jit(solution)/shard_map/ppermute | solution.py:36
  88.9 0.9 collective-permute-done.6.got
  89.9 2.4 %collective-permute-start.7 = (bf16[128,384]{1,0:T(8,128)(2,1)S(1)}, bf16[128,384]{1,0:T(8,128)(2,1)S(1)}, u32[]{:S(2)}, u32[]{:S(2)}) collective-permute-start(bf16[128,384]{1,0:T(8,128)(2,1)S(1)} %get-tuple-element.26), channel_id=1, source_target_pairs={{0,2},{1,3},{2,0},{3,1},{4,6},{5,7},{6,4},{7,5},{8,10},{9,11},{10,... | collective-permute-start | bytes 294920 | tf_op jit(solution)/shard_map/ppermute | solution.py:36
  92.2 3.5 %collective-permute-start.8 = (bf16[128,384]{1,0:T(8,128)(2,1)S(1)}, bf16[128,384]{1,0:T(8,128)(2,1)S(1)}, u32[]{:S(2)}, u32[]{:S(2)}) collective-permute-start(bf16[128,384]{1,0:T(8,128)(2,1)S(1)} %get-tuple-element.27), channel_id=1, source_target_pairs={{0,4},{1,5},{2,6},{3,7},{4,0},{5,1},{6,2},{7,3},{8,12},{9,13},{10,... | collective-permute-start | bytes 294920 | tf_op jit(solution)/shard_map/ppermute | solution.py:36
  95.8 3.4 %collective-permute-start.9 = (bf16[128,384]{1,0:T(8,128)(2,1)S(1)}, bf16[128,384]{1,0:T(8,128)(2,1)S(1)}, u32[]{:S(2)}, u32[]{:S(2)}) collective-permute-start(bf16[128,384]{1,0:T(8,128)(2,1)S(1)} %get-tuple-element.28), channel_id=1, source_target_pairs={{0,6},{1,7},{2,4},{3,5},{4,2},{5,3},{6,0},{7,1},{8,14},{9,15},{10,... | collective-permute-start | bytes 294920 | tf_op jit(solution)/shard_map/ppermute | solution.py:36
  99.8 1.3 %collective-permute-done.8.b = bf16[128,384]{1,0:T(8,128)(2,1)S(1)} collective-permute-done((bf16[128,384]{1,0:T(8,128)(2,1)S(1)}, bf16[128,384]{1,0:T(8,128)(2,1)S(1)}, u32[]{:S(2)}, u32[]{:S(2)}) %collective-permute-start.8) | collective-permute-done | bytes 98336 | tf_op jit(solution)/shard_map/ppermute | solution.py:36
  101.1 1.9 %collective-permute-done.9.c = bf16[128,384]{1,0:T(8,128)(2,1)S(1)} collective-permute-done((bf16[128,384]{1,0:T(8,128)(2,1)S(1)}, bf16[128,384]{1,0:T(8,128)(2,1)S(1)}, u32[]{:S(2)}, u32[]{:S(2)}) %collective-permute-start.9) | collective-permute-done | bytes 98336 | tf_op jit(solution)/shard_map/ppermute | solution.py:36
  (30 shorter events, 2.6 us)
Async XLA Ops:
  2.5 32.8 %copy-start.3 = (bf16[2,128,384]{2,1,0:T(8,128)(2,1)S(1)}, bf16[2,128,384]{2,1,0:T(8,128)(2,1)}, u32[]{:S(2)}) copy-start(bf16[2,128,384]{2,1,0:T(8,128)(2,1)} %a) | copy-start | bytes 589828
  2.5 25.9 %collective-permute-start.1 = (bf16[2,128,384]{2,1,0:T(8,128)(2,1)}, bf16[2,128,384]{2,1,0:T(8,128)(2,1)S(1)}, u32[]{:S(2)}, u32[]{:S(2)}) collective-permute-start(bf16[2,128,384]{2,1,0:T(8,128)(2,1)} %a), channel_id=1, source_target_pairs={{0,32},{1,97},{2,34},{3,99},{4,36},{5,101},{6,38},{7,103},{8,40},{... | collective-permute-start | bytes 589832 | tf_op jit(solution)/shard_map/ppermute | solution.py:36
  16.0 11.5 %collective-permute-start = (bf16[128,384]{1,0:T(8,128)(2,1)}, bf16[128,384]{1,0:T(8,128)(2,1)S(1)}, u32[]{:S(2)}, u32[]{:S(2)}) collective-permute-start(bf16[128,384]{1,0:T(8,128)(2,1)} %get-tuple-element.19.ref.q), channel_id=1, source_target_pairs={{0,96},{1,33},{2,98},{3,35},{4,100},{5,37},{6,102},{7,39},{8,104},... | collective-permute-start | bytes 294920 | tf_op jit(solution)/shard_map/ppermute | solution.py:36
  21.2 0.9 copy-start.6
  28.4 22.2 %all-to-all-start = ((bf16[4,2,128,384]{3,2,1,0:T(8,128)(2,1)}), bf16[4,2,128,384]{3,2,1,0:T(8,128)(2,1)S(1)}, u32[]{:S(2)}, u32[]{:S(2)}) async-start(bf16[4,2,128,384]{3,2,1,0:T(8,128)(2,1)} %spread.1), calls=%async_computation | async-start | bytes 1572864 | tf_op jit(solution)/shard_map/all_to_all | solution.py:54
  35.4 12.0 %collective-permute-start.4 = (bf16[2,2,128,384]{3,2,1,0:T(8,128)(2,1)S(1)}, bf16[2,2,128,384]{3,2,1,0:T(8,128)(2,1)S(1)}, u32[]{:S(2)}, u32[]{:S(2)}) collective-permute-start(bf16[2,2,128,384]{3,2,1,0:T(8,128)(2,1)S(1)} %stack.1.a), channel_id=1, source_target_pairs={{0,408},{1,137},{2,410},{3,139},{4,412},{5,141},{6,414},{7,143},{8... | collective-permute-start | bytes 1179656 | tf_op jit(solution)/shard_map/ppermute | solution.py:36
  37.3 13.3 %collective-permute-start.3 = (bf16[2,2,128,384]{3,2,1,0:T(8,128)(2,1)S(1)}, bf16[2,2,128,384]{3,2,1,0:T(8,128)(2,1)S(1)}, u32[]{:S(2)}, u32[]{:S(2)}) collective-permute-start(bf16[2,2,128,384]{3,2,1,0:T(8,128)(2,1)S(1)} %stack.1.a), channel_id=1, source_target_pairs={{0,384},{1,129},{2,386},{3,131},{4,388},{5,133},{6,390},{7,135},{8... | collective-permute-start | bytes 1179656 | tf_op jit(solution)/shard_map/ppermute | solution.py:36
  40.3 10.3 %collective-permute-start.2 = (bf16[2,2,128,384]{3,2,1,0:T(8,128)(2,1)S(1)}, bf16[2,2,128,384]{3,2,1,0:T(8,128)(2,1)S(1)}, u32[]{:S(2)}, u32[]{:S(2)}) collective-permute-start(bf16[2,2,128,384]{3,2,1,0:T(8,128)(2,1)S(1)} %stack.1.a), channel_id=1, source_target_pairs={{0,24},{1,9},{2,26},{3,11},{4,28},{5,13},{6,30},{7,15},{8,16},{9,1... | collective-permute-start | bytes 1179656 | tf_op jit(solution)/shard_map/ppermute | solution.py:36
  50.6 26.4 %copy-start.2 = (bf16[2,512,384]{2,1,0:T(8,128)(2,1)S(1)}, bf16[2,512,384]{2,1,0:T(8,128)(2,1)}, u32[]{:S(2)}) copy-start(bf16[2,512,384]{2,1,0:T(8,128)(2,1)} %text.1) | copy-start | bytes 2359300
  50.6 26.4 %copy-start.8 = (bf16[128,384]{1,0:T(8,128)(2,1)S(1)}, bf16[128,384]{1,0:T(8,128)(2,1)}, u32[]{:S(2)}) copy-start(bf16[128,384]{1,0:T(8,128)(2,1)} %get-tuple-element.22.k_fresh) | copy-start | bytes 294916
  55.3 21.8 %copy-start.1 = (bf16[3,128,384]{2,1,0:T(8,128)(2,1)S(1)}, bf16[3,128,384]{2,1,0:T(8,128)(2,1)}, u32[]{:S(2)}) copy-start(bf16[3,128,384]{2,1,0:T(8,128)(2,1)} %raw.1) | copy-start | bytes 884740
  55.3 21.8 %copy-start.7 = (bf16[128,384]{1,0:T(8,128)(2,1)S(1)}, bf16[128,384]{1,0:T(8,128)(2,1)}, u32[]{:S(2)}) copy-start(bf16[128,384]{1,0:T(8,128)(2,1)} %get-tuple-element.19.ref.q) | copy-start | bytes 294916
  55.3 28.6 %copy-start = (bf16[384,3072]{1,0:T(8,128)(2,1)S(1)}, bf16[384,3072]{1,0:T(8,128)(2,1)}, u32[]{:S(2)}) copy-start(bf16[384,3072]{1,0:T(8,128)(2,1)} %w.3) | copy-start | bytes 7077892
  71.6 12.3 %collective-permute-start.5 = (bf16[144,384]{1,0:T(8,128)(2,1)S(1)}, bf16[144,384]{1,0:T(8,128)(2,1)S(1)}, u32[]{:S(2)}, u32[]{:S(2)}) collective-permute-start(bf16[144,384]{1,0:T(8,128)(2,1)S(1)} %merge.1), channel_id=1, source_target_pairs={{0,96},{1,33},{2,98},{3,35},{4,100},{5,37},{6,102},{7,39},{8,104},... | collective-permute-start | bytes 331784 | tf_op jit(solution)/shard_map/ppermute | solution.py:36
  85.0 18.1 %copy-start.4 = (bf16[128,384]{1,0:T(8,128)(2,1)S(1)}, bf16[128,384]{1,0:T(8,128)(2,1)}, u32[]{:S(2)}) copy-start(bf16[128,384]{1,0:T(8,128)(2,1)} %hidden.1) | copy-start | bytes 294916
  85.0 18.1 %copy-start.5 = (bf16[128,384]{1,0:T(8,128)(2,1)S(1)}, bf16[128,384]{1,0:T(8,128)(2,1)}, u32[]{:S(2)}) copy-start(bf16[128,384]{1,0:T(8,128)(2,1)} %control.1) | copy-start | bytes 294916
  85.0 18.1 %copy-start.9 = (f32[28,384]{1,0:T(8,128)S(1)}, f32[28,384]{1,0:T(8,128)}, u32[]{:S(2)}) copy-start(f32[28,384]{1,0:T(8,128)} %gate.1) | copy-start | bytes 129028
  85.0 4.8 %collective-permute-start.6 = (bf16[4,128,384]{2,1,0:T(8,128)(2,1)S(1)}, bf16[4,128,384]{2,1,0:T(8,128)(2,1)S(1)}, u32[]{:S(2)}, u32[]{:S(2)}) collective-permute-start(bf16[4,128,384]{2,1,0:T(8,128)(2,1)S(1)} %get-tuple-element.24), channel_id=1, source_target_pairs={{0,1},{1,0},{2,3},{3,2},{4,5},{5,4},{6,7},{7,6},{8,9},{9,8},{10,11... | collective-permute-start | bytes 1179656 | tf_op jit(solution)/shard_map/ppermute | solution.py:36
  89.9 9.9 %collective-permute-start.7 = (bf16[128,384]{1,0:T(8,128)(2,1)S(1)}, bf16[128,384]{1,0:T(8,128)(2,1)S(1)}, u32[]{:S(2)}, u32[]{:S(2)}) collective-permute-start(bf16[128,384]{1,0:T(8,128)(2,1)S(1)} %get-tuple-element.26), channel_id=1, source_target_pairs={{0,2},{1,3},{2,0},{3,1},{4,6},{5,7},{6,4},{7,5},{8,10},{9,11},{10,... | collective-permute-start | bytes 294920 | tf_op jit(solution)/shard_map/ppermute | solution.py:36
  92.2 8.9 %collective-permute-start.8 = (bf16[128,384]{1,0:T(8,128)(2,1)S(1)}, bf16[128,384]{1,0:T(8,128)(2,1)S(1)}, u32[]{:S(2)}, u32[]{:S(2)}) collective-permute-start(bf16[128,384]{1,0:T(8,128)(2,1)S(1)} %get-tuple-element.27), channel_id=1, source_target_pairs={{0,4},{1,5},{2,6},{3,7},{4,0},{5,1},{6,2},{7,3},{8,12},{9,13},{10,... | collective-permute-start | bytes 294920 | tf_op jit(solution)/shard_map/ppermute | solution.py:36
  95.8 7.3 %collective-permute-start.9 = (bf16[128,384]{1,0:T(8,128)(2,1)S(1)}, bf16[128,384]{1,0:T(8,128)(2,1)S(1)}, u32[]{:S(2)}, u32[]{:S(2)}) collective-permute-start(bf16[128,384]{1,0:T(8,128)(2,1)S(1)} %get-tuple-element.28), channel_id=1, source_target_pairs={{0,6},{1,7},{2,4},{3,5},{4,2},{5,3},{6,0},{7,1},{8,14},{9,15},{10,... | collective-permute-start | bytes 294920 | tf_op jit(solution)/shard_map/ppermute | solution.py:36
